TPU v7x, 32 devices: a whole 2x2x4 slice. The times are simulated.
32 devices in a mesh: wide: 16 (over z, x, core), hub: 2 (over y).
Axes of the slice: x: 2, y: 2, z: 4, core: 2. Of those that a mesh axis runs over, the one named last changes fastest.
Arguments:
- low_feats: bfloat16 [8192, 256], P(('wide', 'hub')), may hold values from -6 to 6
- hub_feats: bfloat16 [512, 256], P(('wide', 'hub')), may hold values from -6 to 6
- w_first: bfloat16 [256, 256], replicated, may hold values from -0.375 to 0.375
- w_second: bfloat16 [256, 256], replicated, may hold values from -0.375 to 0.375
- low_tiles: bfloat16 [1024, 128, 128], P(('wide', 'hub')), may hold values from 0 to 1.5
- tile_cols: int32 [64, 16], P(('wide', 'hub')), may hold values from 0 to 31, all different within a row
- edge_rows: int32 [16384], P(('wide', 'hub')), may hold values from 0 to 255
- edge_hubs: int32 [16384], P(('wide', 'hub')), may hold values from 0 to 31
- low_labels: int32 [8192], P(('wide', 'hub')), may hold values from 0 to 255
- hub_labels: int32 [512], P(('wide', 'hub')), may hold values from 0 to 255
Outputs:
- low_logits: float32 [8192, 256], P(('wide', 'hub'))
- hub_logits: float32 [512, 256], P(('wide', 'hub'))
- grad_first: float32 [256, 256], replicated
- grad_second: float32 [256, 256], replicated
Inputs may be any that keep to these rules, and one draw needn't show every extreme that they name: `tile_cols`: the 16 tiles of one row block have different column blocks.
All inputs are finite; a program needn't handle non-finite values.
Results may differ from a plain program's by a relative error of at most 0.0022.
The roundings to bfloat16 on the way count: a program that leaves them out, or rounds other values in their place, can miss the bound.
Values may be sent and summed in bfloat16 or wider, within the bound.
No kernel may reach another device: no remote copies, remote signals or barrier semaphores. Data moves between devices by JAX's collectives and lax.ppermute only.
A program may use at most 64 MiB of HBM per device.

v0:
```python
import jax
import jax.numpy as jnp
from jax import lax
from jax.sharding import PartitionSpec as P


def one_hot_rows(indices, count):
    return (indices[:, None] == jnp.arange(count, dtype=jnp.int32)[None, :]).astype(jnp.bfloat16)


def tile_terms(gathered, low_tiles, cols_flat, row_blocks):
    tile = low_tiles.shape[1]
    width = gathered.shape[1]
    blocks = gathered.reshape(gathered.shape[0] // tile, tile, width)
    picked = jnp.take(blocks, cols_flat, axis=0)
    per_block = low_tiles.shape[0] // row_blocks
    picked = picked.reshape(row_blocks, per_block, tile, width)
    shaped = low_tiles.reshape(row_blocks, per_block, tile, tile)
    summed = jnp.einsum("rkij,rkjf->rif", shaped, picked, preferred_element_type=jnp.float32)
    return summed.reshape(row_blocks * tile, width)


def mirrors(field):
    return lax.all_gather(field, "hub", axis=0, tiled=True)


def hub_totals(partials, counts):
    return (
        lax.psum_scatter(partials, "hub", scatter_dimension=0, tiled=True),
        lax.psum_scatter(counts, "hub", scatter_dimension=0, tiled=True),
    )


def local(
    low_feats,
    hub_feats,
    w_first,
    w_second,
    low_tiles,
    tile_cols,
    edge_rows,
    edge_hubs,
    low_labels,
    hub_labels,
):
    rows = low_feats.shape[0]
    hub_rows = hub_feats.shape[0]
    tile = low_tiles.shape[1]
    n_tiles = low_tiles.shape[0]
    row_blocks = rows // tile
    per_block = n_tiles // row_blocks
    classes = w_second.shape[1]
    n_wide = lax.axis_size("wide")
    group_hubs = hub_rows * lax.axis_size("hub")
    total = (rows + hub_rows) * n_wide * lax.axis_size("hub")
    cols_flat = tile_cols.reshape(n_tiles)
    hub_hot = one_hot_rows(edge_hubs, group_hubs)
    row_hot = one_hot_rows(edge_rows, rows)
    links = jnp.einsum("eg,er->gr", hub_hot, row_hot, preferred_element_type=jnp.float32)
    link_bf = links.astype(jnp.bfloat16)
    low_count = jnp.sum(links, axis=0)
    hub_partial_count = jnp.sum(links, axis=1)
    tile_rows = jnp.sum(low_tiles, axis=2, dtype=jnp.float32)
    tile_rows = jnp.sum(tile_rows.reshape(row_blocks, per_block, tile), axis=1).reshape(rows)
    low_scale = lax.rsqrt(1.0 + tile_rows + low_count)

    def low_side(field_low, hub_whole):
        gathered = lax.all_gather(field_low, "wide", axis=0, tiled=True)
        tiles_part = tile_terms(gathered, low_tiles, cols_flat, row_blocks)
        hub_part = jnp.einsum("gr,gf->rf", link_bf, hub_whole, preferred_element_type=jnp.float32)
        return (field_low.astype(jnp.float32) + tiles_part + hub_part) * low_scale[:, None]

    def to_hubs(field_low):
        return jnp.einsum("gr,rf->gf", link_bf, field_low, preferred_element_type=jnp.float32)

    hub_whole_x = mirrors(hub_feats)
    agg1_low = low_side(low_feats, hub_whole_x).astype(jnp.bfloat16)
    sums, counts = hub_totals(to_hubs(low_feats), hub_partial_count)
    hub_scale = lax.rsqrt(1.0 + counts)
    agg1_hub = ((hub_feats.astype(jnp.float32) + sums) * hub_scale[:, None]).astype(jnp.bfloat16)
    z1_hub = jnp.dot(agg1_hub, w_first, preferred_element_type=jnp.float32)
    h1_hub = jnp.maximum(z1_hub, 0.0).astype(jnp.bfloat16)
    h1_hub_whole = lax.all_gather(h1_hub, "hub", axis=0, tiled=True)
    z1_low = jnp.dot(agg1_low, w_first, preferred_element_type=jnp.float32)
    h1_low = jnp.maximum(z1_low, 0.0).astype(jnp.bfloat16)
    agg2_low = low_side(h1_low, h1_hub_whole).astype(jnp.bfloat16)
    sums, _ = hub_totals(to_hubs(h1_low), hub_partial_count)
    agg2_hub = ((h1_hub.astype(jnp.float32) + sums) * hub_scale[:, None]).astype(jnp.bfloat16)
    low_logits = jnp.dot(agg2_low, w_second, preferred_element_type=jnp.float32)
    hub_logits = jnp.dot(agg2_hub, w_second, preferred_element_type=jnp.float32)
    class_ids = jnp.arange(classes, dtype=jnp.int32)
    low_target = (low_labels[:, None] == class_ids[None, :]).astype(jnp.float32)
    hub_target = (hub_labels[:, None] == class_ids[None, :]).astype(jnp.float32)
    dz2_low = ((low_logits - low_target) / total).astype(jnp.bfloat16)
    dz2_hub = ((hub_logits - hub_target) / total).astype(jnp.bfloat16)
    grad_second = jnp.einsum("rh,rc->hc", agg2_low, dz2_low, preferred_element_type=jnp.float32)
    grad_second = grad_second + jnp.einsum(
        "rh,rc->hc", agg2_hub, dz2_hub, preferred_element_type=jnp.float32
    )
    q_low = (
        jnp.einsum("rc,hc->rh", dz2_low, w_second, preferred_element_type=jnp.float32)
        * low_scale[:, None]
    ).astype(jnp.bfloat16)
    q_hub = (
        jnp.einsum("rc,hc->rh", dz2_hub, w_second, preferred_element_type=jnp.float32)
        * hub_scale[:, None]
    ).astype(jnp.bfloat16)
    width = q_low.shape[1]
    shaped = low_tiles.reshape(row_blocks, per_block, tile, tile)
    contrib = jnp.einsum(
        "rkij,rif->rkjf",
        shaped,
        q_low.reshape(row_blocks, tile, width),
        preferred_element_type=jnp.float32,
    )
    contrib = contrib.reshape(n_tiles, tile, width)
    placed = jnp.zeros((n_wide * row_blocks, tile, width), jnp.float32).at[cols_flat].add(contrib)
    placed = placed.reshape(n_wide * rows, width)
    back_low = lax.psum_scatter(
        placed.astype(jnp.bfloat16), "wide", scatter_dimension=0, tiled=True
    ).astype(jnp.float32)
    q_hub_whole = mirrors(q_hub)
    hub_back = jnp.einsum("gr,gf->rf", link_bf, q_hub_whole, preferred_element_type=jnp.float32)
    dh1_low = q_low.astype(jnp.float32) + back_low + hub_back
    sums, _ = hub_totals(to_hubs(q_low), hub_partial_count)
    dh1_hub = q_hub.astype(jnp.float32) + sums
    dz1_low = jnp.where(z1_low > 0.0, dh1_low, 0.0).astype(jnp.bfloat16)
    dz1_hub = jnp.where(z1_hub > 0.0, dh1_hub, 0.0).astype(jnp.bfloat16)
    grad_first = jnp.einsum("rf,rh->fh", agg1_low, dz1_low, preferred_element_type=jnp.float32)
    grad_first = grad_first + jnp.einsum(
        "rf,rh->fh", agg1_hub, dz1_hub, preferred_element_type=jnp.float32
    )
    grad_first, grad_second = lax.psum((grad_first, grad_second), ("wide", "hub"))
    return (low_logits, hub_logits, grad_first, grad_second)


def solution(mesh):
    in_specs = (
        P(("wide", "hub"), None),
        P(("wide", "hub"), None),
        P(),
        P(),
        P(("wide", "hub"), None, None),
        P(("wide", "hub"), None),
        P(("wide", "hub")),
        P(("wide", "hub")),
        P(("wide", "hub")),
        P(("wide", "hub")),
    )
    out_specs = (P(("wide", "hub"), None), P(("wide", "hub"), None), P(), P())
    return jax.shard_map(local, mesh=mesh, in_specs=in_specs, out_specs=out_specs, check_vma=False)
```

profile of v0, /device:TPU:0, one launch (start us, length us, event | category | flops | bytes accessed | tf_op | source)
XLA Modules:
  0.0 339.8 jit_solution(1729086777295400081)
XLA Ops:
  8.8 1.2 fusion.24
  10.0 1.7 fusion.25
  11.7 0.8 reshape.98
  12.5 1.6 convert_reduce_fusion
  14.1 5.6 %all_gather.16 = bf16[32,256]{1,0:T(8,128)(2,1)S(1)} all-gather(bf16[16,256]{1,0:T(8,128)(2,1)} %param.13), channel_id=1, replica_groups=mesh['wide'=16,'hub'=2] {'hub'}, dimensions={0}, use_global_device_ids=true | all-gather | bytes 24576 | tf_op jit(solution)/shard_map/all_gather | solution.py:24
  19.7 35.4 %all-gather.3.cloned.1.call-done = bf16[4096,256]{1,0:T(8,128)(2,1)} async-done(((bf16[256,256]{1,0:T(8,128)(2,1)}), bf16[4096,256]{1,0:T(8,128)(2,1)}) %all-gather.3.cloned.1.call-update) | async-done | bytes 2097168 | tf_op jit(solution)/shard_map/all_gather | solution.py:68
  55.1 2.3 gather_fusion
  57.7 0.9 copy-done.1
  59.4 0.9 maximum_convert_fusion
  60.3 0.8 fusion.27
  61.1 0.7 all-gather.5.cloned.1.call-update
  63.2 4.9 %all-reduce = f32[32]{0:T(128)S(1)} all-reduce(f32[32]{0:T(128)S(1)} %get-tuple-element.5), channel_id=3, replica_groups=mesh['wide'=16,'hub'=2] {'hub'}, use_global_device_ids=true, to_apply=%region_5.7.clone | all-reduce | flops 32 | bytes 256
  68.2 0.8 multiply_convert_fusion.3
  69.0 0.7 reduce-scatter.7.cloned.1.call-done
  69.8 0.8 multiply_convert_fusion.2
  70.6 4.4 %all_gather.18 = bf16[32,256]{1,0:T(8,128)(2,1)S(1)} all-gather(bf16[16,256]{1,0:T(8,128)(2,1)S(1)} %get-tuple-element.10), channel_id=1, replica_groups=mesh['wide'=16,'hub'=2] {'hub'}, dimensions={0}, use_global_device_ids=true | all-gather | bytes 24576 | tf_op jit(solution)/shard_map/all_gather | solution.py:83
  75.0 29.9 %all-gather.5.cloned.1.call-done = bf16[4096,256]{1,0:T(8,128)(2,1)} async-done(((bf16[256,256]{1,0:T(8,128)(2,1)}), bf16[4096,256]{1,0:T(8,128)(2,1)}) %all-gather.5.cloned.1.call-update) | async-done | bytes 2097168 | tf_op jit(solution)/shard_map/all_gather | solution.py:68
  104.9 2.3 gather_fusion.1
  109.0 0.8 fusion.30
  109.9 2.7 fusion.29
  112.6 5.6 %copy.19 = f32[32,128,256]{2,1,0:T(8,128)} copy(f32[32,128,256]{1,2,0:T(8,128)} %bitcast.69) | data formatting | bytes 8388608 | tf_op jit(solution)/shard_map/reshape | solution.py:116
  118.2 2.5 broadcast_in_dim.13
  120.7 10.2 %scatter_fusion = f32[32,128,256]{2,1,0:T(8,128)} fusion(f32[32,128,256]{2,1,0:T(8,128)} %broadcast_in_dim.13, s32[32]{0:T(128)S(1)} %fusion.19, f32[32,128,256]{2,1,0:T(8,128)} %copy.19), kind=kCustom, calls=%fused_computation.2 | custom fusion | flops 1048576 | bytes 12583040 | tf_op jit(solution)/shard_map/scatter-add | solution.py:117
  130.8 3.8 %convert_element_type.93 = bf16[32,128,256]{2,1,0:T(8,128)(2,1)} convert(f32[32,128,256]{2,1,0:T(8,128)} %scatter_fusion) | non-fusion elementwise | flops 1048576 | bytes 6291456 | tf_op jit(solution)/shard_map/convert_element_type | solution.py:120
  135.5 4.4 %all_gather.19 = bf16[32,256]{1,0:T(8,128)(2,1)S(1)} all-gather(bf16[16,256]{1,0:T(8,128)(2,1)S(1)} %fusion.7), channel_id=1, replica_groups=mesh['wide'=16,'hub'=2] {'hub'}, dimensions={0}, use_global_device_ids=true | all-gather | bytes 24576 | tf_op jit(solution)/shard_map/all_gather | solution.py:24
  140.1 1.0 convolution_add_fusion
  141.1 0.9 fusion.16
  142.0 53.0 %reduce-scatter.9.cloned.1.call-done = bf16[256,256]{1,0:T(8,128)(2,1)} async-done(((bf16[4096,256]{1,0:T(8,128)(2,1)}), bf16[256,256]{1,0:T(8,128)(2,1)}) %reduce-scatter.9.cloned.1.call-update) | async-done | bytes 131088 | tf_op jit(solution)/shard_map/reduce_scatter | solution.py:119
  195.1 2.0 convolution_add_fusion.1
  197.1 131.7 %all-reduce.4.cloned.1.call-done = (f32[256,256]{1,0:T(8,128)}, f32[256,256]{1,0:T(8,128)}) async-done(((f32[256,256]{1,0:T(8,128)}, f32[256,256]{1,0:T(8,128)}), (f32[256,256]{1,0:T(8,128)}, f32[256,256]{1,0:T(8,128)})) %all-reduce.4.cloned.1.call-update) | async-done | bytes 524304 | tf_op jit(solution)/shard_map/psum | solution.py:133
  328.8 1.7 copy.28
  330.5 1.7 copy.29
  (64 shorter events, 5.6 us)
Async XLA Ops:
  8.0 51.4 %copy-start = (bf16[256,256]{1,0:T(8,128)(2,1)S(1)}, bf16[256,256]{1,0:T(8,128)(2,1)}, u32[]{:S(2)}) copy-start(bf16[256,256]{1,0:T(8,128)(2,1)} %param.14) | copy-start | bytes 393220
  8.0 47.1 %all-gather.3.cloned.1.call-start = ((), (), s32[]{:S(2)}) async-start(), calls=%async_computation.4 | async-start | bytes 2228224 | tf_op jit(solution)/shard_map/all_gather | solution.py:68
  8.7 59.5 %reduce-scatter.5.cloned.1.call-start = ((), (), s32[]{:S(2)}) async-start(), calls=%async_computation.6 | async-start | bytes 49152 | tf_op jit(solution)/shard_map/reduce_scatter | solution.py:29
  11.7 58.1 %reduce-scatter.7.cloned.1.call-start = ((), (), s32[]{:S(2)}) async-start(), calls=%async_computation.7 | async-start | bytes 49152 | tf_op jit(solution)/shard_map/reduce_scatter | solution.py:29
  57.4 1.2 copy-start.1
  57.7 1.4 copy-start.5
  58.6 3.2 copy-start.12
  58.6 3.3 copy-start.13
  58.7 9.6 %copy-start.9 = (bf16[16,256]{1,0:T(8,128)(2,1)S(1)}, bf16[16,256]{1,0:T(8,128)(2,1)}, u32[]{:S(2)}) copy-start(bf16[16,256]{1,0:T(8,128)(2,1)} %param.13) | copy-start | bytes 24580
  60.3 0.8 copy-start.3
  61.1 43.8 %all-gather.5.cloned.1.call-start = ((), (), s32[]{:S(2)}) async-start(), calls=%async_computation.5 | async-start | bytes 2228224 | tf_op jit(solution)/shard_map/all_gather | solution.py:68
  61.8 79.3 %reduce-scatter.11.cloned.1.call-start = ((), (), s32[]{:S(2)}) async-start(), calls=%async_computation.9 | async-start | bytes 49152 | tf_op jit(solution)/shard_map/reduce_scatter | solution.py:29
  107.4 0.9 copy-start.4
  107.4 1.1 copy-start.6
  107.4 1.3 copy-start.10
  108.8 31.3 %copy-start.2 = (f32[256,256]{1,0:T(8,128)}, f32[256,256]{1,0:T(8,128)S(1)}, u32[]{:S(2)}) copy-start(f32[256,256]{1,0:T(8,128)S(1)} %fusion.26) | copy-start | bytes 786436
  109.8 85.3 %reduce-scatter.9.cloned.1.call-start = ((), (), s32[]{:S(2)}) async-start(), calls=%async_computation.8 | async-start | bytes 2228224 | tf_op jit(solution)/shard_map/reduce_scatter | solution.py:119
  134.7 0.7 copy-start.11
  134.7 60.4 %copy-start.7 = (f32[256,256]{1,0:T(8,128)S(1)}, f32[256,256]{1,0:T(8,128)}, u32[]{:S(2)}) copy-start(f32[256,256]{1,0:T(8,128)} %get-tuple-element.14) | copy-start | bytes 786436
  134.7 194.2 %all-reduce.4.cloned.1.call-start = ((), (), s32[]{:S(2)}) async-start(), calls=%async_computation.10 | async-start | bytes 1048576 | tf_op jit(solution)/shard_map/psum | solution.py:133
  135.3 196.9 %copy-start.8 = (f32[16,256]{1,0:T(8,128)}, f32[16,256]{1,0:T(8,128)S(1)}, u32[]{:S(2)}) copy-start(f32[16,256]{1,0:T(8,128)S(1)} %fusion.28) | copy-start | bytes 49156
Sparse Core Ops, SparseCore 0:
  11.0 44.0 all-gather.2
  64.7 40.1 all-gather.4
Sparse Core Ops, SparseCore 1:
  11.8 12.5 reduce-scatter.4
  61.2 8.6 reduce-scatter.6
  109.9 8.5 reduce-scatter.10
  134.8 60.2 reduce-scatter.8
  202.0 126.8 all-reduce.3
where the time goes:
time: 341 us; the launch traced here: 340 us
  waiting for transfers between devices  252 us (74%)
  blocking collectives  19.3 us (6%)
  local copies, waits for them, and re-layouts  19.2 us (6%)
  other arithmetic  17.1 us (5%)
  between operations  16.6 us (5%)
  matrix products  15.1 us (4%)
    psum x1, waiting for transfers between devices, local(): lax.psum((grad_first, grad_second), ('wide', 'hub'))  132 us
    all_gather x2, waiting for transfers between devices, low_side(): gathered = lax.all_gather(field_low, 'wide', axis=0, tiled=True)  65.3 us
    reduce_scatter x1, waiting for transfers between devices, local(): lax.psum_scatter(placed.astype(jnp.bfloat16), 'wide', scatter_dimension=0...  53 us
    scatter-add x1, other arithmetic, local(): jnp.zeros((n_wide * row_blocks, tile, width), jnp.float32).at[cols_flat]  10.2 us
    all_gather x2, blocking collectives, mirrors(): return lax.all_gather(field, 'hub', axis=0, tiled=True)  9.93 us
  transfers between devices with their start and end apart: 7, of which 5 were waited for; matrix products, arithmetic and copies ran while one was open for 12% of the time, Pallas kernels for 0%

commit v1 on v0

v1 whole, which is shorter than its diff:
```python
import jax
import jax.numpy as jnp
from jax import lax
from jax.experimental import pallas as pl
from jax.experimental.pallas import tpu as pltpu
from jax.sharding import PartitionSpec as P

F32 = jnp.float32
BF16 = jnp.bfloat16
WIDE = "wide"
HUB = "hub"
LANES = 128


def shaped(rows, cols, dtype):
    return jax.ShapeDtypeStruct((rows, cols), dtype)


def call(body, name, outs, ins, smem=(), scratch=()):
    spaces = [pltpu.SMEM if i in smem else pltpu.VMEM for i in range(len(ins))]
    return pl.pallas_call(
        body,
        name=name,
        out_shape=outs,
        in_specs=[pl.BlockSpec(memory_space=s) for s in spaces],
        out_specs=[pl.BlockSpec(memory_space=pltpu.VMEM) for _ in outs],
        scratch_shapes=list(scratch),
        compiler_params=pltpu.CompilerParams(vmem_limit_bytes=28 * 1024 * 1024),
    )(*ins)


def dot(a, b):
    return lax.dot_general(a, b, (((1,), (0,)), ((), ())), preferred_element_type=F32)


def dot_nt(a, b):
    return lax.dot_general(a, b, (((1,), (1,)), ((), ())), preferred_element_type=F32)


def dot_tn(a, b):
    return lax.dot_general(a, b, (((0,), (0,)), ((), ())), preferred_element_type=F32)


def to_wide(x, k):
    return lax.ppermute(x, WIDE, [(i, i ^ k) for i in range(lax.axis_size(WIDE))])


def to_both(x, k, j):
    n, m = lax.axis_size(WIDE), lax.axis_size(HUB)
    pairs = [(i * m + h, (i ^ k) * m + (h ^ j)) for i in range(n) for h in range(m)]
    return lax.ppermute(x, (WIDE, HUB), pairs)


def gather_wide(first, second):
    nz = lax.axis_size(WIDE) // 4
    xb = to_wide(second, 2)
    za = [to_wide(first, 4 * k) for k in range(1, nz)]
    b2 = jnp.concatenate([second, xb], axis=0)
    a4 = jnp.concatenate([first] + za, axis=0)
    xa = to_wide(a4, 2)
    zb = [to_wide(b2, 4 * k) for k in range(1, nz)]
    near = [a4, xa, b2] + zb
    return near + [to_wide(p, 1) for p in near]


def pairwise(parts):
    while len(parts) > 1:
        parts = [parts[i] + parts[i + 1] for i in range(0, len(parts), 2)]
    return parts[0]


def tile_sum(adj_ref, piece_refs):
    at, total = 0, None
    for ref in piece_refs:
        n = ref.shape[0]
        term = dot(adj_ref[:, at : at + n], ref[...])
        total = term if total is None else total + term
        at += n
    return total


def local(
    low_feats,
    hub_feats,
    w_first,
    w_second,
    low_tiles,
    tile_cols,
    edge_rows,
    edge_hubs,
    low_labels,
    hub_labels,
):
    rows, feat = low_feats.shape
    hr = hub_feats.shape[0]
    n_tiles, tile, _ = low_tiles.shape
    blocks = rows // tile
    per_block = n_tiles // blocks
    units = w_first.shape[1]
    classes = w_second.shape[1]
    n_wide, n_hub = lax.axis_size(WIDE), lax.axis_size(HUB)
    nz = n_wide // 4
    group = hr * n_hub
    total = (rows + hr) * n_wide * n_hub
    edges = edge_rows.shape[0]
    half = n_wide * rows // 2
    pay = feat + LANES

    def prep(tiles, cols, e_rows, e_hubs, feats, adj, adj_t, adj_t_give, link, link_t, scale, *parts):
        w, h = lax.axis_index(WIDE), lax.axis_index(HUB)
        adj[...] = jnp.zeros_like(adj)
        adj_t[...] = jnp.zeros_like(adj_t)
        adj_t_give[...] = jnp.zeros_like(adj_t_give)
        for r in range(blocks):
            for k in range(per_block):
                b = cols[r, k]
                rel = (b // 2) ^ w
                rc, rx, rz = rel & 1, (rel >> 1) & 1, rel >> 2
                place = jnp.where(b % 2 == 0, rx * nz + rz, 2 * nz + rz * 2 + rx)
                start = pl.multiple_of(place * tile, tile)
                value = tiles[r * per_block + k]
                turned = value.T
                adj[r * tile : (r + 1) * tile, pl.ds(pl.multiple_of(rc * half + start, tile), tile)] = value

                @pl.when(rc == 0)
                def _():
                    adj_t[pl.ds(start, tile), r * tile : (r + 1) * tile] = turned

                @pl.when(rc == 1)
                def _():
                    adj_t_give[pl.ds(start, tile), r * tile : (r + 1) * tile] = turned

        hubs = e_hubs[...]
        hubs = ((hubs // hr) ^ h) * hr + hubs % hr
        row_hot = (lax.broadcasted_iota(jnp.int32, (rows, edges), 0) == e_rows[...]).astype(BF16)
        hub_hot = (lax.broadcasted_iota(jnp.int32, (group, edges), 0) == hubs).astype(BF16)
        links = dot_nt(hub_hot, row_hot)
        links_t = dot_nt(row_hot, hub_hot)
        hi, hi_t = links.astype(BF16), links_t.astype(BF16)
        lo, lo_t = (links - hi.astype(F32)).astype(BF16), (links_t - hi_t.astype(F32)).astype(BF16)
        link[:, :rows] = hi
        link[:, rows:] = lo
        link_t[...] = jnp.concatenate([hi_t, lo_t], axis=1)
        deg = dot(adj[...], jnp.ones((2 * half, LANES), BF16))
        deg = 1.0 + deg + jnp.sum(links_t, axis=1, keepdims=True)
        scale[...] = lax.rsqrt(deg)
        sums = dot(hi, feats[...]) + dot(lo, feats[...])
        counts = jnp.broadcast_to(jnp.sum(links, axis=1, keepdims=True), (group, LANES))
        for k, part in enumerate(parts):
            part[:, :feat] = sums[k * hr : (k + 1) * hr]
            part[:, feat:] = counts[k * hr : (k + 1) * hr]

    adj, adj_t, adj_t_give, link, link_t, scale, *parts1 = call(
        prep,
        "prep",
        [
            shaped(rows, 2 * half, BF16),
            shaped(half, rows, BF16),
            shaped(half, rows, BF16),
            shaped(group, 2 * rows, BF16),
            shaped(rows, 2 * group, BF16),
            shaped(rows, LANES, F32),
        ]
        + [shaped(hr, pay, F32) for _ in range(n_hub)],
        [low_tiles, tile_cols, edge_rows.reshape(1, edges), edge_hubs.reshape(1, edges), low_feats],
        smem=(1,),
    )
    adj_t_mate = to_wide(adj_t_give, 1)

    def to_hub(x, k):
        return lax.ppermute(x, HUB, [(i, i ^ k) for i in range(n_hub)])

    mates = range(1, n_hub)
    feats_mates = [to_hub(hub_feats, k) for k in mates]
    got1 = [to_hub(parts1[k], k) for k in mates]

    def hub_first(feats, w, own, *refs):
        got, (hub_scale, agg, act, live) = refs[:-4], refs[-4:]
        sums = own[...]
        for g in got:
            sums = sums + g[...]
        s = lax.rsqrt(1.0 + sums[:, feat : feat + 1])
        hub_scale[...] = jnp.broadcast_to(s, (hr, LANES))
        a = ((feats[...].astype(F32) + sums[:, :feat]) * s).astype(BF16)
        agg[...] = a
        z = dot(a, w[...])
        act[...] = jnp.maximum(z, 0.0).astype(BF16)
        live[...] = (z > 0.0).astype(F32)

    hub_scale, agg1_hub, h1_hub, live_hub = call(
        hub_first,
        "hub_first",
        [shaped(hr, LANES, F32), shaped(hr, feat, BF16), shaped(hr, units, BF16), shaped(hr, units, F32)],
        [hub_feats, w_first, parts1[0]] + got1,
    )

    first, second = low_feats[:tile], low_feats[tile:]
    pieces1 = gather_wide(first, second)
    n_pieces = len(pieces1)

    def low_first(adj, link, link_t, scale, field, w, act_hub, *refs):
        pieces, refs = refs[:n_pieces], refs[n_pieces:]
        hubs, refs = refs[:n_hub], refs[n_hub:]
        agg, act_a, act_b, live, own, *sends = refs
        around = jnp.concatenate([r[...] for r in hubs] * 2, axis=0)
        s = tile_sum(adj, pieces) + field[...].astype(F32) + dot(link_t[...], around)
        a = (s * scale[:, :1]).astype(BF16)
        agg[...] = a
        z = dot(a, w[...])
        act = jnp.maximum(z, 0.0).astype(BF16)
        act_a[...] = act[:tile]
        act_b[...] = act[tile:]
        live[...] = (z > 0.0).astype(BF16)
        sums = dot(link[:, :rows], act) + dot(link[:, rows:], act)
        own[...] = sums[:hr]
        for k, send in enumerate(sends, 1):
            send[:hr] = act_hub[...].astype(F32)
            send[hr:] = sums[k * hr : (k + 1) * hr]

    agg1, h1_a, h1_b, live, own2, *sends2 = call(
        low_first,
        "low_first",
        [
            shaped(rows, feat, BF16),
            shaped(tile, units, BF16),
            shaped(rows - tile, units, BF16),
            shaped(rows, units, BF16),
            shaped(hr, units, F32),
        ]
        + [shaped(2 * hr, units, F32) for _ in mates],
        [adj, link, link_t, scale, low_feats, w_first, h1_hub] + pieces1 + [hub_feats] + feats_mates,
    )
    pieces2 = gather_wide(h1_a, h1_b)
    got2 = [to_hub(x, k) for k, x in enumerate(sends2, 1)]

    def hub_second(act, hub_scale, w, labels, own, *refs):
        got, (logits, agg, dz, q) = refs[:-4], refs[-4:]
        sums = own[...]
        for g in got:
            sums = sums + g[hr:]
        s = hub_scale[:, :1]
        a = ((act[...].astype(F32) + sums) * s).astype(BF16)
        agg[...] = a
        y = dot(a, w[...])
        logits[...] = y
        target = (lax.broadcasted_iota(jnp.int32, (hr, classes), 1) == labels[...]).astype(F32)
        d = ((y - target) / total).astype(BF16)
        dz[...] = d
        q[...] = (dot_nt(d, w[...]) * s).astype(BF16)

    hub_logits, agg2_hub, dz2_hub, q_hub = call(
        hub_second,
        "hub_second",
        [shaped(hr, classes, F32), shaped(hr, units, BF16), shaped(hr, classes, BF16), shaped(hr, units, BF16)],
        [h1_hub, hub_scale, w_second, hub_labels.reshape(hr, 1), own2] + got2,
    )

    def low_second(adj, link, link_t, scale, act_a, act_b, w, labels, act_hub, agg_hub, dz_hub, q_hub, *refs):
        pieces, refs = refs[:n_pieces], refs[n_pieces:]
        got, refs = refs[: n_hub - 1], refs[n_hub - 1 :]
        logits, grad, q_out, own, *sends = refs
        around = jnp.concatenate([act_hub[...]] + [g[:hr].astype(BF16) for g in got], axis=0)
        around = jnp.concatenate([around, around], axis=0)
        field = jnp.concatenate([act_a[...], act_b[...]], axis=0).astype(F32)
        s = tile_sum(adj, pieces) + field + dot(link_t[...], around)
        a = (s * scale[:, :1]).astype(BF16)
        y = dot(a, w[...])
        logits[...] = y
        target = (lax.broadcasted_iota(jnp.int32, (rows, classes), 1) == labels[...]).astype(F32)
        d = ((y - target) / total).astype(BF16)
        q = (dot_nt(d, w[...]) * scale[:, :1]).astype(BF16)
        q_out[...] = q
        grad[...] = dot_tn(a, d) + dot_tn(agg_hub[...], dz_hub[...])
        sums = dot(link[:, :rows], q) + dot(link[:, rows:], q)
        own[...] = sums[:hr]
        for k, send in enumerate(sends, 1):
            send[:hr] = q_hub[...].astype(F32)
            send[hr:] = sums[k * hr : (k + 1) * hr]

    low_logits, grad_second, q_low, own3, *sends3 = call(
        low_second,
        "low_second",
        [shaped(rows, classes, F32), shaped(units, classes, F32), shaped(rows, units, BF16), shaped(hr, units, F32)]
        + [shaped(2 * hr, units, F32) for _ in mates],
        [adj, link, link_t, scale, h1_a, h1_b, w_second, low_labels.reshape(rows, 1), h1_hub, agg2_hub, dz2_hub, q_hub]
        + pieces2
        + got2,
    )
    q_mate = to_wide(q_low, 1)
    got3 = [to_hub(x, k) for k, x in enumerate(sends3, 1)]

    quarter = nz * tile

    def transposed(adj_t, adj_t_mate, q, q_mate, keep_a, keep_b, send_x, *sends_z):
        def terms(at, n):
            return dot(adj_t[at : at + n], q[...]) + dot(adj_t_mate[at : at + n], q_mate[...])

        send_x[...] = terms(quarter, quarter).astype(BF16)
        for k, send in enumerate(sends_z, 1):
            send[...] = terms(2 * quarter + 2 * k * tile, 2 * tile).astype(BF16)
        keep_a[...] = terms(0, quarter)
        keep_b[...] = terms(2 * quarter, 2 * tile)

    keep_a, keep_b, send_x, *sends_z = call(
        transposed,
        "transposed",
        [shaped(quarter, units, F32), shaped(2 * tile, units, F32), shaped(quarter, units, BF16)]
        + [shaped(2 * tile, units, BF16) for _ in range(1, nz)],
        [adj_t, adj_t_mate, q_low, q_mate],
    )
    got_x = to_wide(send_x, 2)
    gots_z = [to_wide(x, 4 * k) for k, x in enumerate(sends_z, 1)]

    def sum_x(keep, got, own, *sends):
        own[...] = keep[:tile] + got[:tile].astype(F32)
        for k, send in enumerate(sends, 1):
            at = slice(k * tile, (k + 1) * tile)
            send[...] = (keep[at] + got[at].astype(F32)).astype(BF16)

    own_a, *sends_a = call(
        sum_x,
        "sum_x",
        [shaped(tile, units, F32)] + [shaped(tile, units, BF16) for _ in range(1, nz)],
        [keep_a, got_x],
    )
    gots_a = [to_wide(x, 4 * k) for k, x in enumerate(sends_a, 1)]

    def sum_z(keep, *refs):
        gots, (own, send) = refs[:-2], refs[-2:]
        s = keep[...]
        for g in gots:
            s = s + g[...].astype(F32)
        own[...] = s[:tile]
        send[...] = s[tile:].astype(BF16)

    own_b, send_b = call(sum_z, "sum_z", [shaped(tile, units, F32), shaped(tile, units, BF16)], [keep_b] + gots_z)
    got_b = to_wide(send_b, 2)

    def back_first(own_a, own_b, got_b, q, live, link_t, agg, agg_hub, q_hub, live_hub, own3, grad_second, *refs):
        gots_a, refs = refs[: nz - 1], refs[nz - 1 :]
        got3, (keep, give) = refs[: n_hub - 1], refs[n_hub - 1 :]
        back_a = own_a[...]
        for g in gots_a:
            back_a = back_a + g[...].astype(F32)
        back_b = own_b[...] + got_b[...].astype(F32)
        around = jnp.concatenate([q_hub[...]] + [g[:hr].astype(BF16) for g in got3], axis=0)
        around = jnp.concatenate([around, around], axis=0)
        dh = q[...].astype(F32) + jnp.concatenate([back_a, back_b], axis=0) + dot(link_t[...], around)
        dz = jnp.where(live[...].astype(F32) > 0.0, dh, 0.0).astype(BF16)
        sums = own3[...]
        for g in got3:
            sums = sums + g[hr:]
        dh_hub = q_hub[...].astype(F32) + sums
        dz_hub = jnp.where(live_hub[...] > 0.0, dh_hub, 0.0).astype(BF16)
        grad = dot_tn(agg[...], dz) + dot_tn(agg_hub[...], dz_hub)
        core = lax.axis_index(WIDE) & 1

        @pl.when(core == 0)
        def _():
            keep[...] = grad
            give[...] = grad_second[...]

        @pl.when(core == 1)
        def _():
            keep[...] = grad_second[...]
            give[...] = grad

    keep, give = call(
        back_first,
        "back_first",
        [shaped(units, classes, F32), shaped(units, classes, F32)],
        [own_a, own_b, got_b, q_low, live, link_t, agg1, agg1_hub, q_hub, live_hub, own3, grad_second] + gots_a + got3,
    )
    got = to_wide(give, 1)

    n_share = 2 * n_hub
    share = units // n_share
    steps = [(2 * (k // n_hub), k % n_hub) for k in range(n_share)]

    def place_of():
        return ((lax.axis_index(WIDE) >> 1) & 1) * n_hub + lax.axis_index(HUB)

    def split(keep, got, *outs):
        me = place_of()
        for k, out in enumerate(outs):
            at = pl.ds(pl.multiple_of((me ^ k) * share, share), share)
            out[...] = keep[at] + got[at]

    shares = call(split, "split", [shaped(share, classes, F32) for _ in range(n_share)], [keep, got])
    shares = [shares[0]] + [to_both(shares[k], *steps[k]) for k in range(1, n_share)]

    def add_up(*refs):
        refs[-1][...] = pairwise([r[...] for r in refs[:-1]])

    (mine,) = call(add_up, "add_xy", [shaped(share, classes, F32)], shares)
    (mine,) = call(
        add_up, "add_z", [shaped(share, classes, F32)], [mine] + [to_wide(mine, 4 * k) for k in range(1, nz)]
    )
    mine = [mine] + [to_both(mine, *steps[k]) for k in range(1, n_share)]
    other = [to_wide(m, 1) for m in mine]

    def assemble(*refs):
        mine, other, (grad_first, grad_second) = refs[:n_share], refs[n_share : 2 * n_share], refs[2 * n_share :]
        me = place_of()
        core = lax.axis_index(WIDE) & 1

        def write(mine_out, other_out):
            for k in range(n_share):
                at = pl.ds(pl.multiple_of((me ^ k) * share, share), share)
                mine_out[at] = mine[k][...]
                other_out[at] = other[k][...]

        @pl.when(core == 0)
        def _():
            write(grad_first, grad_second)

        @pl.when(core == 1)
        def _():
            write(grad_second, grad_first)

    grad_first, grad_second = call(
        assemble, "assemble", [shaped(units, classes, F32), shaped(units, classes, F32)], mine + other
    )
    return (low_logits, hub_logits, grad_first, grad_second)


def solution(mesh):
    in_specs = (
        P((WIDE, HUB), None),
        P((WIDE, HUB), None),
        P(),
        P(),
        P((WIDE, HUB), None, None),
        P((WIDE, HUB), None),
        P((WIDE, HUB)),
        P((WIDE, HUB)),
        P((WIDE, HUB)),
        P((WIDE, HUB)),
    )
    out_specs = (P((WIDE, HUB), None), P((WIDE, HUB), None), P(), P())
    return jax.shard_map(local, mesh=mesh, in_specs=in_specs, out_specs=out_specs, check_vma=False)
```

time: 341 us -> 140 us (0.41)
  waiting for transfers between devices: 252 us -> 48.8 us
  starting transfers between devices: 0.3 us -> 54.4 us
  blocking collectives: 19.3 us -> 0 us
  other arithmetic: 17.1 us -> 0.03 us
  between operations: 16.6 us -> 0.92 us
  matrix products: 15.1 us -> 0 us
  Pallas kernels: 0 us -> 13.4 us
    psum x1 -> x0, waiting for transfers between devices: 132 us -> none  [local(): lax.psum((grad_first, grad_second), ('wide', 'hub'))]
    all_gather x2 -> x0, waiting for transfers between devices: 65.3 us -> none  [low_side(): gathered = lax.all_gather(field_low, 'wide', axis=0, tiled=True)]
    ppermute x0 -> x56, starting transfers between devices: none -> 54.4 us  [the longest x46 43.3 us: to_wide(): lax.ppermute(x, WIDE, [(i, i ^ k) for i in range(lax.axis_size(WIDE))])]
    reduce_scatter x4 -> x0, waiting for transfers between devices: 53.8 us -> none  [the longest x1 53 us: local(): lax.psum_scatter(placed.astype(jnp.bfloat16), 'wide', scatter_dimension=0...]
    ppermute x0 -> x56, waiting for transfers between devices: none -> 48.8 us  [the longest x46 37.9 us: to_wide(): lax.ppermute(x, WIDE, [(i, i ^ k) for i in range(lax.axis_size(WIDE))])]
    dot_general x19 -> x0, matrix products: 15.1 us -> none  [the longest x3 3.17 us: to_hubs(): jnp.einsum('gr,rf->gf', link_bf, field_low, preferred_element_type=jnp.fl...]
    all_gather x3 -> x0, blocking collectives: 14.3 us -> none  [the longest x2 9.93 us: mirrors(): return lax.all_gather(field, 'hub', axis=0, tiled=True)]
    pallas_call x0 -> x13, Pallas kernels: none -> 13.4 us  [call(): pl.pallas_call(body, name=name, out_shape=outs, in_specs=[pl.BlockSpec(me...]
  transfers between devices with their start and end apart: 7 -> 56, of which waited for: 5 -> 27; matrix products, arithmetic and copies ran while one was open for 12% -> 3% of each run, Pallas kernels for 0% -> 7%
where the time goes in v1:
time: 140 us
  starting transfers between devices  54.4 us (39%)
  waiting for transfers between devices  48.8 us (35%)
  local copies, waits for them, and re-layouts  22.1 us (16%)
  Pallas kernels  13.4 us (10%)
    ppermute x46, starting transfers between devices, to_wide(): lax.ppermute(x, WIDE, [(i, i ^ k) for i in range(lax.axis_size(WIDE))])  43.3 us
    ppermute x46, waiting for transfers between devices, to_wide(): lax.ppermute(x, WIDE, [(i, i ^ k) for i in range(lax.axis_size(WIDE))])  37.9 us
    unnamed x74, local copies, waits for them, and re-layouts  18.3 us
    pallas_call x13, Pallas kernels, call(): pl.pallas_call(body, name=name, out_shape=outs, in_specs=[pl.BlockSpec(me...  13.4 us
    ppermute x6, starting transfers between devices, to_both(): return lax.ppermute(x, (WIDE, HUB), pairs)  7.11 us
    ppermute x6, waiting for transfers between devices, to_both(): return lax.ppermute(x, (WIDE, HUB), pairs)  6.79 us
    ppermute x4, waiting for transfers between devices, to_hub(): return lax.ppermute(x, HUB, [(i, i ^ k) for i in range(n_hub)])  4.1 us
    ppermute x4, starting transfers between devices, to_hub(): return lax.ppermute(x, HUB, [(i, i ^ k) for i in range(n_hub)])  4.02 us
  transfers between devices with their start and end apart: 56, of which 27 were waited for; matrix products, arithmetic and copies ran while one was open for 3% of the time, Pallas kernels for 7%

profile of v1, /device:TPU:0, one launch (start us, length us, event | category | flops | bytes accessed | tf_op | source)
XLA Modules:
  0.0 139.7 jit_solution(11135331703345841667)
XLA Ops:
  1.6 5.1 %collective-permute-start.3 = (bf16[128,256]{1,0:T(8,128)(2,1)S(1)}, bf16[128,256]{1,0:T(8,128)(2,1)S(1)}, u32[]{:S(2)}, u32[]{:S(2)}) collective-permute-start(bf16[128,256]{1,0:T(8,128)(2,1)S(1)} %get-tuple-element.99), channel_id=1, source_target_pairs={{0,24},{2,26},{4,28},{6,30},{8,16},{10,18},{12,20},{14,22},{16,8},... | collective-permute-start | bytes 196616 | tf_op jit(solution)/shard_map/ppermute | solution.py:45
  7.3 1.6 %collective-permute-start.5 = (bf16[128,256]{1,0:T(8,128)(2,1)S(1)}, bf16[128,256]{1,0:T(8,128)(2,1)S(1)}, u32[]{:S(2)}, u32[]{:S(2)}) collective-permute-start(bf16[128,256]{1,0:T(8,128)(2,1)S(1)} %get-tuple-element.98), channel_id=1, source_target_pairs={{0,4},{2,6},{4,0},{6,2},{8,12},{10,14},{12,8},{14,10},{16,20},{18,... | collective-permute-start | bytes 196616 | tf_op jit(solution)/shard_map/ppermute | solution.py:45
  9.3 3.0 %collective-permute-done.2 = bf16[128,256]{1,0:T(8,128)(2,1)S(1)} collective-permute-done((bf16[128,256]{1,0:T(8,128)(2,1)S(1)}, bf16[128,256]{1,0:T(8,128)(2,1)S(1)}, u32[]{:S(2)}, u32[]{:S(2)}) %collective-permute-start.2) | collective-permute-done | bytes 65568 | tf_op jit(solution)/shard_map/ppermute | solution.py:45
  12.3 1.6 %collective-permute-start.4 = (bf16[512,256]{1,0:T(8,128)(2,1)S(1)}, bf16[512,256]{1,0:T(8,128)(2,1)S(1)}, u32[]{:S(2)}, u32[]{:S(2)}) collective-permute-start(bf16[512,256]{1,0:T(8,128)(2,1)S(1)} %pad_maximum_fusion.refs_0_), channel_id=1, source_target_pairs={{0,4},{2,6},{4,0},{6,2},{8,12},{10,14},{12,8},{14,10},{16,20},{18,... | collective-permute-start | bytes 786440 | tf_op jit(solution)/shard_map/ppermute | solution.py:45
  18.1 4.8 %prep.1 = (bf16[256,4096]{1,0:T(8,128)(2,1)S(1)}, bf16[2048,256]{1,0:T(8,128)(2,1)S(1)}, bf16[2048,256]{1,0:T(8,128)(2,1)}, bf16[32,512]{1,0:T(8,128)(2,1)S(1)},...) custom-call(bf16[32,128,128]{2,1,0:T(8,128)(2,1)S(1)} %copy-done.1, ...), custom_call_target="tpu_custom_call" | custom-call | tf_op jit(solution)/shard_map/prep/pallas_call | solution.py:21
  22.9 1.5 %collective-permute-start = (f32[16,384]{1,0:T(8,128)S(1)}, f32[16,384]{1,0:T(8,128)S(1)}, u32[]{:S(2)}, u32[]{:S(2)}) collective-permute-start(f32[16,384]{1,0:T(8,128)S(1)} %get-tuple-element.56), channel_id=1, source_target_pairs={{0,1},{1,0},{2,3},{3,2},{4,5},{5,4},{6,7},{7,6},{8,9},{9,8},{10,11... | collective-permute-start | bytes 73736 | tf_op jit(solution)/shard_map/ppermute | solution.py:171
  25.0 2.7 %collective-permute-start.8 = (bf16[256,256]{1,0:T(8,128)(2,1)S(1)}, bf16[256,256]{1,0:T(8,128)(2,1)S(1)}, u32[]{:S(2)}, u32[]{:S(2)}) collective-permute-start(bf16[256,256]{1,0:T(8,128)(2,1)S(1)} %pad_maximum_fusion.1.refs_2_), channel_id=1, source_target_pairs={{0,24},{2,26},{4,28},{6,30},{8,16},{10,18},{12,20},{14,22},{16,8},... | collective-permute-start | bytes 393224 | tf_op jit(solution)/shard_map/ppermute | solution.py:45
  28.1 1.6 %collective-permute-start.7 = (bf16[256,256]{1,0:T(8,128)(2,1)S(1)}, bf16[256,256]{1,0:T(8,128)(2,1)S(1)}, u32[]{:S(2)}, u32[]{:S(2)}) collective-permute-start(bf16[256,256]{1,0:T(8,128)(2,1)S(1)} %pad_maximum_fusion.1.refs_2_), channel_id=1, source_target_pairs={{0,16},{2,18},{4,20},{6,22},{8,24},{10,26},{12,28},{14,30},{16,0},... | collective-permute-start | bytes 393224 | tf_op jit(solution)/shard_map/ppermute | solution.py:45
  29.7 1.7 %collective-permute-start.6 = (bf16[256,256]{1,0:T(8,128)(2,1)S(1)}, bf16[256,256]{1,0:T(8,128)(2,1)S(1)}, u32[]{:S(2)}, u32[]{:S(2)}) collective-permute-start(bf16[256,256]{1,0:T(8,128)(2,1)S(1)} %pad_maximum_fusion.1.refs_2_), channel_id=1, source_target_pairs={{0,8},{2,10},{4,12},{6,14},{8,0},{10,2},{12,4},{14,6},{16,24},{18,... | collective-permute-start | bytes 393224 | tf_op jit(solution)/shard_map/ppermute | solution.py:45
  33.2 6.1 %collective-permute-done.7.refs_4_ = bf16[256,256]{1,0:T(8,128)(2,1)S(1)} collective-permute-done((bf16[256,256]{1,0:T(8,128)(2,1)S(1)}, bf16[256,256]{1,0:T(8,128)(2,1)S(1)}, u32[]{:S(2)}, u32[]{:S(2)}) %collective-permute-start.7) | collective-permute-done | bytes 131104 | tf_op jit(solution)/shard_map/ppermute | solution.py:45
  42.0 2.0 %collective-permute-start.19 = (bf16[128,256]{1,0:T(8,128)(2,1)S(1)}, bf16[128,256]{1,0:T(8,128)(2,1)S(1)}, u32[]{:S(2)}, u32[]{:S(2)}) collective-permute-start(bf16[128,256]{1,0:T(8,128)(2,1)S(1)} %get-tuple-element.58.act_a), channel_id=1, source_target_pairs={{0,24},{2,26},{4,28},{6,30},{8,16},{10,18},{12,20},{14,22},{16,8},... | collective-permute-start | bytes 196616 | tf_op jit(solution)/shard_map/ppermute | solution.py:45
  44.0 2.4 %collective-permute-start.17 = (bf16[128,256]{1,0:T(8,128)(2,1)S(1)}, bf16[128,256]{1,0:T(8,128)(2,1)S(1)}, u32[]{:S(2)}, u32[]{:S(2)}) collective-permute-start(bf16[128,256]{1,0:T(8,128)(2,1)S(1)} %get-tuple-element.58.act_a), channel_id=1, source_target_pairs={{0,8},{2,10},{4,12},{6,14},{8,0},{10,2},{12,4},{14,6},{16,24},{18,... | collective-permute-start | bytes 196616 | tf_op jit(solution)/shard_map/ppermute | solution.py:45
  47.6 2.6 %collective-permute-done.17 = bf16[128,256]{1,0:T(8,128)(2,1)S(1)} collective-permute-done((bf16[128,256]{1,0:T(8,128)(2,1)S(1)}, bf16[128,256]{1,0:T(8,128)(2,1)S(1)}, u32[]{:S(2)}, u32[]{:S(2)}) %collective-permute-start.17) | collective-permute-done | bytes 65568 | tf_op jit(solution)/shard_map/ppermute | solution.py:45
  54.4 2.1 %collective-permute-start.24 = (bf16[256,256]{1,0:T(8,128)(2,1)S(1)}, bf16[256,256]{1,0:T(8,128)(2,1)S(1)}, u32[]{:S(2)}, u32[]{:S(2)}) collective-permute-start(bf16[256,256]{1,0:T(8,128)(2,1)S(1)} %constant_dynamic-update-slice_fusion.4.refs_2_), channel_id=1, source_target_pairs={{0,24},{2,26},{4,28},{6,30},{8,16},{10,18},{12,20},{14,22},{16,8},... | collective-permute-start | bytes 393224 | tf_op jit(solution)/shard_map/ppermute | solution.py:45
  63.3 5.8 %collective-permute-done.23.refs_4_ = bf16[256,256]{1,0:T(8,128)(2,1)} collective-permute-done((bf16[256,256]{1,0:T(8,128)(2,1)S(1)}, bf16[256,256]{1,0:T(8,128)(2,1)}, u32[]{:S(2)}, u32[]{:S(2)}) %collective-permute-start.23) | collective-permute-done | bytes 131104 | tf_op jit(solution)/shard_map/ppermute | solution.py:45
  82.2 3.2 %low_second.1 = (f32[256,256]{1,0:T(8,128)}, f32[256,256]{1,0:T(8,128)S(1)}, bf16[256,256]{1,0:T(8,128)(2,1)S(1)}, f32[16,256]{1,0:T(8,128)S(1)}, f32[32,256]{1,0:T(8,128)S(1)}) custom-call(bf16[256,4096]{1,0:T(8,128)(2,1)S(1)} %get-tuple-element.51.adj, bf16[32,512]{1,0:T(8,128)(2,1)S(1)} %copy-done.10, bf16[256,64]{1,0:T(8,128)(2,1)S(1)} %get-tuple-element.53.link_t, ...), custom_call_target="tpu_custom_call" | custom-call | tf_op jit(solution)/shard_map/low_second/pallas_call | solution.py:21
  86.8 1.9 %transposed.1 = (f32[512,256]{1,0:T(8,128)S(1)}, f32[256,256]{1,0:T(8,128)S(1)}, bf16[512,256]{1,0:T(8,128)(2,1)S(1)}, bf16[256,256]{1,0:T(8,128)(2,1)S(1)}, bf1...) custom-call(bf16[2048,256]{1,0:T(8,128)(2,1)S(1)} %get-tuple-element.68.adj_t, ...), custom_call_target="tpu_custom_call" | custom-call | tf_op jit(solution)/shard_map/transposed/pallas_call | solution.py:21
  88.8 1.5 %collective-permute-start.33 = (bf16[512,256]{1,0:T(8,128)(2,1)S(1)}, bf16[512,256]{1,0:T(8,128)(2,1)S(1)}, u32[]{:S(2)}, u32[]{:S(2)}) collective-permute-start(bf16[512,256]{1,0:T(8,128)(2,1)S(1)} %get-tuple-element.72), channel_id=1, source_target_pairs={{0,4},{2,6},{4,0},{6,2},{8,12},{10,14},{12,8},{14,10},{16,20},{18,... | collective-permute-start | bytes 786440 | tf_op jit(solution)/shard_map/ppermute | solution.py:45
  90.3 2.4 %collective-permute-start.35 = (bf16[256,256]{1,0:T(8,128)(2,1)S(1)}, bf16[256,256]{1,0:T(8,128)(2,1)S(1)}, u32[]{:S(2)}, u32[]{:S(2)}) collective-permute-start(bf16[256,256]{1,0:T(8,128)(2,1)S(1)} %get-tuple-element.76), channel_id=1, source_target_pairs={{0,16},{2,18},{4,20},{6,22},{8,24},{10,26},{12,28},{14,30},{16,0},... | collective-permute-start | bytes 393224 | tf_op jit(solution)/shard_map/ppermute | solution.py:45
  92.7 2.0 %collective-permute-start.36 = (bf16[256,256]{1,0:T(8,128)(2,1)S(1)}, bf16[256,256]{1,0:T(8,128)(2,1)S(1)}, u32[]{:S(2)}, u32[]{:S(2)}) collective-permute-start(bf16[256,256]{1,0:T(8,128)(2,1)S(1)} %get-tuple-element.77), channel_id=1, source_target_pairs={{0,24},{2,26},{4,28},{6,30},{8,16},{10,18},{12,20},{14,22},{16,8},... | collective-permute-start | bytes 393224 | tf_op jit(solution)/shard_map/ppermute | solution.py:45
  94.7 2.8 %collective-permute-done.34.refs_0_ = bf16[256,256]{1,0:T(8,128)(2,1)S(1)} collective-permute-done((bf16[256,256]{1,0:T(8,128)(2,1)S(1)}, bf16[256,256]{1,0:T(8,128)(2,1)S(1)}, u32[]{:S(2)}, u32[]{:S(2)}) %collective-permute-start.34) | collective-permute-done | bytes 131104 | tf_op jit(solution)/shard_map/ppermute | solution.py:45
  97.5 5.7 %collective-permute-done.35.refs_1_ = bf16[256,256]{1,0:T(8,128)(2,1)S(1)} collective-permute-done((bf16[256,256]{1,0:T(8,128)(2,1)S(1)}, bf16[256,256]{1,0:T(8,128)(2,1)S(1)}, u32[]{:S(2)}, u32[]{:S(2)}) %collective-permute-start.35) | collective-permute-done | bytes 131104 | tf_op jit(solution)/shard_map/ppermute | solution.py:45
  103.9 2.4 %collective-permute-start.38 = (bf16[128,256]{1,0:T(8,128)(2,1)S(1)}, bf16[128,256]{1,0:T(8,128)(2,1)S(1)}, u32[]{:S(2)}, u32[]{:S(2)}) collective-permute-start(bf16[128,256]{1,0:T(8,128)(2,1)S(1)} %get-tuple-element.86), channel_id=1, source_target_pairs={{0,8},{2,10},{4,12},{6,14},{8,0},{10,2},{12,4},{14,6},{16,24},{18,... | collective-permute-start | bytes 196616 | tf_op jit(solution)/shard_map/ppermute | solution.py:45
  106.7 2.0 %collective-permute-start.40 = (bf16[128,256]{1,0:T(8,128)(2,1)S(1)}, bf16[128,256]{1,0:T(8,128)(2,1)S(1)}, u32[]{:S(2)}, u32[]{:S(2)}) collective-permute-start(bf16[128,256]{1,0:T(8,128)(2,1)S(1)} %get-tuple-element.88), channel_id=1, source_target_pairs={{0,24},{2,26},{4,28},{6,30},{8,16},{10,18},{12,20},{14,22},{16,8},... | collective-permute-start | bytes 196616 | tf_op jit(solution)/shard_map/ppermute | solution.py:45
  109.2 3.4 %collective-permute-done.41.refs_3_ = f32[32,256]{1,0:T(8,128)S(1)} collective-permute-done((f32[32,256]{1,0:T(8,128)S(1)}, f32[32,256]{1,0:T(8,128)S(1)}, u32[]{:S(2)}, u32[]{:S(2)}) %collective-permute-start.41) | collective-permute-done | bytes 32800 | tf_op jit(solution)/shard_map/ppermute | solution.py:171
  113.6 1.5 %collective-permute-done.42.got = f32[256,256]{1,0:T(8,128)S(1)} collective-permute-done((f32[256,256]{1,0:T(8,128)S(1)}, f32[256,256]{1,0:T(8,128)S(1)}, u32[]{:S(2)}, u32[]{:S(2)}) %collective-permute-start.42) | collective-permute-done | bytes 262176 | tf_op jit(solution)/shard_map/ppermute | solution.py:45
  120.0 2.4 %collective-permute-done.45.refs_3_ = f32[64,256]{1,0:T(8,128)S(1)} collective-permute-done((f32[64,256]{1,0:T(8,128)S(1)}, f32[64,256]{1,0:T(8,128)S(1)}, u32[]{:S(2)}, u32[]{:S(2)}) %collective-permute-start.45) | collective-permute-done | bytes 65568 | tf_op jit(solution)/shard_map/ppermute | solution.py:51
  122.4 2.0 %collective-permute-start.48 = (f32[64,256]{1,0:T(8,128)S(1)}, f32[64,256]{1,0:T(8,128)S(1)}, u32[]{:S(2)}, u32[]{:S(2)}) collective-permute-start(f32[64,256]{1,0:T(8,128)S(1)} %add_xy.1.refs_0_), channel_id=1, source_target_pairs={{0,24},{2,26},{4,28},{6,30},{8,16},{10,18},{12,20},{14,22},{16,8},... | collective-permute-start | bytes 196616 | tf_op jit(solution)/shard_map/ppermute | solution.py:45
  125.2 1.7 %collective-permute-start.46 = (f32[64,256]{1,0:T(8,128)S(1)}, f32[64,256]{1,0:T(8,128)S(1)}, u32[]{:S(2)}, u32[]{:S(2)}) collective-permute-start(f32[64,256]{1,0:T(8,128)S(1)} %add_xy.1.refs_0_), channel_id=1, source_target_pairs={{0,8},{2,10},{4,12},{6,14},{8,0},{10,2},{12,4},{14,6},{16,24},{18,... | collective-permute-start | bytes 196616 | tf_op jit(solution)/shard_map/ppermute | solution.py:45
  126.9 2.3 %collective-permute-done.48.refs_3_ = f32[64,256]{1,0:T(8,128)S(1)} collective-permute-done((f32[64,256]{1,0:T(8,128)S(1)}, f32[64,256]{1,0:T(8,128)S(1)}, u32[]{:S(2)}, u32[]{:S(2)}) %collective-permute-start.48) | collective-permute-done | bytes 65568 | tf_op jit(solution)/shard_map/ppermute | solution.py:45
  129.2 1.7 %collective-permute-done.47.refs_2_ = f32[64,256]{1,0:T(8,128)S(1)} collective-permute-done((f32[64,256]{1,0:T(8,128)S(1)}, f32[64,256]{1,0:T(8,128)S(1)}, u32[]{:S(2)}, u32[]{:S(2)}) %collective-permute-start.47) | collective-permute-done | bytes 65568 | tf_op jit(solution)/shard_map/ppermute | solution.py:45
  134.5 1.7 %collective-permute-done.51.refs_3_ = f32[64,256]{1,0:T(8,128)S(1)} collective-permute-done((f32[64,256]{1,0:T(8,128)S(1)}, f32[64,256]{1,0:T(8,128)S(1)}, u32[]{:S(2)}, u32[]{:S(2)}) %collective-permute-start.51) | collective-permute-done | bytes 65568 | tf_op jit(solution)/shard_map/ppermute | solution.py:51
  (174 shorter events, 53.5 us)
Async XLA Ops:
  1.6 7.7 %collective-permute-start.3 = (bf16[128,256]{1,0:T(8,128)(2,1)S(1)}, bf16[128,256]{1,0:T(8,128)(2,1)S(1)}, u32[]{:S(2)}, u32[]{:S(2)}) collective-permute-start(bf16[128,256]{1,0:T(8,128)(2,1)S(1)} %get-tuple-element.99), channel_id=1, source_target_pairs={{0,24},{2,26},{4,28},{6,30},{8,16},{10,18},{12,20},{14,22},{16,8},... | collective-permute-start | bytes 196616 | tf_op jit(solution)/shard_map/ppermute | solution.py:45
  7.3 6.5 %collective-permute-start.5 = (bf16[128,256]{1,0:T(8,128)(2,1)S(1)}, bf16[128,256]{1,0:T(8,128)(2,1)S(1)}, u32[]{:S(2)}, u32[]{:S(2)}) collective-permute-start(bf16[128,256]{1,0:T(8,128)(2,1)S(1)} %get-tuple-element.98), channel_id=1, source_target_pairs={{0,4},{2,6},{4,0},{6,2},{8,12},{10,14},{12,8},{14,10},{16,20},{18,... | collective-permute-start | bytes 196616 | tf_op jit(solution)/shard_map/ppermute | solution.py:45
  12.3 19.1 %collective-permute-start.4 = (bf16[512,256]{1,0:T(8,128)(2,1)S(1)}, bf16[512,256]{1,0:T(8,128)(2,1)S(1)}, u32[]{:S(2)}, u32[]{:S(2)}) collective-permute-start(bf16[512,256]{1,0:T(8,128)(2,1)S(1)} %pad_maximum_fusion.refs_0_), channel_id=1, source_target_pairs={{0,4},{2,6},{4,0},{6,2},{8,12},{10,14},{12,8},{14,10},{16,20},{18,... | collective-permute-start | bytes 786440 | tf_op jit(solution)/shard_map/ppermute | solution.py:45
  13.9 17.5 %collective-permute-start.11 = (bf16[256,256]{1,0:T(8,128)(2,1)S(1)}, bf16[256,256]{1,0:T(8,128)(2,1)S(1)}, u32[]{:S(2)}, u32[]{:S(2)}) collective-permute-start(bf16[256,256]{1,0:T(8,128)(2,1)S(1)} %pad_maximum_fusion.1.refs_2_), channel_id=1, source_target_pairs={{0,2},{2,0},{4,6},{6,4},{8,10},{10,8},{12,14},{14,12},{16,18},{18,... | collective-permute-start | bytes 393224 | tf_op jit(solution)/shard_map/ppermute | solution.py:45
  22.9 6.8 %collective-permute-start = (f32[16,384]{1,0:T(8,128)S(1)}, f32[16,384]{1,0:T(8,128)S(1)}, u32[]{:S(2)}, u32[]{:S(2)}) collective-permute-start(f32[16,384]{1,0:T(8,128)S(1)} %get-tuple-element.56), channel_id=1, source_target_pairs={{0,1},{1,0},{2,3},{3,2},{4,5},{5,4},{6,7},{7,6},{8,9},{9,8},{10,11... | collective-permute-start | bytes 73736 | tf_op jit(solution)/shard_map/ppermute | solution.py:171
  25.0 8.2 %collective-permute-start.8 = (bf16[256,256]{1,0:T(8,128)(2,1)S(1)}, bf16[256,256]{1,0:T(8,128)(2,1)S(1)}, u32[]{:S(2)}, u32[]{:S(2)}) collective-permute-start(bf16[256,256]{1,0:T(8,128)(2,1)S(1)} %pad_maximum_fusion.1.refs_2_), channel_id=1, source_target_pairs={{0,24},{2,26},{4,28},{6,30},{8,16},{10,18},{12,20},{14,22},{16,8},... | collective-permute-start | bytes 393224 | tf_op jit(solution)/shard_map/ppermute | solution.py:45
  28.1 11.1 %collective-permute-start.7 = (bf16[256,256]{1,0:T(8,128)(2,1)S(1)}, bf16[256,256]{1,0:T(8,128)(2,1)S(1)}, u32[]{:S(2)}, u32[]{:S(2)}) collective-permute-start(bf16[256,256]{1,0:T(8,128)(2,1)S(1)} %pad_maximum_fusion.1.refs_2_), channel_id=1, source_target_pairs={{0,16},{2,18},{4,20},{6,22},{8,24},{10,26},{12,28},{14,30},{16,0},... | collective-permute-start | bytes 393224 | tf_op jit(solution)/shard_map/ppermute | solution.py:45
  29.7 9.6 %collective-permute-start.6 = (bf16[256,256]{1,0:T(8,128)(2,1)S(1)}, bf16[256,256]{1,0:T(8,128)(2,1)S(1)}, u32[]{:S(2)}, u32[]{:S(2)}) collective-permute-start(bf16[256,256]{1,0:T(8,128)(2,1)S(1)} %pad_maximum_fusion.1.refs_2_), channel_id=1, source_target_pairs={{0,8},{2,10},{4,12},{6,14},{8,0},{10,2},{12,4},{14,6},{16,24},{18,... | collective-permute-start | bytes 393224 | tf_op jit(solution)/shard_map/ppermute | solution.py:45
  31.4 9.4 %collective-permute-start.9 = (bf16[512,256]{1,0:T(8,128)(2,1)S(1)}, bf16[512,256]{1,0:T(8,128)(2,1)S(1)}, u32[]{:S(2)}, u32[]{:S(2)}) collective-permute-start(bf16[512,256]{1,0:T(8,128)(2,1)S(1)} %pad_maximum_fusion.refs_0_), channel_id=1, source_target_pairs={{0,2},{2,0},{4,6},{6,4},{8,10},{10,8},{12,14},{14,12},{16,18},{18,... | collective-permute-start | bytes 786440 | tf_op jit(solution)/shard_map/ppermute | solution.py:45
  31.4 9.4 %collective-permute-start.10 = (bf16[512,256]{1,0:T(8,128)(2,1)S(1)}, bf16[512,256]{1,0:T(8,128)(2,1)S(1)}, u32[]{:S(2)}, u32[]{:S(2)}) collective-permute-start(bf16[512,256]{1,0:T(8,128)(2,1)S(1)} %collective-permute-done.4.refs_1_), channel_id=1, source_target_pairs={{0,2},{2,0},{4,6},{6,4},{8,10},{10,8},{12,14},{14,12},{16,18},{18,... | collective-permute-start | bytes 786440 | tf_op jit(solution)/shard_map/ppermute | solution.py:45
  33.2 7.4 %collective-permute-start.14 = (bf16[256,256]{1,0:T(8,128)(2,1)S(1)}, bf16[256,256]{1,0:T(8,128)(2,1)S(1)}, u32[]{:S(2)}, u32[]{:S(2)}) collective-permute-start(bf16[256,256]{1,0:T(8,128)(2,1)S(1)} %collective-permute-done.8.refs_5_), channel_id=1, source_target_pairs={{0,2},{2,0},{4,6},{6,4},{8,10},{10,8},{12,14},{14,12},{16,18},{18,... | collective-permute-start | bytes 393224 | tf_op jit(solution)/shard_map/ppermute | solution.py:45
  40.6 45.0 %collective-permute-start.31 = (bf16[2048,256]{1,0:T(8,128)(2,1)}, bf16[2048,256]{1,0:T(8,128)(2,1)}, u32[]{:S(2)}, u32[]{:S(2)}) collective-permute-start(bf16[2048,256]{1,0:T(8,128)(2,1)} %get-tuple-element.69), channel_id=1, source_target_pairs={{0,2},{2,0},{4,6},{6,4},{8,10},{10,8},{12,14},{14,12},{16,18},{18,... | collective-permute-start | bytes 3145736 | tf_op jit(solution)/shard_map/ppermute | solution.py:45
  42.0 9.6 %collective-permute-start.19 = (bf16[128,256]{1,0:T(8,128)(2,1)S(1)}, bf16[128,256]{1,0:T(8,128)(2,1)S(1)}, u32[]{:S(2)}, u32[]{:S(2)}) collective-permute-start(bf16[128,256]{1,0:T(8,128)(2,1)S(1)} %get-tuple-element.58.act_a), channel_id=1, source_target_pairs={{0,24},{2,26},{4,28},{6,30},{8,16},{10,18},{12,20},{14,22},{16,8},... | collective-permute-start | bytes 196616 | tf_op jit(solution)/shard_map/ppermute | solution.py:45
  44.0 7.0 %collective-permute-start.18 = (bf16[128,256]{1,0:T(8,128)(2,1)S(1)}, bf16[128,256]{1,0:T(8,128)(2,1)S(1)}, u32[]{:S(2)}, u32[]{:S(2)}) collective-permute-start(bf16[128,256]{1,0:T(8,128)(2,1)S(1)} %get-tuple-element.58.act_a), channel_id=1, source_target_pairs={{0,16},{2,18},{4,20},{6,22},{8,24},{10,26},{12,28},{14,30},{16,0},... | collective-permute-start | bytes 196616 | tf_op jit(solution)/shard_map/ppermute | solution.py:45
  46.4 7.9 %collective-permute-start.21 = (bf16[128,256]{1,0:T(8,128)(2,1)S(1)}, bf16[128,256]{1,0:T(8,128)(2,1)S(1)}, u32[]{:S(2)}, u32[]{:S(2)}) collective-permute-start(bf16[128,256]{1,0:T(8,128)(2,1)S(1)} %get-tuple-element.59.act_b), channel_id=1, source_target_pairs={{0,4},{2,6},{4,0},{6,2},{8,12},{10,14},{12,8},{14,10},{16,20},{18,... | collective-permute-start | bytes 196616 | tf_op jit(solution)/shard_map/ppermute | solution.py:45
  52.3 16.9 %collective-permute-start.20 = (bf16[512,256]{1,0:T(8,128)(2,1)}, bf16[512,256]{1,0:T(8,128)(2,1)}, u32[]{:S(2)}, u32[]{:S(2)}) collective-permute-start(bf16[512,256]{1,0:T(8,128)(2,1)} %constant_dynamic-update-slice_fusion.refs_0_), channel_id=1, source_target_pairs={{0,4},{2,6},{4,0},{6,2},{8,12},{10,14},{12,8},{14,10},{16,20},{18,... | collective-permute-start | bytes 786440 | tf_op jit(solution)/shard_map/ppermute | solution.py:45
  54.4 8.3 %collective-permute-start.24 = (bf16[256,256]{1,0:T(8,128)(2,1)S(1)}, bf16[256,256]{1,0:T(8,128)(2,1)S(1)}, u32[]{:S(2)}, u32[]{:S(2)}) collective-permute-start(bf16[256,256]{1,0:T(8,128)(2,1)S(1)} %constant_dynamic-update-slice_fusion.4.refs_2_), channel_id=1, source_target_pairs={{0,24},{2,26},{4,28},{6,30},{8,16},{10,18},{12,20},{14,22},{16,8},... | collective-permute-start | bytes 393224 | tf_op jit(solution)/shard_map/ppermute | solution.py:45
  57.3 11.8 %collective-permute-start.23 = (bf16[256,256]{1,0:T(8,128)(2,1)S(1)}, bf16[256,256]{1,0:T(8,128)(2,1)}, u32[]{:S(2)}, u32[]{:S(2)}) collective-permute-start(bf16[256,256]{1,0:T(8,128)(2,1)S(1)} %constant_dynamic-update-slice_fusion.4.refs_2_), channel_id=1, source_target_pairs={{0,16},{2,18},{4,20},{6,22},{8,24},{10,26},{12,28},{14,30},{16,0},... | collective-permute-start | bytes 393224 | tf_op jit(solution)/shard_map/ppermute | solution.py:45
  59.2 10.4 %collective-permute-start.22 = (bf16[256,256]{1,0:T(8,128)(2,1)S(1)}, bf16[256,256]{1,0:T(8,128)(2,1)}, u32[]{:S(2)}, u32[]{:S(2)}) collective-permute-start(bf16[256,256]{1,0:T(8,128)(2,1)S(1)} %constant_dynamic-update-slice_fusion.4.refs_2_), channel_id=1, source_target_pairs={{0,8},{2,10},{4,12},{6,14},{8,0},{10,2},{12,4},{14,6},{16,24},{18,... | collective-permute-start | bytes 393224 | tf_op jit(solution)/shard_map/ppermute | solution.py:45
  62.7 7.1 %collective-permute-start.30 = (bf16[256,256]{1,0:T(8,128)(2,1)S(1)}, bf16[256,256]{1,0:T(8,128)(2,1)S(1)}, u32[]{:S(2)}, u32[]{:S(2)}) collective-permute-start(bf16[256,256]{1,0:T(8,128)(2,1)S(1)} %collective-permute-done.24.refs_5_), channel_id=1, source_target_pairs={{0,2},{2,0},{4,6},{6,4},{8,10},{10,8},{12,14},{14,12},{16,18},{18,... | collective-permute-start | bytes 393224 | tf_op jit(solution)/shard_map/ppermute | solution.py:45
  69.1 6.9 %collective-permute-start.25 = (bf16[512,256]{1,0:T(8,128)(2,1)}, bf16[512,256]{1,0:T(8,128)(2,1)}, u32[]{:S(2)}, u32[]{:S(2)}) collective-permute-start(bf16[512,256]{1,0:T(8,128)(2,1)} %constant_dynamic-update-slice_fusion.refs_0_), channel_id=1, source_target_pairs={{0,2},{2,0},{4,6},{6,4},{8,10},{10,8},{12,14},{14,12},{16,18},{18,... | collective-permute-start | bytes 786440 | tf_op jit(solution)/shard_map/ppermute | solution.py:45
  69.1 6.9 %collective-permute-start.26 = (bf16[512,256]{1,0:T(8,128)(2,1)}, bf16[512,256]{1,0:T(8,128)(2,1)}, u32[]{:S(2)}, u32[]{:S(2)}) collective-permute-start(bf16[512,256]{1,0:T(8,128)(2,1)} %collective-permute-done.20.refs_1_), channel_id=1, source_target_pairs={{0,2},{2,0},{4,6},{6,4},{8,10},{10,8},{12,14},{14,12},{16,18},{18,... | collective-permute-start | bytes 786440 | tf_op jit(solution)/shard_map/ppermute | solution.py:45
  69.6 6.4 %collective-permute-start.29 = (bf16[256,256]{1,0:T(8,128)(2,1)}, bf16[256,256]{1,0:T(8,128)(2,1)}, u32[]{:S(2)}, u32[]{:S(2)}) collective-permute-start(bf16[256,256]{1,0:T(8,128)(2,1)} %collective-permute-done.23.refs_4_), channel_id=1, source_target_pairs={{0,2},{2,0},{4,6},{6,4},{8,10},{10,8},{12,14},{14,12},{16,18},{18,... | collective-permute-start | bytes 393224 | tf_op jit(solution)/shard_map/ppermute | solution.py:45
  88.8 15.1 %collective-permute-start.33 = (bf16[512,256]{1,0:T(8,128)(2,1)S(1)}, bf16[512,256]{1,0:T(8,128)(2,1)S(1)}, u32[]{:S(2)}, u32[]{:S(2)}) collective-permute-start(bf16[512,256]{1,0:T(8,128)(2,1)S(1)} %get-tuple-element.72), channel_id=1, source_target_pairs={{0,4},{2,6},{4,0},{6,2},{8,12},{10,14},{12,8},{14,10},{16,20},{18,... | collective-permute-start | bytes 786440 | tf_op jit(solution)/shard_map/ppermute | solution.py:45
  90.3 7.2 %collective-permute-start.34 = (bf16[256,256]{1,0:T(8,128)(2,1)S(1)}, bf16[256,256]{1,0:T(8,128)(2,1)S(1)}, u32[]{:S(2)}, u32[]{:S(2)}) collective-permute-start(bf16[256,256]{1,0:T(8,128)(2,1)S(1)} %get-tuple-element.75), channel_id=1, source_target_pairs={{0,8},{2,10},{4,12},{6,14},{8,0},{10,2},{12,4},{14,6},{16,24},{18,... | collective-permute-start | bytes 393224 | tf_op jit(solution)/shard_map/ppermute | solution.py:45
  90.3 12.9 %collective-permute-start.35 = (bf16[256,256]{1,0:T(8,128)(2,1)S(1)}, bf16[256,256]{1,0:T(8,128)(2,1)S(1)}, u32[]{:S(2)}, u32[]{:S(2)}) collective-permute-start(bf16[256,256]{1,0:T(8,128)(2,1)S(1)} %get-tuple-element.76), channel_id=1, source_target_pairs={{0,16},{2,18},{4,20},{6,22},{8,24},{10,26},{12,28},{14,30},{16,0},... | collective-permute-start | bytes 393224 | tf_op jit(solution)/shard_map/ppermute | solution.py:45
  92.7 10.5 %collective-permute-start.36 = (bf16[256,256]{1,0:T(8,128)(2,1)S(1)}, bf16[256,256]{1,0:T(8,128)(2,1)S(1)}, u32[]{:S(2)}, u32[]{:S(2)}) collective-permute-start(bf16[256,256]{1,0:T(8,128)(2,1)S(1)} %get-tuple-element.77), channel_id=1, source_target_pairs={{0,24},{2,26},{4,28},{6,30},{8,16},{10,18},{12,20},{14,22},{16,8},... | collective-permute-start | bytes 393224 | tf_op jit(solution)/shard_map/ppermute | solution.py:45
  103.3 9.4 %collective-permute-start.37 = (bf16[128,256]{1,0:T(8,128)(2,1)S(1)}, bf16[128,256]{1,0:T(8,128)(2,1)S(1)}, u32[]{:S(2)}, u32[]{:S(2)}) collective-permute-start(bf16[128,256]{1,0:T(8,128)(2,1)S(1)} %get-tuple-element.79), channel_id=1, source_target_pairs={{0,4},{2,6},{4,0},{6,2},{8,12},{10,14},{12,8},{14,10},{16,20},{18,... | collective-permute-start | bytes 196616 | tf_op jit(solution)/shard_map/ppermute | solution.py:45
  103.9 8.7 %collective-permute-start.38 = (bf16[128,256]{1,0:T(8,128)(2,1)S(1)}, bf16[128,256]{1,0:T(8,128)(2,1)S(1)}, u32[]{:S(2)}, u32[]{:S(2)}) collective-permute-start(bf16[128,256]{1,0:T(8,128)(2,1)S(1)} %get-tuple-element.86), channel_id=1, source_target_pairs={{0,8},{2,10},{4,12},{6,14},{8,0},{10,2},{12,4},{14,6},{16,24},{18,... | collective-permute-start | bytes 196616 | tf_op jit(solution)/shard_map/ppermute | solution.py:45
  106.3 6.8 %collective-permute-start.39 = (bf16[128,256]{1,0:T(8,128)(2,1)S(1)}, bf16[128,256]{1,0:T(8,128)(2,1)S(1)}, u32[]{:S(2)}, u32[]{:S(2)}) collective-permute-start(bf16[128,256]{1,0:T(8,128)(2,1)S(1)} %get-tuple-element.87), channel_id=1, source_target_pairs={{0,16},{2,18},{4,20},{6,22},{8,24},{10,26},{12,28},{14,30},{16,0},... | collective-permute-start | bytes 196616 | tf_op jit(solution)/shard_map/ppermute | solution.py:45
  122.4 6.8 %collective-permute-start.48 = (f32[64,256]{1,0:T(8,128)S(1)}, f32[64,256]{1,0:T(8,128)S(1)}, u32[]{:S(2)}, u32[]{:S(2)}) collective-permute-start(f32[64,256]{1,0:T(8,128)S(1)} %add_xy.1.refs_0_), channel_id=1, source_target_pairs={{0,24},{2,26},{4,28},{6,30},{8,16},{10,18},{12,20},{14,22},{16,8},... | collective-permute-start | bytes 196616 | tf_op jit(solution)/shard_map/ppermute | solution.py:45
  124.4 6.4 %collective-permute-start.47 = (f32[64,256]{1,0:T(8,128)S(1)}, f32[64,256]{1,0:T(8,128)S(1)}, u32[]{:S(2)}, u32[]{:S(2)}) collective-permute-start(f32[64,256]{1,0:T(8,128)S(1)} %add_xy.1.refs_0_), channel_id=1, source_target_pairs={{0,16},{2,18},{4,20},{6,22},{8,24},{10,26},{12,28},{14,30},{16,0},... | collective-permute-start | bytes 196616 | tf_op jit(solution)/shard_map/ppermute | solution.py:45
  (59 other events, 448.4 us)

commit v2 on v1

v2 whole, which is shorter than its diff:
```python
import jax
import jax.numpy as jnp
from jax import lax
from jax.experimental import pallas as pl
from jax.experimental.pallas import tpu as pltpu
from jax.sharding import PartitionSpec as P

F32 = jnp.float32
BF16 = jnp.bfloat16
WIDE = "wide"
HUB = "hub"
LANES = 128
VMEM_BYTES = 16 * 1024 * 1024


def shaped(rows, cols, dtype):
    return jax.ShapeDtypeStruct((rows, cols), dtype)


def call(body, name, outs, ins, smem=(), traffic=1 << 20):
    spaces = [pltpu.SMEM if i in smem else pltpu.VMEM for i in range(len(ins))]
    return pl.pallas_call(
        body,
        name=name,
        out_shape=outs,
        in_specs=[pl.BlockSpec(memory_space=s) for s in spaces],
        out_specs=[pl.BlockSpec(memory_space=pltpu.VMEM) for _ in outs],
        cost_estimate=pl.CostEstimate(flops=0, bytes_accessed=traffic, transcendentals=0),
        compiler_params=pltpu.CompilerParams(vmem_limit_bytes=VMEM_BYTES),
    )(*ins)


def dot(a, b):
    return lax.dot_general(a, b, (((1,), (0,)), ((), ())), preferred_element_type=F32)


def dot_nt(a, b):
    return lax.dot_general(a, b, (((1,), (1,)), ((), ())), preferred_element_type=F32)


def dot_tn(a, b):
    return lax.dot_general(a, b, (((0,), (0,)), ((), ())), preferred_element_type=F32)


def to_wide(x, k):
    return lax.ppermute(x, WIDE, [(i, i ^ k) for i in range(lax.axis_size(WIDE))])


def to_both(x, k, j):
    n, m = lax.axis_size(WIDE), lax.axis_size(HUB)
    pairs = [(i * m + h, (i ^ k) * m + (h ^ j)) for i in range(n) for h in range(m)]
    return lax.ppermute(x, (WIDE, HUB), pairs)


def together(*values):
    return lax.optimization_barrier(values)


def gather_wide(own, beside=lambda: (), after=lambda early: ()):
    nz = lax.axis_size(WIDE) // 4
    zs = [to_wide(own, 4 * k) for k in range(1, nz)]
    xo = to_wide(own, 2)
    xo, early = together(xo, beside())
    xz = [to_wide(z, 2) for z in zs]
    near = [own, xo] + [p for pair in zip(zs, xz) for p in pair]
    late = after(early)
    return near + [to_wide(p, 1) for p in near], early, late


def pairwise(parts):
    while len(parts) > 1:
        parts = [parts[i] + parts[i + 1] for i in range(0, len(parts), 2)]
    return parts[0]


def tile_sum(adj_ref, piece_refs, rows=None):
    total = None
    for k, ref in enumerate(piece_refs):
        n = rows or ref.shape[0]
        term = dot(adj_ref[:, k * n : (k + 1) * n], ref[:n])
        total = term if total is None else total + term
    return total


def local(
    low_feats,
    hub_feats,
    w_first,
    w_second,
    low_tiles,
    tile_cols,
    edge_rows,
    edge_hubs,
    low_labels,
    hub_labels,
):
    rows, feat = low_feats.shape
    hr = hub_feats.shape[0]
    n_tiles, tile, _ = low_tiles.shape
    blocks = rows // tile
    per_block = n_tiles // blocks
    units = w_first.shape[1]
    classes = w_second.shape[1]
    n_wide, n_hub = lax.axis_size(WIDE), lax.axis_size(HUB)
    nz = n_wide // 4
    group = hr * n_hub
    total = (rows + hr) * n_wide * n_hub
    edges = edge_rows.shape[0]
    pay = feat + LANES

    at = [0]
    for n in (edges, edges, rows):
        at.append(at[-1] + n)
    ints = jnp.concatenate([edge_rows, edge_hubs, low_labels, hub_labels]).reshape(1, at[-1] + hr)

    def edge_tables(ints, feats, hub_rows, link, link_t, low_count, low_hot, hub_hot_out, *parts):
        e_rows, e_hubs, labels = (ints[:, at[i] : at[i + 1]] for i in range(3))
        labels_hub = ints[:, at[3] :]
        h = lax.axis_index(HUB)
        hubs = ((e_hubs // hr) ^ h) * hr + e_hubs % hr
        row_hot = (lax.broadcasted_iota(jnp.int32, (rows, edges), 0) == e_rows).astype(BF16)
        hub_hot = (lax.broadcasted_iota(jnp.int32, (group, edges), 0) == hubs).astype(BF16)
        links = dot_nt(hub_hot, row_hot)
        links_t = dot_nt(row_hot, hub_hot)
        hi, hi_t = links.astype(BF16), links_t.astype(BF16)
        lo, lo_t = (links - hi.astype(F32)).astype(BF16), (links_t - hi_t.astype(F32)).astype(BF16)
        link[:, :rows] = hi
        link[:, rows:] = lo
        link_t[...] = jnp.concatenate([hi_t, lo_t], axis=1)
        low_count[...] = jnp.broadcast_to(jnp.sum(links_t, axis=1, keepdims=True), (rows, LANES))
        sums = dot(hi, feats[...]) + dot(lo, feats[...])
        counts = jnp.broadcast_to(jnp.sum(links, axis=1, keepdims=True), (group, LANES))
        for k, part in enumerate(parts):
            part[:hr, :feat] = sums[k * hr : (k + 1) * hr]
            part[:hr, feat:] = counts[k * hr : (k + 1) * hr]
            part[hr:, :feat] = hub_rows[...].astype(F32)
            part[hr:, feat:] = jnp.zeros((hr, LANES), F32)
        hot = (lax.broadcasted_iota(jnp.int32, (classes, rows), 0) == labels).astype(F32)
        low_hot[...] = hot.T.astype(BF16)
        hot = (lax.broadcasted_iota(jnp.int32, (classes, hr), 0) == labels_hub).astype(F32)
        hub_hot_out[...] = hot.T.astype(BF16)

    link, link_t, low_count, low_target, hub_target, *parts1 = call(
        edge_tables,
        "edge_tables",
        [
            shaped(group, 2 * rows, BF16),
            shaped(rows, 2 * group, BF16),
            shaped(rows, LANES, F32),
            shaped(rows, classes, BF16),
            shaped(hr, classes, BF16),
        ]
        + [shaped(2 * hr, pay, F32) for _ in range(n_hub)],
        [ints, low_feats, hub_feats],
        traffic=4 << 20,
    )

    def adjacency(tiles, cols, low_count, adj, adj_t, scale):
        w = lax.axis_index(WIDE)
        adj[...] = jnp.zeros_like(adj)
        adj_t[...] = jnp.zeros_like(adj_t)
        for r in range(blocks):
            for k in range(per_block):
                b = cols[r, k]
                rel = (b // blocks) ^ w
                place = (rel & 1) * (n_wide // 2) + (rel >> 2) * 2 + ((rel >> 1) & 1)
                at = pl.ds(pl.multiple_of((place * blocks + b % blocks) * tile, tile), tile)
                value = tiles[r * per_block + k]
                adj[r * tile : (r + 1) * tile, at] = value
                adj_t[at, r * tile : (r + 1) * tile] = value.T
        deg = dot(adj[...], jnp.ones((n_wide * rows, LANES), BF16))
        scale[...] = lax.rsqrt(1.0 + deg + low_count[...])

    adj, adj_t, scale = call(
        adjacency,
        "adjacency",
        [shaped(rows, n_wide * rows, BF16), shaped(n_wide * rows, rows, BF16), shaped(rows, LANES, F32)],
        [low_tiles, tile_cols, low_count],
        smem=(1,),
        traffic=14 << 20,
    )

    def to_hub(x, k):
        return lax.ppermute(x, HUB, [(i, i ^ k) for i in range(n_hub)])

    mates = range(1, n_hub)

    def hub_first(feats, w, own, *refs):
        got, (hub_scale, agg, act) = refs[:-3], refs[-3:]
        sums = own[:hr]
        for g in got:
            sums = sums + g[:hr]
        s = lax.rsqrt(1.0 + sums[:, feat : feat + 1])
        hub_scale[...] = jnp.broadcast_to(s, (hr, LANES))
        a = ((feats[...].astype(F32) + sums[:, :feat]) * s).astype(BF16)
        agg[...] = a
        act[...] = jnp.maximum(dot(a, w[...]), 0.0).astype(BF16)

    def hubs_to_first(early):
        parts1 = early[0]
        got1 = [to_hub(parts1[k], k) for k in mates]
        outs = [shaped(hr, LANES, F32), shaped(hr, feat, BF16), shaped(hr, units, BF16)]
        return call(hub_first, "hub_first", outs, [hub_feats, w_first, parts1[0]] + got1), got1

    pieces1, (parts1, scale), ((hub_scale, agg1_hub, h1_hub), got1) = gather_wide(
        low_feats, lambda: (parts1, scale), hubs_to_first
    )
    n_pieces = len(pieces1)

    def low_first(adj, link, link_t, scale, field, w, act_hub, agg_hub, *refs):
        pieces, refs = refs[:n_pieces], refs[n_pieces:]
        hubs, (packed, own, *sends) = refs[:n_hub], refs[n_hub:]
        around = jnp.concatenate([r[hr:, :feat] for r in hubs] * 2, axis=0).astype(BF16)
        s = tile_sum(adj, pieces) + field[...].astype(F32) + dot(link_t[...], around)
        a = (s * scale[:, :1]).astype(BF16)
        act = jnp.maximum(dot(a, w[...]), 0.0).astype(BF16)
        packed[:rows] = act
        packed[rows:] = a.T
        sums = dot(link[:, :rows], act) + dot(link[:, rows:], act)
        own[...] = sums[:hr]
        for k, send in enumerate(sends, 1):
            send[:hr] = act_hub[...].astype(F32)
            send[hr : 2 * hr] = sums[k * hr : (k + 1) * hr]
            send[2 * hr :] = agg_hub[...].astype(F32)

    packed, own2, *sends2 = call(
        low_first,
        "low_first",
        [shaped(2 * rows, units, BF16), shaped(hr, units, F32)] + [shaped(3 * hr, units, F32) for _ in mates],
        [adj, link, link_t, scale, low_feats, w_first, h1_hub, agg1_hub] + pieces1 + [parts1[0]] + got1,
    )

    def hub_second(act, hub_scale, w, target, own, *refs):
        got, (logits, agg, dz, q) = refs[:-4], refs[-4:]
        sums = own[...]
        for g in got:
            sums = sums + g[hr : 2 * hr]
        s = hub_scale[:, :1]
        a = ((act[...].astype(F32) + sums) * s).astype(BF16)
        agg[...] = a
        y = dot(a, w[...])
        logits[...] = y
        d = ((y - target[...].astype(F32)) / total).astype(BF16)
        dz[...] = d
        q[...] = (dot_nt(d, w[...]) * s).astype(BF16)

    def hubs_to_second(got2):
        outs = [shaped(hr, classes, F32), shaped(hr, units, BF16), shaped(hr, classes, BF16), shaped(hr, units, BF16)]
        made = call(hub_second, "hub_second", outs, [h1_hub, hub_scale, w_second, hub_target, own2] + got2)
        return made, [to_hub(made[3], k) for k in mates]

    pieces2, got2, ((hub_logits, agg2_hub, dz2_hub, q_hub), q_hub_mates) = gather_wide(
        packed, lambda: [to_hub(x, k) for k, x in enumerate(sends2, 1)], hubs_to_second
    )

    def low_second(adj, link_t, scale, packed, w, target, act_hub, agg_hub, dz_hub, *refs):
        pieces, refs = refs[:n_pieces], refs[n_pieces:]
        got, (logits, grad, q_out) = refs[: n_hub - 1], refs[n_hub - 1 :]
        around = jnp.concatenate([act_hub[...]] + [g[:hr].astype(BF16) for g in got], axis=0)
        around = jnp.concatenate([around, around], axis=0)
        s = tile_sum(adj, pieces, rows) + packed[:rows].astype(F32) + dot(link_t[...], around)
        a = (s * scale[:, :1]).astype(BF16)
        y = dot(a, w[...])
        logits[...] = y
        d = ((y - target[...].astype(F32)) / total).astype(BF16)
        q_out[...] = (dot_nt(d, w[...]) * scale[:, :1]).astype(BF16)
        grad[...] = dot_tn(a, d) + dot_tn(agg_hub[...], dz_hub[...])

    low_logits, grad_second, q_low = call(
        low_second,
        "low_second",
        [shaped(rows, classes, F32), shaped(units, classes, F32), shaped(rows, units, BF16)],
        [adj, link_t, scale, packed, w_second, low_target, h1_hub, agg2_hub, dz2_hub] + pieces2 + got2,
    )

    def back_first(adj_t, link, link_t, q, grad_second, act_hub, agg_hub, q_hub, *refs):
        pieces, refs = refs[:n_pieces], refs[n_pieces:]
        got, refs = refs[: n_hub - 1], refs[n_hub - 1 :]
        q_mates, (keep, give) = refs[: n_hub - 1], refs[n_hub - 1 :]
        q_own = q[...]
        around = jnp.concatenate([q_hub[...]] + [g[...] for g in q_mates], axis=0)
        around = jnp.concatenate([around, around], axis=0)
        grad = None
        for k, piece in enumerate(pieces):
            term = dot(adj_t[k * rows : (k + 1) * rows], q_own)
            if k == 0:
                term = term + q_own.astype(F32) + dot(link_t[...], around)
            term = jnp.where(piece[:rows].astype(F32) > 0.0, term, 0.0).astype(BF16)
            term = dot(piece[rows:], term)
            grad = term if grad is None else grad + term
        sums = dot(link[:, :rows], q_own) + dot(link[:, rows:], q_own)
        for k in range(n_hub):
            term = sums[k * hr : (k + 1) * hr]
            act = act_hub[...].astype(F32) if k == 0 else got[k - 1][:hr]
            agg = agg_hub[...] if k == 0 else got[k - 1][2 * hr :].astype(BF16)
            if k == 0:
                term = term + q_hub[...].astype(F32)
            grad = grad + dot_tn(agg, jnp.where(act > 0.0, term, 0.0).astype(BF16))
        core = lax.axis_index(WIDE) & 1

        @pl.when(core == 0)
        def _():
            keep[...] = grad
            give[...] = grad_second[...]

        @pl.when(core == 1)
        def _():
            keep[...] = grad_second[...]
            give[...] = grad

    keep, give = call(
        back_first,
        "back_first",
        [shaped(units, classes, F32), shaped(units, classes, F32)],
        [adj_t, link, link_t, q_low, grad_second, h1_hub, agg1_hub, q_hub] + pieces2 + got2 + q_hub_mates,
    )
    got = to_wide(give, 1)

    n_share = 2 * n_hub
    share = units // n_share
    steps = [(2 * (k // n_hub), k % n_hub) for k in range(n_share)]

    def place_of():
        return ((lax.axis_index(WIDE) >> 1) & 1) * n_hub + lax.axis_index(HUB)

    def split(keep, got, *outs):
        me = place_of()
        for k, out in enumerate(outs):
            at = pl.ds(pl.multiple_of((me ^ k) * share, share), share)
            out[...] = keep[at] + got[at]

    shares = call(split, "split", [shaped(share, classes, F32) for _ in range(n_share)], [keep, got])
    shares = [shares[0]] + [to_both(shares[k], *steps[k]) for k in range(1, n_share)]

    def add_up(*refs):
        refs[-1][...] = pairwise([r[...] for r in refs[:-1]])

    (mine,) = call(add_up, "add_xy", [shaped(share, classes, F32)], shares)
    (mine,) = call(
        add_up, "add_z", [shaped(share, classes, F32)], [mine] + [to_wide(mine, 4 * k) for k in range(1, nz)]
    )
    mine = [mine] + [to_both(mine, *steps[k]) for k in range(1, n_share)]
    other = [to_wide(m, 1) for m in mine]

    def assemble(*refs):
        mine, other, (grad_first, grad_second) = refs[:n_share], refs[n_share : 2 * n_share], refs[2 * n_share :]
        me = place_of()
        core = lax.axis_index(WIDE) & 1

        def write(mine_out, other_out):
            for k in range(n_share):
                at = pl.ds(pl.multiple_of((me ^ k) * share, share), share)
                mine_out[at] = mine[k][...]
                other_out[at] = other[k][...]

        @pl.when(core == 0)
        def _():
            write(grad_first, grad_second)

        @pl.when(core == 1)
        def _():
            write(grad_second, grad_first)

    grad_first, grad_second = call(
        assemble, "assemble", [shaped(units, classes, F32), shaped(units, classes, F32)], mine + other
    )
    return (low_logits, hub_logits, grad_first, grad_second)


def solution(mesh):
    in_specs = (
        P((WIDE, HUB), None),
        P((WIDE, HUB), None),
        P(),
        P(),
        P((WIDE, HUB), None, None),
        P((WIDE, HUB), None),
        P((WIDE, HUB)),
        P((WIDE, HUB)),
        P((WIDE, HUB)),
        P((WIDE, HUB)),
    )
    out_specs = (P((WIDE, HUB), None), P((WIDE, HUB), None), P(), P())
    return jax.shard_map(local, mesh=mesh, in_specs=in_specs, out_specs=out_specs, check_vma=False)
```

time: 140 us -> 103 us (0.74)
  starting transfers between devices: 54.4 us -> 34.9 us
  local copies, waits for them, and re-layouts: 22.1 us -> 6.91 us
  Pallas kernels: 13.4 us -> 9.09 us
    ppermute x46 -> x38, starting transfers between devices: 43.3 us -> 24.2 us  [to_wide(): lax.ppermute(x, WIDE, [(i, i ^ k) for i in range(lax.axis_size(WIDE))])]
    unnamed x74 -> x18, local copies, waits for them, and re-layouts: 18.3 us -> 6.9 us
    pallas_call x13 -> x11, Pallas kernels: 13.4 us -> 9.09 us  [call(): pl.pallas_call(body, name=name, out_shape=outs, in_specs=[pl.BlockSpec(me...]
    ppermute x46 -> x38, waiting for transfers between devices: 37.9 us -> 42.1 us  [to_wide(): lax.ppermute(x, WIDE, [(i, i ^ k) for i in range(lax.axis_size(WIDE))])]
    ppermute x4 -> x3, waiting for transfers between devices: 4.1 us -> 0.25 us  [to_hub(): return lax.ppermute(x, HUB, [(i, i ^ k) for i in range(n_hub)])]
    reshape x2 -> x1, local copies, waits for them, and re-layouts: 2.2 us -> 0.01 us  [local(): jnp.concatenate([edge_rows, edge_hubs, low_labels, hub_labels])]
    ppermute x4 -> x3, starting transfers between devices: 4.02 us -> 3.62 us  [to_hub(): return lax.ppermute(x, HUB, [(i, i ^ k) for i in range(n_hub)])]
  transfers between devices with their start and end apart: 56 -> 47, of which waited for: 27 -> 20; matrix products, arithmetic and copies ran while one was open for 3% -> 1% of each run, Pallas kernels for 7% -> 5%
where the time goes in v2:
time: 103 us
  waiting for transfers between devices  50.1 us (49%)
  starting transfers between devices  34.9 us (34%)
  Pallas kernels  9.09 us (9%)
  local copies, waits for them, and re-layouts  6.91 us (7%)
    ppermute x38, waiting for transfers between devices, to_wide(): lax.ppermute(x, WIDE, [(i, i ^ k) for i in range(lax.axis_size(WIDE))])  42.1 us
    ppermute x38, starting transfers between devices, to_wide(): lax.ppermute(x, WIDE, [(i, i ^ k) for i in range(lax.axis_size(WIDE))])  24.2 us
    pallas_call x11, Pallas kernels, call(): pl.pallas_call(body, name=name, out_shape=outs, in_specs=[pl.BlockSpec(me...  9.09 us
    ppermute x6, waiting for transfers between devices, to_both(): return lax.ppermute(x, (WIDE, HUB), pairs)  7.77 us
    ppermute x6, starting transfers between devices, to_both(): return lax.ppermute(x, (WIDE, HUB), pairs)  7.11 us
    unnamed x18, local copies, waits for them, and re-layouts  6.9 us
    ppermute x3, starting transfers between devices, to_hub(): return lax.ppermute(x, HUB, [(i, i ^ k) for i in range(n_hub)])  3.62 us
  transfers between devices with their start and end apart: 47, of which 20 were waited for; matrix products, arithmetic and copies ran while one was open for 1% of the time, Pallas kernels for 5%

profile of v2, /device:TPU:0, one launch (start us, length us, event | category | flops | bytes accessed | tf_op | source)
XLA Modules:
  0.0 102.5 jit_solution(7834029716468462432)
XLA Ops:
  0.6 3.0 %collective-permute-start = (bf16[256,256]{1,0:T(8,128)(2,1)}, bf16[256,256]{1,0:T(8,128)(2,1)S(1)}, u32[]{:S(2)}, u32[]{:S(2)}) collective-permute-start(bf16[256,256]{1,0:T(8,128)(2,1)} %refs_0_.1), channel_id=1, source_target_pairs={{0,4},{2,6},{4,0},{6,2},{8,12},{10,14},{12,8},{14,10},{16,20},{18,... | collective-permute-start | bytes 393224 | tf_op jit(solution)/shard_map/ppermute | solution.py:46
  3.6 1.6 %collective-permute-start.2 = (bf16[256,256]{1,0:T(8,128)(2,1)}, bf16[256,256]{1,0:T(8,128)(2,1)S(1)}, u32[]{:S(2)}, u32[]{:S(2)}) collective-permute-start(bf16[256,256]{1,0:T(8,128)(2,1)} %refs_0_.1), channel_id=1, source_target_pairs={{0,8},{2,10},{4,12},{6,14},{8,0},{10,2},{12,4},{14,6},{16,24},{18,... | collective-permute-start | bytes 393224 | tf_op jit(solution)/shard_map/ppermute | solution.py:46
  5.2 2.6 %collective-permute-start.4 = (bf16[256,256]{1,0:T(8,128)(2,1)}, bf16[256,256]{1,0:T(8,128)(2,1)S(1)}, u32[]{:S(2)}, u32[]{:S(2)}) collective-permute-start(bf16[256,256]{1,0:T(8,128)(2,1)} %refs_0_.1), channel_id=1, source_target_pairs={{0,16},{2,18},{4,20},{6,22},{8,24},{10,26},{12,28},{14,30},{16,0},... | collective-permute-start | bytes 393224 | tf_op jit(solution)/shard_map/ppermute | solution.py:46
  10.9 1.2 %copy-done.2 = bf16[32,128,128]{2,1,0:T(8,128)(2,1)S(1)} copy-done((bf16[32,128,128]{2,1,0:T(8,128)(2,1)S(1)}, bf16[32,128,128]{2,1,0:T(8,128)(2,1)}, u32[]{:S(2)}) %copy-start.2) | copy-done | bytes 1048600
  12.8 1.9 %adjacency.1 = (bf16[256,4096]{1,0:T(8,128)(2,1)S(1)}, bf16[4096,256]{1,0:T(8,128)(2,1)S(1)}, f32[256,128]{1,0:T(8,128)S(1)}) custom-call(bf16[32,128,128]{2,1,0:T(8,128)(2,1)S(1)} %copy-done.2, s32[2,16]{1,0:T(2,128)S(1)} %copy-done.8, f32[256,128]{1,0:T(8,128)S(1)} %get-tuple-element.41.low_count), custom_call_target="tpu_custom_call" | custom-call | bytes 14680064 | tf_op jit(solution)/shard_map/adjacency/pallas_call | solution.py:22
  14.8 1.6 %collective-permute-start.1 = (f32[32,384]{1,0:T(8,128)S(1)}, f32[32,384]{1,0:T(8,128)S(1)}, u32[]{:S(2)}, u32[]{:S(2)}) collective-permute-start(f32[32,384]{1,0:T(8,128)S(1)} %get-tuple-element.50), channel_id=1, source_target_pairs={{0,1},{1,0},{2,3},{3,2},{4,5},{5,4},{6,7},{7,6},{8,9},{9,8},{10,11... | collective-permute-start | bytes 147464 | tf_op jit(solution)/shard_map/ppermute | solution.py:184
  16.6 1.5 %collective-permute-done.4.refs_4_ = bf16[256,256]{1,0:T(8,128)(2,1)S(1)} collective-permute-done((bf16[256,256]{1,0:T(8,128)(2,1)}, bf16[256,256]{1,0:T(8,128)(2,1)S(1)}, u32[]{:S(2)}, u32[]{:S(2)}) %collective-permute-start.4) | collective-permute-done | bytes 131104 | tf_op jit(solution)/shard_map/ppermute | solution.py:46
  18.6 1.5 %collective-permute-start.5 = (bf16[256,256]{1,0:T(8,128)(2,1)S(1)}, bf16[256,256]{1,0:T(8,128)(2,1)S(1)}, u32[]{:S(2)}, u32[]{:S(2)}) collective-permute-start(bf16[256,256]{1,0:T(8,128)(2,1)S(1)} %collective-permute-done.4.refs_4_), channel_id=1, source_target_pairs={{0,4},{2,6},{4,0},{6,2},{8,12},{10,14},{12,8},{14,10},{16,20},{18,... | collective-permute-start | bytes 393224 | tf_op jit(solution)/shard_map/ppermute | solution.py:46
  21.2 3.4 %collective-permute-done.3.refs_3_ = bf16[256,256]{1,0:T(8,128)(2,1)S(1)} collective-permute-done((bf16[256,256]{1,0:T(8,128)(2,1)S(1)}, bf16[256,256]{1,0:T(8,128)(2,1)S(1)}, u32[]{:S(2)}, u32[]{:S(2)}) %collective-permute-start.3) | collective-permute-done | bytes 131104 | tf_op jit(solution)/shard_map/ppermute | solution.py:46
  24.5 2.0 %collective-permute-done.5.refs_5_ = bf16[256,256]{1,0:T(8,128)(2,1)S(1)} collective-permute-done((bf16[256,256]{1,0:T(8,128)(2,1)S(1)}, bf16[256,256]{1,0:T(8,128)(2,1)S(1)}, u32[]{:S(2)}, u32[]{:S(2)}) %collective-permute-start.5) | collective-permute-done | bytes 131104 | tf_op jit(solution)/shard_map/ppermute | solution.py:46
  26.5 1.4 %collective-permute-done.7.refs_7_ = bf16[256,256]{1,0:T(8,128)(2,1)S(1)} collective-permute-done((bf16[256,256]{1,0:T(8,128)(2,1)S(1)}, bf16[256,256]{1,0:T(8,128)(2,1)S(1)}, u32[]{:S(2)}, u32[]{:S(2)}) %collective-permute-start.7) | collective-permute-done | bytes 131104 | tf_op jit(solution)/shard_map/ppermute | solution.py:46
  35.4 3.0 %collective-permute-start.20 = (bf16[512,256]{1,0:T(8,128)(2,1)S(1)}, bf16[512,256]{1,0:T(8,128)(2,1)S(1)}, u32[]{:S(2)}, u32[]{:S(2)}) collective-permute-start(bf16[512,256]{1,0:T(8,128)(2,1)S(1)} %get-tuple-element.54.packed.refs_0_), channel_id=1, source_target_pairs={{0,16},{2,18},{4,20},{6,22},{8,24},{10,26},{12,28},{14,30},{16,0},... | collective-permute-start | bytes 786440 | tf_op jit(solution)/shard_map/ppermute | solution.py:46
  38.4 7.8 %collective-permute-done.18.refs_2_ = bf16[512,256]{1,0:T(8,128)(2,1)S(1)} collective-permute-done((bf16[512,256]{1,0:T(8,128)(2,1)S(1)}, bf16[512,256]{1,0:T(8,128)(2,1)S(1)}, u32[]{:S(2)}, u32[]{:S(2)}) %collective-permute-start.18) | collective-permute-done | bytes 262176 | tf_op jit(solution)/shard_map/ppermute | solution.py:46
  46.2 10.6 %collective-permute-done.20.refs_4_ = bf16[512,256]{1,0:T(8,128)(2,1)S(1)} collective-permute-done((bf16[512,256]{1,0:T(8,128)(2,1)S(1)}, bf16[512,256]{1,0:T(8,128)(2,1)S(1)}, u32[]{:S(2)}, u32[]{:S(2)}) %collective-permute-start.20) | collective-permute-done | bytes 262176 | tf_op jit(solution)/shard_map/ppermute | solution.py:46
  56.9 1.5 %collective-permute-start.21 = (bf16[512,256]{1,0:T(8,128)(2,1)S(1)}, bf16[512,256]{1,0:T(8,128)(2,1)S(1)}, u32[]{:S(2)}, u32[]{:S(2)}) collective-permute-start(bf16[512,256]{1,0:T(8,128)(2,1)S(1)} %collective-permute-done.20.refs_4_), channel_id=1, source_target_pairs={{0,4},{2,6},{4,0},{6,2},{8,12},{10,14},{12,8},{14,10},{16,20},{18,... | collective-permute-start | bytes 786440 | tf_op jit(solution)/shard_map/ppermute | solution.py:46
  59.5 3.8 %collective-permute-done.21.refs_5_ = bf16[512,256]{1,0:T(8,128)(2,1)S(1)} collective-permute-done((bf16[512,256]{1,0:T(8,128)(2,1)S(1)}, bf16[512,256]{1,0:T(8,128)(2,1)S(1)}, u32[]{:S(2)}, u32[]{:S(2)}) %collective-permute-start.21) | collective-permute-done | bytes 262176 | tf_op jit(solution)/shard_map/ppermute | solution.py:46
  63.2 2.8 %collective-permute-done.23.refs_7_ = bf16[512,256]{1,0:T(8,128)(2,1)S(1)} collective-permute-done((bf16[512,256]{1,0:T(8,128)(2,1)S(1)}, bf16[512,256]{1,0:T(8,128)(2,1)S(1)}, u32[]{:S(2)}, u32[]{:S(2)}) %collective-permute-start.23) | collective-permute-done | bytes 262176 | tf_op jit(solution)/shard_map/ppermute | solution.py:46
  67.4 1.5 %collective-permute-start.32 = (bf16[16,256]{1,0:T(8,128)(2,1)S(1)}, bf16[16,256]{1,0:T(8,128)(2,1)S(1)}, u32[]{:S(2)}, u32[]{:S(2)}) collective-permute-start(bf16[16,256]{1,0:T(8,128)(2,1)S(1)} %get-tuple-element.69.q_hub), channel_id=1, source_target_pairs={{0,1},{1,0},{2,3},{3,2},{4,5},{5,4},{6,7},{7,6},{8,9},{9,8},{10,11... | collective-permute-start | bytes 24584 | tf_op jit(solution)/shard_map/ppermute | solution.py:184
  69.0 1.9 %low_second.1 = (f32[256,256]{1,0:T(8,128)}, f32[256,256]{1,0:T(8,128)S(1)}, bf16[256,256]{1,0:T(8,128)(2,1)S(1)}) custom-call(bf16[256,4096]{1,0:T(8,128)(2,1)S(1)} %get-tuple-element.42.adj, bf16[256,64]{1,0:T(8,128)(2,1)S(1)} %get-tuple-element.43.link_t, f32[256,128]{1,0:T(8,128)S(1)} %get-tuple-element.47.scale, ...), custom_call_target="tpu_custom_call" | custom-call | bytes 1048576 | tf_op jit(solution)/shard_map/low_second/pallas_call | solution.py:22
  71.1 1.8 %back_first.1 = (f32[256,256]{1,0:T(8,128)S(1)}, f32[256,256]{1,0:T(8,128)S(1)}) custom-call(bf16[4096,256]{1,0:T(8,128)(2,1)S(1)} %get-tuple-element.66.adj_t, bf16[32,512]{1,0:T(8,128)(2,1)S(1)} %get-tuple-element.48.link, bf16[256,64]{1,0:T(8,128)(2,1)S(1)} %get-tuple-element.43.link_t, bf16[256,256]{1,0:T(8,128)(2,1)S(1)} %get-tuple-element.67.q, ...), custom_call_target="tpu_custom_call" | custom-call | bytes 1048576 | tf_op jit(solution)/shard_map/back_first/pallas_call | solution.py:22
  73.0 1.5 %collective-permute-done.33.got = f32[256,256]{1,0:T(8,128)S(1)} collective-permute-done((f32[256,256]{1,0:T(8,128)S(1)}, f32[256,256]{1,0:T(8,128)S(1)}, u32[]{:S(2)}, u32[]{:S(2)}) %collective-permute-start.33) | collective-permute-done | bytes 262176 | tf_op jit(solution)/shard_map/ppermute | solution.py:46
  74.5 1.6 %collective-permute-start.34 = (f32[64,256]{1,0:T(8,128)S(1)}, f32[64,256]{1,0:T(8,128)S(1)}, u32[]{:S(2)}, u32[]{:S(2)}) collective-permute-start(f32[64,256]{1,0:T(8,128)S(1)} %get-tuple-element.73), channel_id=1, source_target_pairs={{0,1},{1,0},{2,3},{3,2},{4,5},{5,4},{6,7},{7,6},{8,9},{9,8},{10,11... | collective-permute-start | bytes 196616 | tf_op jit(solution)/shard_map/ppermute | solution.py:52
  76.1 1.5 %collective-permute-start.35 = (f32[64,256]{1,0:T(8,128)S(1)}, f32[64,256]{1,0:T(8,128)S(1)}, u32[]{:S(2)}, u32[]{:S(2)}) collective-permute-start(f32[64,256]{1,0:T(8,128)S(1)} %get-tuple-element.74), channel_id=1, source_target_pairs={{0,4},{1,5},{2,6},{3,7},{4,0},{5,1},{6,2},{7,3},{8,12},{9,13},{10,... | collective-permute-start | bytes 196616 | tf_op jit(solution)/shard_map/ppermute | solution.py:52
  78.8 2.2 %collective-permute-done.35.refs_2_ = f32[64,256]{1,0:T(8,128)S(1)} collective-permute-done((f32[64,256]{1,0:T(8,128)S(1)}, f32[64,256]{1,0:T(8,128)S(1)}, u32[]{:S(2)}, u32[]{:S(2)}) %collective-permute-start.35) | collective-permute-done | bytes 65568 | tf_op jit(solution)/shard_map/ppermute | solution.py:52
  81.0 1.7 %collective-permute-done.36.refs_3_ = f32[64,256]{1,0:T(8,128)S(1)} collective-permute-done((f32[64,256]{1,0:T(8,128)S(1)}, f32[64,256]{1,0:T(8,128)S(1)}, u32[]{:S(2)}, u32[]{:S(2)}) %collective-permute-start.36) | collective-permute-done | bytes 65568 | tf_op jit(solution)/shard_map/ppermute | solution.py:52
  82.8 2.3 %collective-permute-start.37 = (f32[64,256]{1,0:T(8,128)S(1)}, f32[64,256]{1,0:T(8,128)S(1)}, u32[]{:S(2)}, u32[]{:S(2)}) collective-permute-start(f32[64,256]{1,0:T(8,128)S(1)} %add_xy.1.refs_0_), channel_id=1, source_target_pairs={{0,8},{2,10},{4,12},{6,14},{8,0},{10,2},{12,4},{14,6},{16,24},{18,... | collective-permute-start | bytes 196616 | tf_op jit(solution)/shard_map/ppermute | solution.py:46
  85.1 2.5 %collective-permute-start.38 = (f32[64,256]{1,0:T(8,128)S(1)}, f32[64,256]{1,0:T(8,128)S(1)}, u32[]{:S(2)}, u32[]{:S(2)}) collective-permute-start(f32[64,256]{1,0:T(8,128)S(1)} %add_xy.1.refs_0_), channel_id=1, source_target_pairs={{0,16},{2,18},{4,20},{6,22},{8,24},{10,26},{12,28},{14,30},{16,0},... | collective-permute-start | bytes 196616 | tf_op jit(solution)/shard_map/ppermute | solution.py:46
  88.0 3.7 %collective-permute-done.38.refs_2_ = f32[64,256]{1,0:T(8,128)S(1)} collective-permute-done((f32[64,256]{1,0:T(8,128)S(1)}, f32[64,256]{1,0:T(8,128)S(1)}, u32[]{:S(2)}, u32[]{:S(2)}) %collective-permute-start.38) | collective-permute-done | bytes 65568 | tf_op jit(solution)/shard_map/ppermute | solution.py:46
  91.6 2.0 %collective-permute-done.39.refs_3_ = f32[64,256]{1,0:T(8,128)S(1)} collective-permute-done((f32[64,256]{1,0:T(8,128)S(1)}, f32[64,256]{1,0:T(8,128)S(1)}, u32[]{:S(2)}, u32[]{:S(2)}) %collective-permute-start.39) | collective-permute-done | bytes 65568 | tf_op jit(solution)/shard_map/ppermute | solution.py:46
  95.3 1.9 %collective-permute-start.42 = (f32[64,256]{1,0:T(8,128)S(1)}, f32[64,256]{1,0:T(8,128)S(1)}, u32[]{:S(2)}, u32[]{:S(2)}) collective-permute-start(f32[64,256]{1,0:T(8,128)S(1)} %add_z.1.refs_0_), channel_id=1, source_target_pairs={{0,5},{1,4},{2,7},{3,6},{4,1},{5,0},{6,3},{7,2},{8,13},{9,12},{10,... | collective-permute-start | bytes 196616 | tf_op jit(solution)/shard_map/ppermute | solution.py:52
  98.5 1.9 %collective-permute-done.42.refs_3_ = f32[64,256]{1,0:T(8,128)S(1)} collective-permute-done((f32[64,256]{1,0:T(8,128)S(1)}, f32[64,256]{1,0:T(8,128)S(1)}, u32[]{:S(2)}, u32[]{:S(2)}) %collective-permute-start.42) | collective-permute-done | bytes 65568 | tf_op jit(solution)/shard_map/ppermute | solution.py:52
  100.5 1.2 %collective-permute-done.46.refs_7_ = f32[64,256]{1,0:T(8,128)S(1)} collective-permute-done((f32[64,256]{1,0:T(8,128)S(1)}, f32[64,256]{1,0:T(8,128)S(1)}, u32[]{:S(2)}, u32[]{:S(2)}) %collective-permute-start.46) | collective-permute-done | bytes 65568 | tf_op jit(solution)/shard_map/ppermute | solution.py:46
  (93 shorter events, 21.4 us)
Async XLA Ops:
  0.6 14.1 %collective-permute-start = (bf16[256,256]{1,0:T(8,128)(2,1)}, bf16[256,256]{1,0:T(8,128)(2,1)S(1)}, u32[]{:S(2)}, u32[]{:S(2)}) collective-permute-start(bf16[256,256]{1,0:T(8,128)(2,1)} %refs_0_.1), channel_id=1, source_target_pairs={{0,4},{2,6},{4,0},{6,2},{8,12},{10,14},{12,8},{14,10},{16,20},{18,... | collective-permute-start | bytes 393224 | tf_op jit(solution)/shard_map/ppermute | solution.py:46
  3.6 12.7 %collective-permute-start.2 = (bf16[256,256]{1,0:T(8,128)(2,1)}, bf16[256,256]{1,0:T(8,128)(2,1)S(1)}, u32[]{:S(2)}, u32[]{:S(2)}) collective-permute-start(bf16[256,256]{1,0:T(8,128)(2,1)} %refs_0_.1), channel_id=1, source_target_pairs={{0,8},{2,10},{4,12},{6,14},{8,0},{10,2},{12,4},{14,6},{16,24},{18,... | collective-permute-start | bytes 393224 | tf_op jit(solution)/shard_map/ppermute | solution.py:46
  5.2 12.9 %collective-permute-start.4 = (bf16[256,256]{1,0:T(8,128)(2,1)}, bf16[256,256]{1,0:T(8,128)(2,1)S(1)}, u32[]{:S(2)}, u32[]{:S(2)}) collective-permute-start(bf16[256,256]{1,0:T(8,128)(2,1)} %refs_0_.1), channel_id=1, source_target_pairs={{0,16},{2,18},{4,20},{6,22},{8,24},{10,26},{12,28},{14,30},{16,0},... | collective-permute-start | bytes 393224 | tf_op jit(solution)/shard_map/ppermute | solution.py:46
  7.8 10.8 %collective-permute-start.6 = (bf16[256,256]{1,0:T(8,128)(2,1)}, bf16[256,256]{1,0:T(8,128)(2,1)S(1)}, u32[]{:S(2)}, u32[]{:S(2)}) collective-permute-start(bf16[256,256]{1,0:T(8,128)(2,1)} %refs_0_.1), channel_id=1, source_target_pairs={{0,24},{2,26},{4,28},{6,30},{8,16},{10,18},{12,20},{14,22},{16,8},... | collective-permute-start | bytes 393224 | tf_op jit(solution)/shard_map/ppermute | solution.py:46
  8.0 12.1 %collective-permute-start.8 = (bf16[256,256]{1,0:T(8,128)(2,1)}, bf16[256,256]{1,0:T(8,128)(2,1)S(1)}, u32[]{:S(2)}, u32[]{:S(2)}) collective-permute-start(bf16[256,256]{1,0:T(8,128)(2,1)} %refs_0_.1), channel_id=1, source_target_pairs={{0,2},{2,0},{4,6},{6,4},{8,10},{10,8},{12,14},{14,12},{16,18},{18,... | collective-permute-start | bytes 393224 | tf_op jit(solution)/shard_map/ppermute | solution.py:46
  14.8 5.9 %collective-permute-start.1 = (f32[32,384]{1,0:T(8,128)S(1)}, f32[32,384]{1,0:T(8,128)S(1)}, u32[]{:S(2)}, u32[]{:S(2)}) collective-permute-start(f32[32,384]{1,0:T(8,128)S(1)} %get-tuple-element.50), channel_id=1, source_target_pairs={{0,1},{1,0},{2,3},{3,2},{4,5},{5,4},{6,7},{7,6},{8,9},{9,8},{10,11... | collective-permute-start | bytes 147464 | tf_op jit(solution)/shard_map/ppermute | solution.py:184
  18.1 6.4 %collective-permute-start.3 = (bf16[256,256]{1,0:T(8,128)(2,1)S(1)}, bf16[256,256]{1,0:T(8,128)(2,1)S(1)}, u32[]{:S(2)}, u32[]{:S(2)}) collective-permute-start(bf16[256,256]{1,0:T(8,128)(2,1)S(1)} %collective-permute-done.2.refs_2_), channel_id=1, source_target_pairs={{0,4},{2,6},{4,0},{6,2},{8,12},{10,14},{12,8},{14,10},{16,20},{18,... | collective-permute-start | bytes 393224 | tf_op jit(solution)/shard_map/ppermute | solution.py:46
  18.6 7.9 %collective-permute-start.5 = (bf16[256,256]{1,0:T(8,128)(2,1)S(1)}, bf16[256,256]{1,0:T(8,128)(2,1)S(1)}, u32[]{:S(2)}, u32[]{:S(2)}) collective-permute-start(bf16[256,256]{1,0:T(8,128)(2,1)S(1)} %collective-permute-done.4.refs_4_), channel_id=1, source_target_pairs={{0,4},{2,6},{4,0},{6,2},{8,12},{10,14},{12,8},{14,10},{16,20},{18,... | collective-permute-start | bytes 393224 | tf_op jit(solution)/shard_map/ppermute | solution.py:46
  20.1 7.8 %collective-permute-start.7 = (bf16[256,256]{1,0:T(8,128)(2,1)S(1)}, bf16[256,256]{1,0:T(8,128)(2,1)S(1)}, u32[]{:S(2)}, u32[]{:S(2)}) collective-permute-start(bf16[256,256]{1,0:T(8,128)(2,1)S(1)} %collective-permute-done.6.refs_6_), channel_id=1, source_target_pairs={{0,4},{2,6},{4,0},{6,2},{8,12},{10,14},{12,8},{14,10},{16,20},{18,... | collective-permute-start | bytes 393224 | tf_op jit(solution)/shard_map/ppermute | solution.py:46
  20.7 7.3 %collective-permute-start.10 = (bf16[256,256]{1,0:T(8,128)(2,1)S(1)}, bf16[256,256]{1,0:T(8,128)(2,1)S(1)}, u32[]{:S(2)}, u32[]{:S(2)}) collective-permute-start(bf16[256,256]{1,0:T(8,128)(2,1)S(1)} %collective-permute-done.2.refs_2_), channel_id=1, source_target_pairs={{0,2},{2,0},{4,6},{6,4},{8,10},{10,8},{12,14},{14,12},{16,18},{18,... | collective-permute-start | bytes 393224 | tf_op jit(solution)/shard_map/ppermute | solution.py:46
  20.7 9.5 %collective-permute-start.12 = (bf16[256,256]{1,0:T(8,128)(2,1)S(1)}, bf16[256,256]{1,0:T(8,128)(2,1)S(1)}, u32[]{:S(2)}, u32[]{:S(2)}) collective-permute-start(bf16[256,256]{1,0:T(8,128)(2,1)S(1)} %collective-permute-done.4.refs_4_), channel_id=1, source_target_pairs={{0,2},{2,0},{4,6},{6,4},{8,10},{10,8},{12,14},{14,12},{16,18},{18,... | collective-permute-start | bytes 393224 | tf_op jit(solution)/shard_map/ppermute | solution.py:46
  24.5 5.7 %collective-permute-start.14 = (bf16[256,256]{1,0:T(8,128)(2,1)S(1)}, bf16[256,256]{1,0:T(8,128)(2,1)S(1)}, u32[]{:S(2)}, u32[]{:S(2)}) collective-permute-start(bf16[256,256]{1,0:T(8,128)(2,1)S(1)} %collective-permute-done.6.refs_6_), channel_id=1, source_target_pairs={{0,2},{2,0},{4,6},{6,4},{8,10},{10,8},{12,14},{14,12},{16,18},{18,... | collective-permute-start | bytes 393224 | tf_op jit(solution)/shard_map/ppermute | solution.py:46
  33.2 5.3 %collective-permute-start.17 = (f32[48,256]{1,0:T(8,128)S(1)}, f32[48,256]{1,0:T(8,128)S(1)}, u32[]{:S(2)}, u32[]{:S(2)}) collective-permute-start(f32[48,256]{1,0:T(8,128)S(1)} %get-tuple-element.59), channel_id=1, source_target_pairs={{0,1},{1,0},{2,3},{3,2},{4,5},{5,4},{6,7},{7,6},{8,9},{9,8},{10,11... | collective-permute-start | bytes 147464 | tf_op jit(solution)/shard_map/ppermute | solution.py:184
  33.7 12.5 %collective-permute-start.18 = (bf16[512,256]{1,0:T(8,128)(2,1)S(1)}, bf16[512,256]{1,0:T(8,128)(2,1)S(1)}, u32[]{:S(2)}, u32[]{:S(2)}) collective-permute-start(bf16[512,256]{1,0:T(8,128)(2,1)S(1)} %get-tuple-element.54.packed.refs_0_), channel_id=1, source_target_pairs={{0,8},{2,10},{4,12},{6,14},{8,0},{10,2},{12,4},{14,6},{16,24},{18,... | collective-permute-start | bytes 786440 | tf_op jit(solution)/shard_map/ppermute | solution.py:46
  34.9 11.4 %collective-permute-start.16 = (bf16[512,256]{1,0:T(8,128)(2,1)S(1)}, bf16[512,256]{1,0:T(8,128)(2,1)S(1)}, u32[]{:S(2)}, u32[]{:S(2)}) collective-permute-start(bf16[512,256]{1,0:T(8,128)(2,1)S(1)} %get-tuple-element.54.packed.refs_0_), channel_id=1, source_target_pairs={{0,4},{2,6},{4,0},{6,2},{8,12},{10,14},{12,8},{14,10},{16,20},{18,... | collective-permute-start | bytes 786440 | tf_op jit(solution)/shard_map/ppermute | solution.py:46
  35.4 21.5 %collective-permute-start.20 = (bf16[512,256]{1,0:T(8,128)(2,1)S(1)}, bf16[512,256]{1,0:T(8,128)(2,1)S(1)}, u32[]{:S(2)}, u32[]{:S(2)}) collective-permute-start(bf16[512,256]{1,0:T(8,128)(2,1)S(1)} %get-tuple-element.54.packed.refs_0_), channel_id=1, source_target_pairs={{0,16},{2,18},{4,20},{6,22},{8,24},{10,26},{12,28},{14,30},{16,0},... | collective-permute-start | bytes 786440 | tf_op jit(solution)/shard_map/ppermute | solution.py:46
  38.4 19.9 %collective-permute-start.22 = (bf16[512,256]{1,0:T(8,128)(2,1)S(1)}, bf16[512,256]{1,0:T(8,128)(2,1)S(1)}, u32[]{:S(2)}, u32[]{:S(2)}) collective-permute-start(bf16[512,256]{1,0:T(8,128)(2,1)S(1)} %get-tuple-element.54.packed.refs_0_), channel_id=1, source_target_pairs={{0,24},{2,26},{4,28},{6,30},{8,16},{10,18},{12,20},{14,22},{16,8},... | collective-permute-start | bytes 786440 | tf_op jit(solution)/shard_map/ppermute | solution.py:46
  38.4 20.5 %collective-permute-start.24 = (bf16[512,256]{1,0:T(8,128)(2,1)S(1)}, bf16[512,256]{1,0:T(8,128)(2,1)S(1)}, u32[]{:S(2)}, u32[]{:S(2)}) collective-permute-start(bf16[512,256]{1,0:T(8,128)(2,1)S(1)} %get-tuple-element.54.packed.refs_0_), channel_id=1, source_target_pairs={{0,2},{2,0},{4,6},{6,4},{8,10},{10,8},{12,14},{14,12},{16,18},{18,... | collective-permute-start | bytes 786440 | tf_op jit(solution)/shard_map/ppermute | solution.py:46
  46.2 13.2 %collective-permute-start.19 = (bf16[512,256]{1,0:T(8,128)(2,1)S(1)}, bf16[512,256]{1,0:T(8,128)(2,1)S(1)}, u32[]{:S(2)}, u32[]{:S(2)}) collective-permute-start(bf16[512,256]{1,0:T(8,128)(2,1)S(1)} %collective-permute-done.18.refs_2_), channel_id=1, source_target_pairs={{0,4},{2,6},{4,0},{6,2},{8,12},{10,14},{12,8},{14,10},{16,20},{18,... | collective-permute-start | bytes 786440 | tf_op jit(solution)/shard_map/ppermute | solution.py:46
  56.9 6.4 %collective-permute-start.21 = (bf16[512,256]{1,0:T(8,128)(2,1)S(1)}, bf16[512,256]{1,0:T(8,128)(2,1)S(1)}, u32[]{:S(2)}, u32[]{:S(2)}) collective-permute-start(bf16[512,256]{1,0:T(8,128)(2,1)S(1)} %collective-permute-done.20.refs_4_), channel_id=1, source_target_pairs={{0,4},{2,6},{4,0},{6,2},{8,12},{10,14},{12,8},{14,10},{16,20},{18,... | collective-permute-start | bytes 786440 | tf_op jit(solution)/shard_map/ppermute | solution.py:46
  58.3 7.7 %collective-permute-start.23 = (bf16[512,256]{1,0:T(8,128)(2,1)S(1)}, bf16[512,256]{1,0:T(8,128)(2,1)S(1)}, u32[]{:S(2)}, u32[]{:S(2)}) collective-permute-start(bf16[512,256]{1,0:T(8,128)(2,1)S(1)} %collective-permute-done.22.refs_6_), channel_id=1, source_target_pairs={{0,4},{2,6},{4,0},{6,2},{8,12},{10,14},{12,8},{14,10},{16,20},{18,... | collective-permute-start | bytes 786440 | tf_op jit(solution)/shard_map/ppermute | solution.py:46
  58.9 7.2 %collective-permute-start.25 = (bf16[512,256]{1,0:T(8,128)(2,1)S(1)}, bf16[512,256]{1,0:T(8,128)(2,1)S(1)}, u32[]{:S(2)}, u32[]{:S(2)}) collective-permute-start(bf16[512,256]{1,0:T(8,128)(2,1)S(1)} %collective-permute-done.16.refs_1_), channel_id=1, source_target_pairs={{0,2},{2,0},{4,6},{6,4},{8,10},{10,8},{12,14},{14,12},{16,18},{18,... | collective-permute-start | bytes 786440 | tf_op jit(solution)/shard_map/ppermute | solution.py:46
  58.9 7.7 %collective-permute-start.26 = (bf16[512,256]{1,0:T(8,128)(2,1)S(1)}, bf16[512,256]{1,0:T(8,128)(2,1)S(1)}, u32[]{:S(2)}, u32[]{:S(2)}) collective-permute-start(bf16[512,256]{1,0:T(8,128)(2,1)S(1)} %collective-permute-done.18.refs_2_), channel_id=1, source_target_pairs={{0,2},{2,0},{4,6},{6,4},{8,10},{10,8},{12,14},{14,12},{16,18},{18,... | collective-permute-start | bytes 786440 | tf_op jit(solution)/shard_map/ppermute | solution.py:46
  59.4 8.0 %collective-permute-start.28 = (bf16[512,256]{1,0:T(8,128)(2,1)S(1)}, bf16[512,256]{1,0:T(8,128)(2,1)S(1)}, u32[]{:S(2)}, u32[]{:S(2)}) collective-permute-start(bf16[512,256]{1,0:T(8,128)(2,1)S(1)} %collective-permute-done.20.refs_4_), channel_id=1, source_target_pairs={{0,2},{2,0},{4,6},{6,4},{8,10},{10,8},{12,14},{14,12},{16,18},{18,... | collective-permute-start | bytes 786440 | tf_op jit(solution)/shard_map/ppermute | solution.py:46
  63.2 5.7 %collective-permute-start.30 = (bf16[512,256]{1,0:T(8,128)(2,1)S(1)}, bf16[512,256]{1,0:T(8,128)(2,1)S(1)}, u32[]{:S(2)}, u32[]{:S(2)}) collective-permute-start(bf16[512,256]{1,0:T(8,128)(2,1)S(1)} %collective-permute-done.22.refs_6_), channel_id=1, source_target_pairs={{0,2},{2,0},{4,6},{6,4},{8,10},{10,8},{12,14},{14,12},{16,18},{18,... | collective-permute-start | bytes 786440 | tf_op jit(solution)/shard_map/ppermute | solution.py:46
  76.1 4.9 %collective-permute-start.35 = (f32[64,256]{1,0:T(8,128)S(1)}, f32[64,256]{1,0:T(8,128)S(1)}, u32[]{:S(2)}, u32[]{:S(2)}) collective-permute-start(f32[64,256]{1,0:T(8,128)S(1)} %get-tuple-element.74), channel_id=1, source_target_pairs={{0,4},{1,5},{2,6},{3,7},{4,0},{5,1},{6,2},{7,3},{8,12},{9,13},{10,... | collective-permute-start | bytes 196616 | tf_op jit(solution)/shard_map/ppermute | solution.py:52
  77.6 5.2 %collective-permute-start.36 = (f32[64,256]{1,0:T(8,128)S(1)}, f32[64,256]{1,0:T(8,128)S(1)}, u32[]{:S(2)}, u32[]{:S(2)}) collective-permute-start(f32[64,256]{1,0:T(8,128)S(1)} %get-tuple-element.75), channel_id=1, source_target_pairs={{0,5},{1,4},{2,7},{3,6},{4,1},{5,0},{6,3},{7,2},{8,13},{9,12},{10,... | collective-permute-start | bytes 196616 | tf_op jit(solution)/shard_map/ppermute | solution.py:52
  82.8 5.2 %collective-permute-start.37 = (f32[64,256]{1,0:T(8,128)S(1)}, f32[64,256]{1,0:T(8,128)S(1)}, u32[]{:S(2)}, u32[]{:S(2)}) collective-permute-start(f32[64,256]{1,0:T(8,128)S(1)} %add_xy.1.refs_0_), channel_id=1, source_target_pairs={{0,8},{2,10},{4,12},{6,14},{8,0},{10,2},{12,4},{14,6},{16,24},{18,... | collective-permute-start | bytes 196616 | tf_op jit(solution)/shard_map/ppermute | solution.py:46
  85.1 6.6 %collective-permute-start.38 = (f32[64,256]{1,0:T(8,128)S(1)}, f32[64,256]{1,0:T(8,128)S(1)}, u32[]{:S(2)}, u32[]{:S(2)}) collective-permute-start(f32[64,256]{1,0:T(8,128)S(1)} %add_xy.1.refs_0_), channel_id=1, source_target_pairs={{0,16},{2,18},{4,20},{6,22},{8,24},{10,26},{12,28},{14,30},{16,0},... | collective-permute-start | bytes 196616 | tf_op jit(solution)/shard_map/ppermute | solution.py:46
  87.6 6.1 %collective-permute-start.39 = (f32[64,256]{1,0:T(8,128)S(1)}, f32[64,256]{1,0:T(8,128)S(1)}, u32[]{:S(2)}, u32[]{:S(2)}) collective-permute-start(f32[64,256]{1,0:T(8,128)S(1)} %add_xy.1.refs_0_), channel_id=1, source_target_pairs={{0,24},{2,26},{4,28},{6,30},{8,16},{10,18},{12,20},{14,22},{16,8},... | collective-permute-start | bytes 196616 | tf_op jit(solution)/shard_map/ppermute | solution.py:46
  93.6 4.3 %collective-permute-start.40 = (f32[64,256]{1,0:T(8,128)S(1)}, f32[64,256]{1,0:T(8,128)S(1)}, u32[]{:S(2)}, u32[]{:S(2)}) collective-permute-start(f32[64,256]{1,0:T(8,128)S(1)} %add_z.1.refs_0_), channel_id=1, source_target_pairs={{0,1},{1,0},{2,3},{3,2},{4,5},{5,4},{6,7},{7,6},{8,9},{9,8},{10,11... | collective-permute-start | bytes 196616 | tf_op jit(solution)/shard_map/ppermute | solution.py:52
  95.3 5.2 %collective-permute-start.42 = (f32[64,256]{1,0:T(8,128)S(1)}, f32[64,256]{1,0:T(8,128)S(1)}, u32[]{:S(2)}, u32[]{:S(2)}) collective-permute-start(f32[64,256]{1,0:T(8,128)S(1)} %add_z.1.refs_0_), channel_id=1, source_target_pairs={{0,5},{1,4},{2,7},{3,6},{4,1},{5,0},{6,3},{7,2},{8,13},{9,12},{10,... | collective-permute-start | bytes 196616 | tf_op jit(solution)/shard_map/ppermute | solution.py:52
  (24 other events, 85.3 us)

commit v3 on v2

--- a/solution.py
+++ b/solution.py
@@ -56,15 +56,34 @@
     return lax.optimization_barrier(values)
 
 
-def gather_wide(own, beside=lambda: (), after=lambda early: ()):
-    nz = lax.axis_size(WIDE) // 4
-    zs = [to_wide(own, 4 * k) for k in range(1, nz)]
-    xo = to_wide(own, 2)
-    xo, early = together(xo, beside())
-    xz = [to_wide(z, 2) for z in zs]
-    near = [own, xo] + [p for pair in zip(zs, xz) for p in pair]
-    late = after(early)
-    return near + [to_wide(p, 1) for p in near], early, late
+def join(*parts):
+    def body(*refs):
+        at = 0
+        for ref in refs[:-1]:
+            refs[-1][at : at + ref.shape[0]] = ref[...]
+            at += ref.shape[0]
+
+    (out,) = call(body, "join", [shaped(sum(p.shape[0] for p in parts), parts[0].shape[1], parts[0].dtype)], parts)
+    return out
+
+
+def direct(nz):
+    return [3, 1] + list(range(4, nz))
+
+
+def over_z(own):
+    return [to_wide(own, 4 * k) for k in direct(lax.axis_size(WIDE) // 4)]
+
+
+def onward(over_x, over_z):
+    return [to_wide(over_z[0], 4), to_wide(over_x, 8), to_wide(join(*over_z), 2)]
+
+
+def place_of_block(z, x, nz):
+    place = jnp.where(z == 2, nz + x, x)
+    for at, k in enumerate(direct(nz), 2):
+        place = jnp.where(z == k, at + x * nz, place)
+    return place
 
 
 def pairwise(parts):
@@ -73,12 +92,13 @@
     return parts[0]
 
 
-def tile_sum(adj_ref, piece_refs, rows=None):
-    total = None
-    for k, ref in enumerate(piece_refs):
-        n = rows or ref.shape[0]
-        term = dot(adj_ref[:, k * n : (k + 1) * n], ref[:n])
+def tile_sum(adj_ref, piece_refs):
+    at, total = 0, None
+    for ref in piece_refs:
+        n = ref.shape[0]
+        term = dot(adj_ref[:, at : at + n], ref[...])
         total = term if total is None else total + term
+        at += n
     return total
 
 
@@ -107,13 +127,23 @@
     total = (rows + hr) * n_wide * n_hub
     edges = edge_rows.shape[0]
     pay = feat + LANES
+    half = n_wide * rows // 2
+
+    feats_z, feats_x = over_z(low_feats), to_wide(low_feats, 2)
+
+    mates = range(1, n_hub)
+
+    def to_hub(x, k):
+        return lax.ppermute(x, HUB, [(i, i ^ k) for i in range(n_hub)])
 
     at = [0]
     for n in (edges, edges, rows):
         at.append(at[-1] + n)
     ints = jnp.concatenate([edge_rows, edge_hubs, low_labels, hub_labels]).reshape(1, at[-1] + hr)
 
-    def edge_tables(ints, feats, hub_rows, link, link_t, low_count, low_hot, hub_hot_out, *parts):
+    def edge_tables(ints, feats, hub_rows, w, link, link_t, low_count, low_hot, hub_hot_out, feats_out, w_out, *parts):
+        feats_out[...] = feats[...]
+        w_out[...] = w[...]
         e_rows, e_hubs, labels = (ints[:, at[i] : at[i + 1]] for i in range(3))
         labels_hub = ints[:, at[3] :]
         h = lax.axis_index(HUB)
@@ -140,7 +170,7 @@
         hot = (lax.broadcasted_iota(jnp.int32, (classes, hr), 0) == labels_hub).astype(F32)
         hub_hot_out[...] = hot.T.astype(BF16)
 
-    link, link_t, low_count, low_target, hub_target, *parts1 = call(
+    link, link_t, low_count, low_target, hub_target, near_feats, near_w, *parts1 = call(
         edge_tables,
         "edge_tables",
         [
@@ -149,73 +179,89 @@
             shaped(rows, LANES, F32),
             shaped(rows, classes, BF16),
             shaped(hr, classes, BF16),
+            shaped(rows, feat, BF16),
+            shaped(feat, units, BF16),
         ]
         + [shaped(2 * hr, pay, F32) for _ in range(n_hub)],
-        [ints, low_feats, hub_feats],
+        [ints, low_feats, hub_feats, w_first],
         traffic=4 << 20,
     )
 
-    def adjacency(tiles, cols, low_count, adj, adj_t, scale):
+    feats_z, feats_x, parts1, low_count, near_feats, near_w = together(
+        feats_z, feats_x, parts1, low_count, near_feats, near_w
+    )
+    feats_on = onward(feats_x, feats_z)
+    feats_mate = [to_wide(join(near_feats, feats_x, *feats_z), 1)]
+
+    def adjacency(tiles, cols, low_count, adj, adj_t, adj_t_give, scale):
         w = lax.axis_index(WIDE)
         adj[...] = jnp.zeros_like(adj)
         adj_t[...] = jnp.zeros_like(adj_t)
+        adj_t_give[...] = jnp.zeros_like(adj_t_give)
         for r in range(blocks):
             for k in range(per_block):
                 b = cols[r, k]
                 rel = (b // blocks) ^ w
-                place = (rel & 1) * (n_wide // 2) + (rel >> 2) * 2 + ((rel >> 1) & 1)
-                at = pl.ds(pl.multiple_of((place * blocks + b % blocks) * tile, tile), tile)
+                place = place_of_block(rel >> 2, (rel >> 1) & 1, nz)
+                start = pl.multiple_of((place * blocks + b % blocks) * tile, tile)
                 value = tiles[r * per_block + k]
+                turned = value.T
+                at = pl.ds(pl.multiple_of((rel & 1) * half + start, tile), tile)
                 adj[r * tile : (r + 1) * tile, at] = value
-                adj_t[at, r * tile : (r + 1) * tile] = value.T
-        deg = dot(adj[...], jnp.ones((n_wide * rows, LANES), BF16))
+
+                @pl.when(rel & 1 == 0)
+                def _():
+                    adj_t[pl.ds(start, tile), r * tile : (r + 1) * tile] = turned
+
+                @pl.when(rel & 1 == 1)
+                def _():
+                    adj_t_give[pl.ds(start, tile), r * tile : (r + 1) * tile] = turned
+
+        deg = dot(adj[...], jnp.ones((2 * half, LANES), BF16))
         scale[...] = lax.rsqrt(1.0 + deg + low_count[...])
 
-    adj, adj_t, scale = call(
+    adj, adj_t, adj_t_give, scale = call(
         adjacency,
         "adjacency",
-        [shaped(rows, n_wide * rows, BF16), shaped(n_wide * rows, rows, BF16), shaped(rows, LANES, F32)],
+        [shaped(rows, 2 * half, BF16), shaped(half, rows, BF16), shaped(half, rows, BF16), shaped(rows, LANES, F32)],
         [low_tiles, tile_cols, low_count],
         smem=(1,),
         traffic=14 << 20,
     )
 
-    def to_hub(x, k):
-        return lax.ppermute(x, HUB, [(i, i ^ k) for i in range(n_hub)])
-
-    mates = range(1, n_hub)
-
-    def hub_first(feats, w, own, *refs):
+
+    def hub_first(w, own, *refs):
         got, (hub_scale, agg, act) = refs[:-3], refs[-3:]
         sums = own[:hr]
         for g in got:
             sums = sums + g[:hr]
         s = lax.rsqrt(1.0 + sums[:, feat : feat + 1])
         hub_scale[...] = jnp.broadcast_to(s, (hr, LANES))
-        a = ((feats[...].astype(F32) + sums[:, :feat]) * s).astype(BF16)
+        a = ((own[hr:, :feat] + sums[:, :feat]) * s).astype(BF16)
         agg[...] = a
         act[...] = jnp.maximum(dot(a, w[...]), 0.0).astype(BF16)
 
-    def hubs_to_first(early):
-        parts1 = early[0]
-        got1 = [to_hub(parts1[k], k) for k in mates]
-        outs = [shaped(hr, LANES, F32), shaped(hr, feat, BF16), shaped(hr, units, BF16)]
-        return call(hub_first, "hub_first", outs, [hub_feats, w_first, parts1[0]] + got1), got1
-
-    pieces1, (parts1, scale), ((hub_scale, agg1_hub, h1_hub), got1) = gather_wide(
-        low_feats, lambda: (parts1, scale), hubs_to_first
-    )
+    feats_on, feats_mate, scale, got1 = together(
+        feats_on, feats_mate, scale, [to_hub(parts1[k], k) for k in mates]
+    )
+    feats_mate.append(to_wide(join(*feats_on), 1))
+    pieces1 = [near_feats, feats_x] + feats_z + feats_on + feats_mate
     n_pieces = len(pieces1)
-
-    def low_first(adj, link, link_t, scale, field, w, act_hub, agg_hub, *refs):
+    hub_scale, agg1_hub, h1_hub = call(
+        hub_first,
+        "hub_first",
+        [shaped(hr, LANES, F32), shaped(hr, feat, BF16), shaped(hr, units, BF16)],
+        [near_w, parts1[0]] + got1,
+    )
+    def low_first(adj, link, link_t, scale, w, act_hub, agg_hub, *refs):
         pieces, refs = refs[:n_pieces], refs[n_pieces:]
-        hubs, (packed, own, *sends) = refs[:n_hub], refs[n_hub:]
+        hubs, (act_out, turned, own, *sends) = refs[:n_hub], refs[n_hub:]
         around = jnp.concatenate([r[hr:, :feat] for r in hubs] * 2, axis=0).astype(BF16)
-        s = tile_sum(adj, pieces) + field[...].astype(F32) + dot(link_t[...], around)
+        s = tile_sum(adj, pieces) + pieces[0][...].astype(F32) + dot(link_t[...], around)
         a = (s * scale[:, :1]).astype(BF16)
         act = jnp.maximum(dot(a, w[...]), 0.0).astype(BF16)
-        packed[:rows] = act
-        packed[rows:] = a.T
+        act_out[...] = act
+        turned[...] = a.T
         sums = dot(link[:, :rows], act) + dot(link[:, rows:], act)
         own[...] = sums[:hr]
         for k, send in enumerate(sends, 1):
@@ -223,11 +269,12 @@
             send[hr : 2 * hr] = sums[k * hr : (k + 1) * hr]
             send[2 * hr :] = agg_hub[...].astype(F32)
 
-    packed, own2, *sends2 = call(
+    h1, agg1_t, own2, *sends2 = call(
         low_first,
         "low_first",
-        [shaped(2 * rows, units, BF16), shaped(hr, units, F32)] + [shaped(3 * hr, units, F32) for _ in mates],
-        [adj, link, link_t, scale, low_feats, w_first, h1_hub, agg1_hub] + pieces1 + [parts1[0]] + got1,
+        [shaped(rows, units, BF16), shaped(feat, rows, BF16), shaped(hr, units, F32)]
+        + [shaped(3 * hr, units, F32) for _ in mates],
+        [adj, link, link_t, scale, near_w, h1_hub, agg1_hub] + pieces1 + [parts1[0]] + got1,
     )
 
     def hub_second(act, hub_scale, w, target, own, *refs):
@@ -244,21 +291,30 @@
         dz[...] = d
         q[...] = (dot_nt(d, w[...]) * s).astype(BF16)
 
-    def hubs_to_second(got2):
-        outs = [shaped(hr, classes, F32), shaped(hr, units, BF16), shaped(hr, classes, BF16), shaped(hr, units, BF16)]
-        made = call(hub_second, "hub_second", outs, [h1_hub, hub_scale, w_second, hub_target, own2] + got2)
-        return made, [to_hub(made[3], k) for k in mates]
-
-    pieces2, got2, ((hub_logits, agg2_hub, dz2_hub, q_hub), q_hub_mates) = gather_wide(
-        packed, lambda: [to_hub(x, k) for k, x in enumerate(sends2, 1)], hubs_to_second
-    )
-
-    def low_second(adj, link_t, scale, packed, w, target, act_hub, agg_hub, dz_hub, *refs):
-        pieces, refs = refs[:n_pieces], refs[n_pieces:]
+    h1_z, h1_x, agg1_x, got2 = together(
+        over_z(h1), to_wide(h1, 2), to_wide(agg1_t, 2), [to_hub(x, k) for k, x in enumerate(sends2, 1)]
+    )
+    hub_logits, agg2_hub, dz2_hub, q_hub = call(
+        hub_second,
+        "hub_second",
+        [shaped(hr, classes, F32), shaped(hr, units, BF16), shaped(hr, classes, BF16), shaped(hr, units, BF16)],
+        [h1_hub, hub_scale, w_second, hub_target, own2] + got2,
+    )
+    h1_on, agg1_z, q_hub, adj_t_give = together(onward(h1_x, h1_z), over_z(agg1_t), q_hub, adj_t_give)
+    adj_t_mate = to_wide(adj_t_give, 1)
+    agg1_on = onward(agg1_x, agg1_z)
+    h1_mate = [to_wide(join(h1, h1_x, *h1_z, *h1_on), 1)]
+    q_hub_mates = [to_hub(q_hub, k) for k in mates]
+    pieces2 = [h1, h1_x] + h1_z + h1_on
+    turned = [agg1_t, agg1_x] + agg1_z + agg1_on
+    n_own = len(pieces2)
+
+    def low_second(adj, link_t, scale, w, target, act_hub, agg_hub, dz_hub, *refs):
+        pieces, refs = refs[: n_own + 1], refs[n_own + 1 :]
         got, (logits, grad, q_out) = refs[: n_hub - 1], refs[n_hub - 1 :]
         around = jnp.concatenate([act_hub[...]] + [g[:hr].astype(BF16) for g in got], axis=0)
         around = jnp.concatenate([around, around], axis=0)
-        s = tile_sum(adj, pieces, rows) + packed[:rows].astype(F32) + dot(link_t[...], around)
+        s = tile_sum(adj, pieces) + pieces[0][...].astype(F32) + dot(link_t[...], around)
         a = (s * scale[:, :1]).astype(BF16)
         y = dot(a, w[...])
         logits[...] = y
@@ -270,24 +326,30 @@
         low_second,
         "low_second",
         [shaped(rows, classes, F32), shaped(units, classes, F32), shaped(rows, units, BF16)],
-        [adj, link_t, scale, packed, w_second, low_target, h1_hub, agg2_hub, dz2_hub] + pieces2 + got2,
-    )
-
-    def back_first(adj_t, link, link_t, q, grad_second, act_hub, agg_hub, q_hub, *refs):
-        pieces, refs = refs[:n_pieces], refs[n_pieces:]
+        [adj, link_t, scale, w_second, low_target, h1_hub, agg2_hub, dz2_hub] + pieces2 + h1_mate + got2,
+    )
+
+    q_low, q_hub_mates = together(q_low, q_hub_mates)
+    q_mate = to_wide(q_low, 1)
+
+    def back_first(adj_t, adj_t_mate, link, link_t, q, q_mate, grad_second, act_hub, agg_hub, q_hub, *refs):
+        pieces, refs = refs[:n_own], refs[n_own:]
+        turned, refs = refs[:n_own], refs[n_own:]
         got, refs = refs[: n_hub - 1], refs[n_hub - 1 :]
         q_mates, (keep, give) = refs[: n_hub - 1], refs[n_hub - 1 :]
         q_own = q[...]
         around = jnp.concatenate([q_hub[...]] + [g[...] for g in q_mates], axis=0)
         around = jnp.concatenate([around, around], axis=0)
-        grad = None
-        for k, piece in enumerate(pieces):
-            term = dot(adj_t[k * rows : (k + 1) * rows], q_own)
-            if k == 0:
-                term = term + q_own.astype(F32) + dot(link_t[...], around)
-            term = jnp.where(piece[:rows].astype(F32) > 0.0, term, 0.0).astype(BF16)
-            term = dot(piece[rows:], term)
-            grad = term if grad is None else grad + term
+        grad, at = None, 0
+        for piece, agg in zip(pieces, turned):
+            for n in range(0, piece.shape[0], rows):
+                term = dot(adj_t[at : at + rows], q_own) + dot(adj_t_mate[at : at + rows], q_mate[...])
+                if at == 0:
+                    term = term + q_own.astype(F32) + dot(link_t[...], around)
+                term = jnp.where(piece[n : n + rows].astype(F32) > 0.0, term, 0.0).astype(BF16)
+                term = dot(agg[n : n + feat], term)
+                grad = term if grad is None else grad + term
+                at += rows
         sums = dot(link[:, :rows], q_own) + dot(link[:, rows:], q_own)
         for k in range(n_hub):
             term = sums[k * hr : (k + 1) * hr]
@@ -312,7 +374,7 @@
         back_first,
         "back_first",
         [shaped(units, classes, F32), shaped(units, classes, F32)],
-        [adj_t, link, link_t, q_low, grad_second, h1_hub, agg1_hub, q_hub] + pieces2 + got2 + q_hub_mates,
+        [adj_t, adj_t_mate, link, link_t, q_low, q_mate, grad_second, h1_hub, agg1_hub, q_hub] + pieces2 + turned + got2 + q_hub_mates,
     )
     got = to_wide(give, 1)
 

time: 103 us -> 92.7 us (0.900)
  waiting for transfers between devices: 50.1 us -> 36.1 us
  starting transfers between devices: 34.9 us -> 40.6 us
  local copies, waits for them, and re-layouts: 6.91 us -> 3.19 us
  Pallas kernels: 9.09 us -> 11 us
    ppermute x38 -> x31, waiting for transfers between devices: 42.1 us -> 26.1 us  [to_wide(): lax.ppermute(x, WIDE, [(i, i ^ k) for i in range(lax.axis_size(WIDE))])]
    ppermute x38 -> x31, starting transfers between devices: 24.2 us -> 28.9 us  [to_wide(): lax.ppermute(x, WIDE, [(i, i ^ k) for i in range(lax.axis_size(WIDE))])]
    unnamed x18 -> x12, local copies, waits for them, and re-layouts: 6.9 us -> 3.19 us
    ppermute x3, waiting for transfers between devices: 0.25 us -> 2.58 us  [to_hub(): return lax.ppermute(x, HUB, [(i, i ^ k) for i in range(n_hub)])]
    pallas_call x11 -> x17, Pallas kernels: 9.09 us -> 11 us  [call(): pl.pallas_call(body, name=name, out_shape=outs, in_specs=[pl.BlockSpec(me...]
  transfers between devices with their start and end apart: 47 -> 40, of which waited for: 20 -> 22; matrix products, arithmetic and copies ran while one was open for 1% -> 1% of each run, Pallas kernels for 5% -> 8%
where the time goes in v3:
time: 92.7 us; the launch traced here: 92.4 us
  starting transfers between devices  40.6 us (44%)
  waiting for transfers between devices  36.1 us (39%)
  Pallas kernels  11 us (12%)
  local copies, waits for them, and re-layouts  3.19 us (3%)
    ppermute x31, starting transfers between devices, to_wide(): lax.ppermute(x, WIDE, [(i, i ^ k) for i in range(lax.axis_size(WIDE))])  28.9 us
    ppermute x31, waiting for transfers between devices, to_wide(): lax.ppermute(x, WIDE, [(i, i ^ k) for i in range(lax.axis_size(WIDE))])  26.1 us
    pallas_call x17, Pallas kernels, call(): pl.pallas_call(body, name=name, out_shape=outs, in_specs=[pl.BlockSpec(me...  11 us
    ppermute x6, waiting for transfers between devices, to_both(): return lax.ppermute(x, (WIDE, HUB), pairs)  7.39 us
    ppermute x6, starting transfers between devices, to_both(): return lax.ppermute(x, (WIDE, HUB), pairs)  7.11 us
    ppermute x3, starting transfers between devices, to_hub(): return lax.ppermute(x, HUB, [(i, i ^ k) for i in range(n_hub)])  4.57 us
    unnamed x12, local copies, waits for them, and re-layouts  3.19 us
    ppermute x3, waiting for transfers between devices, to_hub(): return lax.ppermute(x, HUB, [(i, i ^ k) for i in range(n_hub)])  2.58 us
  transfers between devices with their start and end apart: 40, of which 22 were waited for; matrix products, arithmetic and copies ran while one was open for 1% of the time, Pallas kernels for 8%

profile of v3, /device:TPU:0, one launch (start us, length us, event | category | flops | bytes accessed | tf_op | source)
XLA Modules:
  0.0 92.4 jit_solution(15576038528250846243)
XLA Ops:
  0.6 5.1 %collective-permute-start = (bf16[256,256]{1,0:T(8,128)(2,1)}, bf16[256,256]{1,0:T(8,128)(2,1)S(1)}, u32[]{:S(2)}, u32[]{:S(2)}) collective-permute-start(bf16[256,256]{1,0:T(8,128)(2,1)} %feats.1), channel_id=1, source_target_pairs={{0,24},{2,26},{4,28},{6,30},{8,16},{10,18},{12,20},{14,22},{16,8},... | collective-permute-start | bytes 393224 | tf_op jit(solution)/shard_map/ppermute | solution.py:46
  5.8 1.5 %collective-permute-start.2 = (bf16[256,256]{1,0:T(8,128)(2,1)}, bf16[256,256]{1,0:T(8,128)(2,1)S(1)}, u32[]{:S(2)}, u32[]{:S(2)}) collective-permute-start(bf16[256,256]{1,0:T(8,128)(2,1)} %feats.1), channel_id=1, source_target_pairs={{0,4},{2,6},{4,0},{6,2},{8,12},{10,14},{12,8},{14,10},{16,20},{18,... | collective-permute-start | bytes 393224 | tf_op jit(solution)/shard_map/ppermute | solution.py:46
  11.1 1.3 %collective-permute-done.1.refs_1_.refs_3_ = bf16[256,256]{1,0:T(8,128)(2,1)S(1)} collective-permute-done((bf16[256,256]{1,0:T(8,128)(2,1)}, bf16[256,256]{1,0:T(8,128)(2,1)S(1)}, u32[]{:S(2)}, u32[]{:S(2)}) %collective-permute-start.1) | collective-permute-done | bytes 131104 | tf_op jit(solution)/shard_map/ppermute | solution.py:46
  12.5 1.6 %collective-permute-start.5 = (bf16[512,256]{1,0:T(8,128)(2,1)S(1)}, bf16[512,256]{1,0:T(8,128)(2,1)S(1)}, u32[]{:S(2)}, u32[]{:S(2)}) collective-permute-start(bf16[512,256]{1,0:T(8,128)(2,1)S(1)} %join.6), channel_id=1, source_target_pairs={{0,4},{2,6},{4,0},{6,2},{8,12},{10,14},{12,8},{14,10},{16,20},{18,... | collective-permute-start | bytes 786440 | tf_op jit(solution)/shard_map/ppermute | solution.py:46
  14.1 1.7 %collective-permute-start.3 = (bf16[256,256]{1,0:T(8,128)(2,1)S(1)}, bf16[256,256]{1,0:T(8,128)(2,1)S(1)}, u32[]{:S(2)}, u32[]{:S(2)}) collective-permute-start(bf16[256,256]{1,0:T(8,128)(2,1)S(1)} %collective-permute-done.refs_0_.refs_2_), channel_id=1, source_target_pairs={{0,8},{2,10},{4,12},{6,14},{8,0},{10,2},{12,4},{14,6},{16,24},{18,... | collective-permute-start | bytes 393224 | tf_op jit(solution)/shard_map/ppermute | solution.py:46
  16.4 1.5 %collective-permute-start.7 = (f32[32,384]{1,0:T(8,128)S(1)}, f32[32,384]{1,0:T(8,128)S(1)}, u32[]{:S(2)}, u32[]{:S(2)}) collective-permute-start(f32[32,384]{1,0:T(8,128)S(1)} %get-tuple-element.80), channel_id=1, source_target_pairs={{0,1},{1,0},{2,3},{3,2},{4,5},{5,4},{6,7},{7,6},{8,9},{9,8},{10,11... | collective-permute-start | bytes 147464 | tf_op jit(solution)/shard_map/ppermute | solution.py:137
  18.6 3.8 %adjacency.1 = (bf16[256,4096]{1,0:T(8,128)(2,1)S(1)}, bf16[2048,256]{1,0:T(8,128)(2,1)S(1)}, bf16[2048,256]{1,0:T(8,128)(2,1)S(1)}, f32[256,128]{1,0:T(8,128)S(1)}) custom-call(bf16[32,128,128]{2,1,0:T(8,128)(2,1)S(1)} %copy-done, s32[2,16]{1,0:T(2,128)S(1)} %copy-done.5, f32[256,128]{1,0:T(8,128)S(1)} %get-tuple-element.72.low_count), custom_call_target="tpu_custom_call" | custom-call | bytes 14680064 | tf_op jit(solution)/shard_map/adjacency/pallas_call | solution.py:22
  22.5 2.3 %collective-permute-done.4.refs_1_.refs_5_ = bf16[256,256]{1,0:T(8,128)(2,1)S(1)} collective-permute-done((bf16[256,256]{1,0:T(8,128)(2,1)S(1)}, bf16[256,256]{1,0:T(8,128)(2,1)S(1)}, u32[]{:S(2)}, u32[]{:S(2)}) %collective-permute-start.4) | collective-permute-done | bytes 131104 | tf_op jit(solution)/shard_map/ppermute | solution.py:46
  25.1 1.7 %collective-permute-done.8.refs_8_ = bf16[1024,256]{1,0:T(8,128)(2,1)S(1)} collective-permute-done((bf16[1024,256]{1,0:T(8,128)(2,1)S(1)}, bf16[1024,256]{1,0:T(8,128)(2,1)S(1)}, u32[]{:S(2)}, u32[]{:S(2)}) %collective-permute-start.8) | collective-permute-done | bytes 524320 | tf_op jit(solution)/shard_map/ppermute | solution.py:46
  29.3 1.5 %collective-permute-start.12 = (bf16[256,256]{1,0:T(8,128)(2,1)S(1)}, bf16[256,256]{1,0:T(8,128)(2,1)S(1)}, u32[]{:S(2)}, u32[]{:S(2)}) collective-permute-start(bf16[256,256]{1,0:T(8,128)(2,1)S(1)} %get-tuple-element.97.refs_7_), channel_id=1, source_target_pairs={{0,4},{2,6},{4,0},{6,2},{8,12},{10,14},{12,8},{14,10},{16,20},{18,... | collective-permute-start | bytes 393224 | tf_op jit(solution)/shard_map/ppermute | solution.py:46
  30.8 1.5 %collective-permute-start.13 = (f32[48,256]{1,0:T(8,128)S(1)}, f32[48,256]{1,0:T(8,128)S(1)}, u32[]{:S(2)}, u32[]{:S(2)}) collective-permute-start(f32[48,256]{1,0:T(8,128)S(1)} %get-tuple-element.98), channel_id=1, source_target_pairs={{0,1},{1,0},{2,3},{3,2},{4,5},{5,4},{6,7},{7,6},{8,9},{9,8},{10,11... | collective-permute-start | bytes 147464 | tf_op jit(solution)/shard_map/ppermute | solution.py:137
  32.3 2.6 %collective-permute-done.13.refs_0_.refs_8_.refs_14_ = f32[48,256]{1,0:T(8,128)S(1)} collective-permute-done((f32[48,256]{1,0:T(8,128)S(1)}, f32[48,256]{1,0:T(8,128)S(1)}, u32[]{:S(2)}, u32[]{:S(2)}) %collective-permute-start.13) | collective-permute-done | bytes 49184 | tf_op jit(solution)/shard_map/ppermute | solution.py:137
  37.2 3.2 %collective-permute-start.17 = (bf16[256,256]{1,0:T(8,128)(2,1)S(1)}, bf16[256,256]{1,0:T(8,128)(2,1)S(1)}, u32[]{:S(2)}, u32[]{:S(2)}) collective-permute-start(bf16[256,256]{1,0:T(8,128)(2,1)S(1)} %get-tuple-element.97.refs_7_), channel_id=1, source_target_pairs={{0,24},{2,26},{4,28},{6,30},{8,16},{10,18},{12,20},{14,22},{16,8},... | collective-permute-start | bytes 393224 | tf_op jit(solution)/shard_map/ppermute | solution.py:46
  43.5 1.9 %collective-permute-done.17.refs_0_.refs_9_ = bf16[256,256]{1,0:T(8,128)(2,1)S(1)} collective-permute-done((bf16[256,256]{1,0:T(8,128)(2,1)S(1)}, bf16[256,256]{1,0:T(8,128)(2,1)S(1)}, u32[]{:S(2)}, u32[]{:S(2)}) %collective-permute-start.17) | collective-permute-done | bytes 131104 | tf_op jit(solution)/shard_map/ppermute | solution.py:46
  45.4 4.5 %collective-permute-done.18.refs_1_.refs_10_ = bf16[256,256]{1,0:T(8,128)(2,1)S(1)} collective-permute-done((bf16[256,256]{1,0:T(8,128)(2,1)S(1)}, bf16[256,256]{1,0:T(8,128)(2,1)S(1)}, u32[]{:S(2)}, u32[]{:S(2)}) %collective-permute-start.18) | collective-permute-done | bytes 131104 | tf_op jit(solution)/shard_map/ppermute | solution.py:46
  49.9 1.4 %collective-permute-done.14.refs_4_ = bf16[256,256]{1,0:T(8,128)(2,1)S(1)} collective-permute-done((bf16[256,256]{1,0:T(8,128)(2,1)S(1)}, bf16[256,256]{1,0:T(8,128)(2,1)S(1)}, u32[]{:S(2)}, u32[]{:S(2)}) %collective-permute-start.14) | collective-permute-done | bytes 131104 | tf_op jit(solution)/shard_map/ppermute | solution.py:46
  52.0 1.5 %collective-permute-start.25 = (bf16[512,256]{1,0:T(8,128)(2,1)S(1)}, bf16[512,256]{1,0:T(8,128)(2,1)S(1)}, u32[]{:S(2)}, u32[]{:S(2)}) collective-permute-start(bf16[512,256]{1,0:T(8,128)(2,1)S(1)} %join.11), channel_id=1, source_target_pairs={{0,4},{2,6},{4,0},{6,2},{8,12},{10,14},{12,8},{14,10},{16,20},{18,... | collective-permute-start | bytes 786440 | tf_op jit(solution)/shard_map/ppermute | solution.py:46
  53.5 1.5 %collective-permute-start.21 = (bf16[16,256]{1,0:T(8,128)(2,1)S(1)}, bf16[16,256]{1,0:T(8,128)(2,1)S(1)}, u32[]{:S(2)}, u32[]{:S(2)}) collective-permute-start(bf16[16,256]{1,0:T(8,128)(2,1)S(1)} %get-tuple-element.115.q_hub), channel_id=1, source_target_pairs={{0,1},{1,0},{2,3},{3,2},{4,5},{5,4},{6,7},{7,6},{8,9},{9,8},{10,11... | collective-permute-start | bytes 24584 | tf_op jit(solution)/shard_map/ppermute | solution.py:137
  55.0 2.6 %collective-permute-start.24 = (bf16[256,256]{1,0:T(8,128)(2,1)S(1)}, bf16[256,256]{1,0:T(8,128)(2,1)S(1)}, u32[]{:S(2)}, u32[]{:S(2)}) collective-permute-start(bf16[256,256]{1,0:T(8,128)(2,1)S(1)} %collective-permute-done.12.refs_8_), channel_id=1, source_target_pairs={{0,16},{2,18},{4,20},{6,22},{8,24},{10,26},{12,28},{14,30},{16,0},... | collective-permute-start | bytes 393224 | tf_op jit(solution)/shard_map/ppermute | solution.py:46
  57.6 1.8 %low_second.1 = (f32[256,256]{1,0:T(8,128)}, f32[256,256]{1,0:T(8,128)S(1)}, bf16[256,256]{1,0:T(8,128)(2,1)S(1)}) custom-call(bf16[256,4096]{1,0:T(8,128)(2,1)S(1)} %get-tuple-element.73.adj, bf16[256,64]{1,0:T(8,128)(2,1)S(1)} %get-tuple-element.74.link_t, f32[256,128]{1,0:T(8,128)S(1)} %get-tuple-element.81.scale, bf16[256,256]{1,0:T(8,128)(2,1)S(1)} %copy-done.1, ...), custom_call_target="tpu_custom_call" | custom-call | bytes 1048576 | tf_op jit(solution)/shard_map/low_second/pallas_call | solution.py:22
  59.5 4.2 %collective-permute-done.24.refs_12_ = bf16[256,256]{1,0:T(8,128)(2,1)S(1)} collective-permute-done((bf16[256,256]{1,0:T(8,128)(2,1)S(1)}, bf16[256,256]{1,0:T(8,128)(2,1)S(1)}, u32[]{:S(2)}, u32[]{:S(2)}) %collective-permute-start.24) | collective-permute-done | bytes 131104 | tf_op jit(solution)/shard_map/ppermute | solution.py:46
  63.7 1.3 %collective-permute-done.23.refs_11_ = bf16[256,256]{1,0:T(8,128)(2,1)S(1)} collective-permute-done((bf16[256,256]{1,0:T(8,128)(2,1)S(1)}, bf16[256,256]{1,0:T(8,128)(2,1)S(1)}, u32[]{:S(2)}, u32[]{:S(2)}) %collective-permute-start.23) | collective-permute-done | bytes 131104 | tf_op jit(solution)/shard_map/ppermute | solution.py:46
  65.0 1.7 %back_first.1 = (f32[256,256]{1,0:T(8,128)S(1)}, f32[256,256]{1,0:T(8,128)S(1)}) custom-call(bf16[2048,256]{1,0:T(8,128)(2,1)S(1)} %get-tuple-element.112.adj_t, bf16[2048,256]{1,0:T(8,128)(2,1)S(1)} %collective-permute-done.20.adj_t_mate, bf16[32,512]{1,0:T(8,128)(2,1)S(1)} %get-tuple-element.89.link, bf16[256,64]{1,0:T(8,128)(2,1)S(1)} %get-tuple-element.74.link_t, ...), custom_call_target="tpu_custom_call" | custom-call | bytes 1048576 | tf_op jit(solution)/shard_map/back_first/pallas_call | solution.py:22
  66.7 1.5 %collective-permute-done.26.got = f32[256,256]{1,0:T(8,128)S(1)} collective-permute-done((f32[256,256]{1,0:T(8,128)S(1)}, f32[256,256]{1,0:T(8,128)S(1)}, u32[]{:S(2)}, u32[]{:S(2)}) %collective-permute-start.26) | collective-permute-done | bytes 262176 | tf_op jit(solution)/shard_map/ppermute | solution.py:46
  69.4 2.4 %collective-permute-start.29 = (f32[64,256]{1,0:T(8,128)S(1)}, f32[64,256]{1,0:T(8,128)S(1)}, u32[]{:S(2)}, u32[]{:S(2)}) collective-permute-start(f32[64,256]{1,0:T(8,128)S(1)} %get-tuple-element.127), channel_id=1, source_target_pairs={{0,5},{1,4},{2,7},{3,6},{4,1},{5,0},{6,3},{7,2},{8,13},{9,12},{10,... | collective-permute-start | bytes 196616 | tf_op jit(solution)/shard_map/ppermute | solution.py:52
  73.7 1.4 %collective-permute-done.29.refs_3_ = f32[64,256]{1,0:T(8,128)S(1)} collective-permute-done((f32[64,256]{1,0:T(8,128)S(1)}, f32[64,256]{1,0:T(8,128)S(1)}, u32[]{:S(2)}, u32[]{:S(2)}) %collective-permute-start.29) | collective-permute-done | bytes 65568 | tf_op jit(solution)/shard_map/ppermute | solution.py:52
  76.1 3.5 %collective-permute-start.32 = (f32[64,256]{1,0:T(8,128)S(1)}, f32[64,256]{1,0:T(8,128)S(1)}, u32[]{:S(2)}, u32[]{:S(2)}) collective-permute-start(f32[64,256]{1,0:T(8,128)S(1)} %add_xy.1.refs_0_), channel_id=1, source_target_pairs={{0,24},{2,26},{4,28},{6,30},{8,16},{10,18},{12,20},{14,22},{16,8},... | collective-permute-start | bytes 196616 | tf_op jit(solution)/shard_map/ppermute | solution.py:46
  79.6 1.4 %collective-permute-done.31.refs_2_ = f32[64,256]{1,0:T(8,128)S(1)} collective-permute-done((f32[64,256]{1,0:T(8,128)S(1)}, f32[64,256]{1,0:T(8,128)S(1)}, u32[]{:S(2)}, u32[]{:S(2)}) %collective-permute-start.31) | collective-permute-done | bytes 65568 | tf_op jit(solution)/shard_map/ppermute | solution.py:46
  81.0 1.6 %collective-permute-done.32.refs_3_ = f32[64,256]{1,0:T(8,128)S(1)} collective-permute-done((f32[64,256]{1,0:T(8,128)S(1)}, f32[64,256]{1,0:T(8,128)S(1)}, u32[]{:S(2)}, u32[]{:S(2)}) %collective-permute-start.32) | collective-permute-done | bytes 65568 | tf_op jit(solution)/shard_map/ppermute | solution.py:46
  83.8 1.4 %collective-permute-start.34 = (f32[64,256]{1,0:T(8,128)S(1)}, f32[64,256]{1,0:T(8,128)S(1)}, u32[]{:S(2)}, u32[]{:S(2)}) collective-permute-start(f32[64,256]{1,0:T(8,128)S(1)} %add_z.1.refs_0_), channel_id=1, source_target_pairs={{0,4},{1,5},{2,6},{3,7},{4,0},{5,1},{6,2},{7,3},{8,12},{9,13},{10,... | collective-permute-start | bytes 196616 | tf_op jit(solution)/shard_map/ppermute | solution.py:52
  88.1 2.2 %collective-permute-done.35.refs_3_ = f32[64,256]{1,0:T(8,128)S(1)} collective-permute-done((f32[64,256]{1,0:T(8,128)S(1)}, f32[64,256]{1,0:T(8,128)S(1)}, u32[]{:S(2)}, u32[]{:S(2)}) %collective-permute-start.35) | collective-permute-done | bytes 65568 | tf_op jit(solution)/shard_map/ppermute | solution.py:52
  90.4 1.2 %collective-permute-done.39.refs_7_ = f32[64,256]{1,0:T(8,128)S(1)} collective-permute-done((f32[64,256]{1,0:T(8,128)S(1)}, f32[64,256]{1,0:T(8,128)S(1)}, u32[]{:S(2)}, u32[]{:S(2)}) %collective-permute-start.39) | collective-permute-done | bytes 65568 | tf_op jit(solution)/shard_map/ppermute | solution.py:46
  (79 shorter events, 23.2 us)
Async XLA Ops:
  0.6 10.4 %collective-permute-start = (bf16[256,256]{1,0:T(8,128)(2,1)}, bf16[256,256]{1,0:T(8,128)(2,1)S(1)}, u32[]{:S(2)}, u32[]{:S(2)}) collective-permute-start(bf16[256,256]{1,0:T(8,128)(2,1)} %feats.1), channel_id=1, source_target_pairs={{0,24},{2,26},{4,28},{6,30},{8,16},{10,18},{12,20},{14,22},{16,8},... | collective-permute-start | bytes 393224 | tf_op jit(solution)/shard_map/ppermute | solution.py:46
  5.8 6.6 %collective-permute-start.1 = (bf16[256,256]{1,0:T(8,128)(2,1)}, bf16[256,256]{1,0:T(8,128)(2,1)S(1)}, u32[]{:S(2)}, u32[]{:S(2)}) collective-permute-start(bf16[256,256]{1,0:T(8,128)(2,1)} %feats.1), channel_id=1, source_target_pairs={{0,8},{2,10},{4,12},{6,14},{8,0},{10,2},{12,4},{14,6},{16,24},{18,... | collective-permute-start | bytes 393224 | tf_op jit(solution)/shard_map/ppermute | solution.py:46
  5.8 6.6 %collective-permute-start.2 = (bf16[256,256]{1,0:T(8,128)(2,1)}, bf16[256,256]{1,0:T(8,128)(2,1)S(1)}, u32[]{:S(2)}, u32[]{:S(2)}) collective-permute-start(bf16[256,256]{1,0:T(8,128)(2,1)} %feats.1), channel_id=1, source_target_pairs={{0,4},{2,6},{4,0},{6,2},{8,12},{10,14},{12,8},{14,10},{16,20},{18,... | collective-permute-start | bytes 393224 | tf_op jit(solution)/shard_map/ppermute | solution.py:46
  12.4 12.4 %collective-permute-start.6 = (bf16[1024,256]{1,0:T(8,128)(2,1)S(1)}, bf16[1024,256]{1,0:T(8,128)(2,1)S(1)}, u32[]{:S(2)}, u32[]{:S(2)}) collective-permute-start(bf16[1024,256]{1,0:T(8,128)(2,1)S(1)} %join.7), channel_id=1, source_target_pairs={{0,2},{2,0},{4,6},{6,4},{8,10},{10,8},{12,14},{14,12},{16,18},{18,... | collective-permute-start | bytes 1572872 | tf_op jit(solution)/shard_map/ppermute | solution.py:46
  12.5 12.2 %collective-permute-start.5 = (bf16[512,256]{1,0:T(8,128)(2,1)S(1)}, bf16[512,256]{1,0:T(8,128)(2,1)S(1)}, u32[]{:S(2)}, u32[]{:S(2)}) collective-permute-start(bf16[512,256]{1,0:T(8,128)(2,1)S(1)} %join.6), channel_id=1, source_target_pairs={{0,4},{2,6},{4,0},{6,2},{8,12},{10,14},{12,8},{14,10},{16,20},{18,... | collective-permute-start | bytes 786440 | tf_op jit(solution)/shard_map/ppermute | solution.py:46
  14.1 8.4 %collective-permute-start.3 = (bf16[256,256]{1,0:T(8,128)(2,1)S(1)}, bf16[256,256]{1,0:T(8,128)(2,1)S(1)}, u32[]{:S(2)}, u32[]{:S(2)}) collective-permute-start(bf16[256,256]{1,0:T(8,128)(2,1)S(1)} %collective-permute-done.refs_0_.refs_2_), channel_id=1, source_target_pairs={{0,8},{2,10},{4,12},{6,14},{8,0},{10,2},{12,4},{14,6},{16,24},{18,... | collective-permute-start | bytes 393224 | tf_op jit(solution)/shard_map/ppermute | solution.py:46
  15.8 9.0 %collective-permute-start.4 = (bf16[256,256]{1,0:T(8,128)(2,1)S(1)}, bf16[256,256]{1,0:T(8,128)(2,1)S(1)}, u32[]{:S(2)}, u32[]{:S(2)}) collective-permute-start(bf16[256,256]{1,0:T(8,128)(2,1)S(1)} %collective-permute-done.2.refs_1_), channel_id=1, source_target_pairs={{0,16},{2,18},{4,20},{6,22},{8,24},{10,26},{12,28},{14,30},{16,0},... | collective-permute-start | bytes 393224 | tf_op jit(solution)/shard_map/ppermute | solution.py:46
  16.4 6.0 %collective-permute-start.7 = (f32[32,384]{1,0:T(8,128)S(1)}, f32[32,384]{1,0:T(8,128)S(1)}, u32[]{:S(2)}, u32[]{:S(2)}) collective-permute-start(f32[32,384]{1,0:T(8,128)S(1)} %get-tuple-element.80), channel_id=1, source_target_pairs={{0,1},{1,0},{2,3},{3,2},{4,5},{5,4},{6,7},{7,6},{8,9},{9,8},{10,11... | collective-permute-start | bytes 147464 | tf_op jit(solution)/shard_map/ppermute | solution.py:137
  27.9 8.2 %collective-permute-start.9 = (bf16[256,256]{1,0:T(8,128)(2,1)S(1)}, bf16[256,256]{1,0:T(8,128)(2,1)S(1)}, u32[]{:S(2)}, u32[]{:S(2)}) collective-permute-start(bf16[256,256]{1,0:T(8,128)(2,1)S(1)} %get-tuple-element.96.refs_0_), channel_id=1, source_target_pairs={{0,24},{2,26},{4,28},{6,30},{8,16},{10,18},{12,20},{14,22},{16,8},... | collective-permute-start | bytes 393224 | tf_op jit(solution)/shard_map/ppermute | solution.py:46
  27.9 8.4 %collective-permute-start.10 = (bf16[256,256]{1,0:T(8,128)(2,1)S(1)}, bf16[256,256]{1,0:T(8,128)(2,1)S(1)}, u32[]{:S(2)}, u32[]{:S(2)}) collective-permute-start(bf16[256,256]{1,0:T(8,128)(2,1)S(1)} %get-tuple-element.96.refs_0_), channel_id=1, source_target_pairs={{0,8},{2,10},{4,12},{6,14},{8,0},{10,2},{12,4},{14,6},{16,24},{18,... | collective-permute-start | bytes 393224 | tf_op jit(solution)/shard_map/ppermute | solution.py:46
  28.8 7.5 %collective-permute-start.11 = (bf16[256,256]{1,0:T(8,128)(2,1)S(1)}, bf16[256,256]{1,0:T(8,128)(2,1)S(1)}, u32[]{:S(2)}, u32[]{:S(2)}) collective-permute-start(bf16[256,256]{1,0:T(8,128)(2,1)S(1)} %get-tuple-element.96.refs_0_), channel_id=1, source_target_pairs={{0,4},{2,6},{4,0},{6,2},{8,12},{10,14},{12,8},{14,10},{16,20},{18,... | collective-permute-start | bytes 393224 | tf_op jit(solution)/shard_map/ppermute | solution.py:46
  29.3 7.3 %collective-permute-start.12 = (bf16[256,256]{1,0:T(8,128)(2,1)S(1)}, bf16[256,256]{1,0:T(8,128)(2,1)S(1)}, u32[]{:S(2)}, u32[]{:S(2)}) collective-permute-start(bf16[256,256]{1,0:T(8,128)(2,1)S(1)} %get-tuple-element.97.refs_7_), channel_id=1, source_target_pairs={{0,4},{2,6},{4,0},{6,2},{8,12},{10,14},{12,8},{14,10},{16,20},{18,... | collective-permute-start | bytes 393224 | tf_op jit(solution)/shard_map/ppermute | solution.py:46
  36.6 14.7 %collective-permute-start.16 = (bf16[512,256]{1,0:T(8,128)(2,1)S(1)}, bf16[512,256]{1,0:T(8,128)(2,1)S(1)}, u32[]{:S(2)}, u32[]{:S(2)}) collective-permute-start(bf16[512,256]{1,0:T(8,128)(2,1)S(1)} %join.9), channel_id=1, source_target_pairs={{0,4},{2,6},{4,0},{6,2},{8,12},{10,14},{12,8},{14,10},{16,20},{18,... | collective-permute-start | bytes 786440 | tf_op jit(solution)/shard_map/ppermute | solution.py:46
  37.2 8.2 %collective-permute-start.17 = (bf16[256,256]{1,0:T(8,128)(2,1)S(1)}, bf16[256,256]{1,0:T(8,128)(2,1)S(1)}, u32[]{:S(2)}, u32[]{:S(2)}) collective-permute-start(bf16[256,256]{1,0:T(8,128)(2,1)S(1)} %get-tuple-element.97.refs_7_), channel_id=1, source_target_pairs={{0,24},{2,26},{4,28},{6,30},{8,16},{10,18},{12,20},{14,22},{16,8},... | collective-permute-start | bytes 393224 | tf_op jit(solution)/shard_map/ppermute | solution.py:46
  40.4 9.5 %collective-permute-start.18 = (bf16[256,256]{1,0:T(8,128)(2,1)S(1)}, bf16[256,256]{1,0:T(8,128)(2,1)S(1)}, u32[]{:S(2)}, u32[]{:S(2)}) collective-permute-start(bf16[256,256]{1,0:T(8,128)(2,1)S(1)} %get-tuple-element.97.refs_7_), channel_id=1, source_target_pairs={{0,8},{2,10},{4,12},{6,14},{8,0},{10,2},{12,4},{14,6},{16,24},{18,... | collective-permute-start | bytes 393224 | tf_op jit(solution)/shard_map/ppermute | solution.py:46
  41.2 10.1 %collective-permute-start.14 = (bf16[256,256]{1,0:T(8,128)(2,1)S(1)}, bf16[256,256]{1,0:T(8,128)(2,1)S(1)}, u32[]{:S(2)}, u32[]{:S(2)}) collective-permute-start(bf16[256,256]{1,0:T(8,128)(2,1)S(1)} %collective-permute-done.9.refs_0_.refs_2_), channel_id=1, source_target_pairs={{0,8},{2,10},{4,12},{6,14},{8,0},{10,2},{12,4},{14,6},{16,24},{18,... | collective-permute-start | bytes 393224 | tf_op jit(solution)/shard_map/ppermute | solution.py:46
  42.4 8.9 %collective-permute-start.15 = (bf16[256,256]{1,0:T(8,128)(2,1)S(1)}, bf16[256,256]{1,0:T(8,128)(2,1)S(1)}, u32[]{:S(2)}, u32[]{:S(2)}) collective-permute-start(bf16[256,256]{1,0:T(8,128)(2,1)S(1)} %collective-permute-done.11.refs_1_), channel_id=1, source_target_pairs={{0,16},{2,18},{4,20},{6,22},{8,24},{10,26},{12,28},{14,30},{16,0},... | collective-permute-start | bytes 393224 | tf_op jit(solution)/shard_map/ppermute | solution.py:46
  51.4 6.3 %collective-permute-start.19 = (bf16[2048,256]{1,0:T(8,128)(2,1)S(1)}, bf16[2048,256]{1,0:T(8,128)(2,1)S(1)}, u32[]{:S(2)}, u32[]{:S(2)}) collective-permute-start(bf16[2048,256]{1,0:T(8,128)(2,1)S(1)} %join.10), channel_id=1, source_target_pairs={{0,2},{2,0},{4,6},{6,4},{8,10},{10,8},{12,14},{14,12},{16,18},{18,... | collective-permute-start | bytes 3145736 | tf_op jit(solution)/shard_map/ppermute | solution.py:46
  51.5 13.5 %collective-permute-start.20 = (bf16[2048,256]{1,0:T(8,128)(2,1)S(1)}, bf16[2048,256]{1,0:T(8,128)(2,1)S(1)}, u32[]{:S(2)}, u32[]{:S(2)}) collective-permute-start(bf16[2048,256]{1,0:T(8,128)(2,1)S(1)} %get-tuple-element.113), channel_id=1, source_target_pairs={{0,2},{2,0},{4,6},{6,4},{8,10},{10,8},{12,14},{14,12},{16,18},{18,... | collective-permute-start | bytes 3145736 | tf_op jit(solution)/shard_map/ppermute | solution.py:46
  52.0 13.0 %collective-permute-start.25 = (bf16[512,256]{1,0:T(8,128)(2,1)S(1)}, bf16[512,256]{1,0:T(8,128)(2,1)S(1)}, u32[]{:S(2)}, u32[]{:S(2)}) collective-permute-start(bf16[512,256]{1,0:T(8,128)(2,1)S(1)} %join.11), channel_id=1, source_target_pairs={{0,4},{2,6},{4,0},{6,2},{8,12},{10,14},{12,8},{14,10},{16,20},{18,... | collective-permute-start | bytes 786440 | tf_op jit(solution)/shard_map/ppermute | solution.py:46
  53.5 6.0 %collective-permute-start.21 = (bf16[16,256]{1,0:T(8,128)(2,1)S(1)}, bf16[16,256]{1,0:T(8,128)(2,1)S(1)}, u32[]{:S(2)}, u32[]{:S(2)}) collective-permute-start(bf16[16,256]{1,0:T(8,128)(2,1)S(1)} %get-tuple-element.115.q_hub), channel_id=1, source_target_pairs={{0,1},{1,0},{2,3},{3,2},{4,5},{5,4},{6,7},{7,6},{8,9},{9,8},{10,11... | collective-permute-start | bytes 24584 | tf_op jit(solution)/shard_map/ppermute | solution.py:137
  55.0 8.6 %collective-permute-start.24 = (bf16[256,256]{1,0:T(8,128)(2,1)S(1)}, bf16[256,256]{1,0:T(8,128)(2,1)S(1)}, u32[]{:S(2)}, u32[]{:S(2)}) collective-permute-start(bf16[256,256]{1,0:T(8,128)(2,1)S(1)} %collective-permute-done.12.refs_8_), channel_id=1, source_target_pairs={{0,16},{2,18},{4,20},{6,22},{8,24},{10,26},{12,28},{14,30},{16,0},... | collective-permute-start | bytes 393224 | tf_op jit(solution)/shard_map/ppermute | solution.py:46
  57.6 7.4 %collective-permute-start.23 = (bf16[256,256]{1,0:T(8,128)(2,1)S(1)}, bf16[256,256]{1,0:T(8,128)(2,1)S(1)}, u32[]{:S(2)}, u32[]{:S(2)}) collective-permute-start(bf16[256,256]{1,0:T(8,128)(2,1)S(1)} %collective-permute-done.17.refs_0_.refs_9_), channel_id=1, source_target_pairs={{0,8},{2,10},{4,12},{6,14},{8,0},{10,2},{12,4},{14,6},{16,24},{18,... | collective-permute-start | bytes 393224 | tf_op jit(solution)/shard_map/ppermute | solution.py:46
  59.5 5.5 %collective-permute-start.22 = (bf16[256,256]{1,0:T(8,128)(2,1)S(1)}, bf16[256,256]{1,0:T(8,128)(2,1)S(1)}, u32[]{:S(2)}, u32[]{:S(2)}) collective-permute-start(bf16[256,256]{1,0:T(8,128)(2,1)S(1)} %get-tuple-element.116.q), channel_id=1, source_target_pairs={{0,2},{2,0},{4,6},{6,4},{8,10},{10,8},{12,14},{14,12},{16,18},{18,... | collective-permute-start | bytes 393224 | tf_op jit(solution)/shard_map/ppermute | solution.py:46
  68.3 4.3 %collective-permute-start.27 = (f32[64,256]{1,0:T(8,128)S(1)}, f32[64,256]{1,0:T(8,128)S(1)}, u32[]{:S(2)}, u32[]{:S(2)}) collective-permute-start(f32[64,256]{1,0:T(8,128)S(1)} %get-tuple-element.125), channel_id=1, source_target_pairs={{0,1},{1,0},{2,3},{3,2},{4,5},{5,4},{6,7},{7,6},{8,9},{9,8},{10,11... | collective-permute-start | bytes 196616 | tf_op jit(solution)/shard_map/ppermute | solution.py:52
  68.9 4.9 %collective-permute-start.28 = (f32[64,256]{1,0:T(8,128)S(1)}, f32[64,256]{1,0:T(8,128)S(1)}, u32[]{:S(2)}, u32[]{:S(2)}) collective-permute-start(f32[64,256]{1,0:T(8,128)S(1)} %get-tuple-element.126), channel_id=1, source_target_pairs={{0,4},{1,5},{2,6},{3,7},{4,0},{5,1},{6,2},{7,3},{8,12},{9,13},{10,... | collective-permute-start | bytes 196616 | tf_op jit(solution)/shard_map/ppermute | solution.py:52
  69.4 5.6 %collective-permute-start.29 = (f32[64,256]{1,0:T(8,128)S(1)}, f32[64,256]{1,0:T(8,128)S(1)}, u32[]{:S(2)}, u32[]{:S(2)}) collective-permute-start(f32[64,256]{1,0:T(8,128)S(1)} %get-tuple-element.127), channel_id=1, source_target_pairs={{0,5},{1,4},{2,7},{3,6},{4,1},{5,0},{6,3},{7,2},{8,13},{9,12},{10,... | collective-permute-start | bytes 196616 | tf_op jit(solution)/shard_map/ppermute | solution.py:52
  75.1 4.5 %collective-permute-start.30 = (f32[64,256]{1,0:T(8,128)S(1)}, f32[64,256]{1,0:T(8,128)S(1)}, u32[]{:S(2)}, u32[]{:S(2)}) collective-permute-start(f32[64,256]{1,0:T(8,128)S(1)} %add_xy.1.refs_0_), channel_id=1, source_target_pairs={{0,8},{2,10},{4,12},{6,14},{8,0},{10,2},{12,4},{14,6},{16,24},{18,... | collective-permute-start | bytes 196616 | tf_op jit(solution)/shard_map/ppermute | solution.py:46
  75.6 5.4 %collective-permute-start.31 = (f32[64,256]{1,0:T(8,128)S(1)}, f32[64,256]{1,0:T(8,128)S(1)}, u32[]{:S(2)}, u32[]{:S(2)}) collective-permute-start(f32[64,256]{1,0:T(8,128)S(1)} %add_xy.1.refs_0_), channel_id=1, source_target_pairs={{0,16},{2,18},{4,20},{6,22},{8,24},{10,26},{12,28},{14,30},{16,0},... | collective-permute-start | bytes 196616 | tf_op jit(solution)/shard_map/ppermute | solution.py:46
  76.1 6.5 %collective-permute-start.32 = (f32[64,256]{1,0:T(8,128)S(1)}, f32[64,256]{1,0:T(8,128)S(1)}, u32[]{:S(2)}, u32[]{:S(2)}) collective-permute-start(f32[64,256]{1,0:T(8,128)S(1)} %add_xy.1.refs_0_), channel_id=1, source_target_pairs={{0,24},{2,26},{4,28},{6,30},{8,16},{10,18},{12,20},{14,22},{16,8},... | collective-permute-start | bytes 196616 | tf_op jit(solution)/shard_map/ppermute | solution.py:46
  82.6 4.3 %collective-permute-start.33 = (f32[64,256]{1,0:T(8,128)S(1)}, f32[64,256]{1,0:T(8,128)S(1)}, u32[]{:S(2)}, u32[]{:S(2)}) collective-permute-start(f32[64,256]{1,0:T(8,128)S(1)} %add_z.1.refs_0_), channel_id=1, source_target_pairs={{0,1},{1,0},{2,3},{3,2},{4,5},{5,4},{6,7},{7,6},{8,9},{9,8},{10,11... | collective-permute-start | bytes 196616 | tf_op jit(solution)/shard_map/ppermute | solution.py:52
  85.2 5.2 %collective-permute-start.35 = (f32[64,256]{1,0:T(8,128)S(1)}, f32[64,256]{1,0:T(8,128)S(1)}, u32[]{:S(2)}, u32[]{:S(2)}) collective-permute-start(f32[64,256]{1,0:T(8,128)S(1)} %add_z.1.refs_0_), channel_id=1, source_target_pairs={{0,5},{1,4},{2,7},{3,6},{4,1},{5,0},{6,3},{7,2},{8,13},{9,12},{10,... | collective-permute-start | bytes 196616 | tf_op jit(solution)/shard_map/ppermute | solution.py:52
  (14 other events, 59.5 us)

commit v4 on v3

--- a/solution.py
+++ b/solution.py
@@ -75,12 +75,12 @@
     return [to_wide(own, 4 * k) for k in direct(lax.axis_size(WIDE) // 4)]
 
 
-def onward(over_x, over_z):
-    return [to_wide(over_z[0], 4), to_wide(over_x, 8), to_wide(join(*over_z), 2)]
+def onward(over_x, over_z, late=None):
+    return [to_wide(over_x, 8), to_wide(over_z[0] if late is None else late, 4), to_wide(join(*over_z), 2)]
 
 
 def place_of_block(z, x, nz):
-    place = jnp.where(z == 2, nz + x, x)
+    place = jnp.where(z == 2, nz + 1 - x, x)
     for at, k in enumerate(direct(nz), 2):
         place = jnp.where(z == k, at + x * nz, place)
     return place
@@ -141,7 +141,7 @@
         at.append(at[-1] + n)
     ints = jnp.concatenate([edge_rows, edge_hubs, low_labels, hub_labels]).reshape(1, at[-1] + hr)
 
-    def edge_tables(ints, feats, hub_rows, w, link, link_t, low_count, low_hot, hub_hot_out, feats_out, w_out, *parts):
+    def edge_tables(ints, feats, hub_rows, w, link, link_t, low_count, low_hot, feats_out, w_out, part):
         feats_out[...] = feats[...]
         w_out[...] = w[...]
         e_rows, e_hubs, labels = (ints[:, at[i] : at[i + 1]] for i in range(3))
@@ -160,17 +160,14 @@
         low_count[...] = jnp.broadcast_to(jnp.sum(links_t, axis=1, keepdims=True), (rows, LANES))
         sums = dot(hi, feats[...]) + dot(lo, feats[...])
         counts = jnp.broadcast_to(jnp.sum(links, axis=1, keepdims=True), (group, LANES))
-        for k, part in enumerate(parts):
-            part[:hr, :feat] = sums[k * hr : (k + 1) * hr]
-            part[:hr, feat:] = counts[k * hr : (k + 1) * hr]
-            part[hr:, :feat] = hub_rows[...].astype(F32)
-            part[hr:, feat:] = jnp.zeros((hr, LANES), F32)
+        part[:group, :feat] = sums
+        part[:group, feat:] = counts
+        part[group:, :feat] = hub_rows[...].astype(F32)
+        part[group:, feat:] = jnp.broadcast_to(labels_hub.astype(F32), (LANES, hr)).T
         hot = (lax.broadcasted_iota(jnp.int32, (classes, rows), 0) == labels).astype(F32)
         low_hot[...] = hot.T.astype(BF16)
-        hot = (lax.broadcasted_iota(jnp.int32, (classes, hr), 0) == labels_hub).astype(F32)
-        hub_hot_out[...] = hot.T.astype(BF16)
-
-    link, link_t, low_count, low_target, hub_target, near_feats, near_w, *parts1 = call(
+
+    link, link_t, low_count, low_target, near_feats, near_w, part1 = call(
         edge_tables,
         "edge_tables",
         [
@@ -178,17 +175,16 @@
             shaped(rows, 2 * group, BF16),
             shaped(rows, LANES, F32),
             shaped(rows, classes, BF16),
-            shaped(hr, classes, BF16),
             shaped(rows, feat, BF16),
             shaped(feat, units, BF16),
-        ]
-        + [shaped(2 * hr, pay, F32) for _ in range(n_hub)],
+            shaped(group + hr, pay, F32),
+        ],
         [ints, low_feats, hub_feats, w_first],
         traffic=4 << 20,
     )
 
-    feats_z, feats_x, parts1, low_count, near_feats, near_w = together(
-        feats_z, feats_x, parts1, low_count, near_feats, near_w
+    feats_z, feats_x, part1, low_count, near_feats, near_w = together(
+        feats_z, feats_x, part1, low_count, near_feats, near_w
     )
     feats_on = onward(feats_x, feats_z)
     feats_mate = [to_wide(join(near_feats, feats_x, *feats_z), 1)]
@@ -230,116 +226,126 @@
     )
 
 
+    def group_sum(own, got):
+        blocks = []
+        for m in range(n_hub):
+            block = own[m * hr : (m + 1) * hr]
+            for k, g in enumerate(got, 1):
+                block = block + g[(m ^ k) * hr : ((m ^ k) + 1) * hr]
+            blocks.append(block)
+        return jnp.concatenate(blocks, axis=0)
+
     def hub_first(w, own, *refs):
-        got, (hub_scale, agg, act) = refs[:-3], refs[-3:]
-        sums = own[:hr]
-        for g in got:
-            sums = sums + g[:hr]
+        got, (hub_scale, field, agg, act, target) = refs[:-5], refs[-5:]
+        sums = group_sum(own, got)
+        rest = jnp.concatenate([r[group:] for r in (own, *got)], axis=0)
         s = lax.rsqrt(1.0 + sums[:, feat : feat + 1])
-        hub_scale[...] = jnp.broadcast_to(s, (hr, LANES))
-        a = ((own[hr:, :feat] + sums[:, :feat]) * s).astype(BF16)
+        hub_scale[...] = jnp.broadcast_to(s, (group, LANES))
+        field[...] = rest[:, :feat].astype(BF16)
+        a = ((rest[:, :feat] + sums[:, :feat]) * s).astype(BF16)
         agg[...] = a
         act[...] = jnp.maximum(dot(a, w[...]), 0.0).astype(BF16)
+        labels = rest[:, feat : feat + 1].astype(jnp.int32)
+        target[...] = (lax.broadcasted_iota(jnp.int32, (group, classes), 1) == labels).astype(BF16)
 
     feats_on, feats_mate, scale, got1 = together(
-        feats_on, feats_mate, scale, [to_hub(parts1[k], k) for k in mates]
+        feats_on, feats_mate, scale, [to_hub(part1, k) for k in mates]
     )
     feats_mate.append(to_wide(join(*feats_on), 1))
     pieces1 = [near_feats, feats_x] + feats_z + feats_on + feats_mate
-    n_pieces = len(pieces1)
-    hub_scale, agg1_hub, h1_hub = call(
+    hub_scale, hub_field, agg1_hub, h1_hub, hub_target = call(
         hub_first,
         "hub_first",
-        [shaped(hr, LANES, F32), shaped(hr, feat, BF16), shaped(hr, units, BF16)],
-        [near_w, parts1[0]] + got1,
-    )
-    def low_first(adj, link, link_t, scale, w, act_hub, agg_hub, *refs):
-        pieces, refs = refs[:n_pieces], refs[n_pieces:]
-        hubs, (act_out, turned, own, *sends) = refs[:n_hub], refs[n_hub:]
-        around = jnp.concatenate([r[hr:, :feat] for r in hubs] * 2, axis=0).astype(BF16)
-        s = tile_sum(adj, pieces) + pieces[0][...].astype(F32) + dot(link_t[...], around)
+        [
+            shaped(group, LANES, F32),
+            shaped(group, feat, BF16),
+            shaped(group, feat, BF16),
+            shaped(group, units, BF16),
+            shaped(group, classes, BF16),
+        ],
+        [near_w, part1] + got1,
+    )
+
+    def low_near(adj, link_t, around, *refs):
+        pieces, out = refs[:-1], refs[-1]
+        around = jnp.concatenate([around[...], around[...]], axis=0)
+        out[...] = tile_sum(adj, pieces) + pieces[0][...].astype(F32) + dot(link_t[...], around)
+
+    (sum_near,) = call(
+        low_near, "low_near", [shaped(rows, feat, F32)], [adj, link_t, hub_field] + pieces1[:-1]
+    )
+
+    def low_first(adj, link, scale, w, sum_near, last, act_out, turned, sums):
+        s = sum_near[...] + dot(adj[:, 2 * half - last.shape[0] :], last[...])
         a = (s * scale[:, :1]).astype(BF16)
         act = jnp.maximum(dot(a, w[...]), 0.0).astype(BF16)
         act_out[...] = act
         turned[...] = a.T
-        sums = dot(link[:, :rows], act) + dot(link[:, rows:], act)
-        own[...] = sums[:hr]
-        for k, send in enumerate(sends, 1):
-            send[:hr] = act_hub[...].astype(F32)
-            send[hr : 2 * hr] = sums[k * hr : (k + 1) * hr]
-            send[2 * hr :] = agg_hub[...].astype(F32)
-
-    h1, agg1_t, own2, *sends2 = call(
+        sums[...] = dot(link[:, :rows], act) + dot(link[:, rows:], act)
+
+    h1, agg1_t, part2 = call(
         low_first,
         "low_first",
-        [shaped(rows, units, BF16), shaped(feat, rows, BF16), shaped(hr, units, F32)]
-        + [shaped(3 * hr, units, F32) for _ in mates],
-        [adj, link, link_t, scale, near_w, h1_hub, agg1_hub] + pieces1 + [parts1[0]] + got1,
+        [shaped(rows, units, BF16), shaped(feat, rows, BF16), shaped(group, units, F32)],
+        [adj, link, scale, near_w, sum_near, pieces1[-1]],
     )
 
     def hub_second(act, hub_scale, w, target, own, *refs):
         got, (logits, agg, dz, q) = refs[:-4], refs[-4:]
-        sums = own[...]
-        for g in got:
-            sums = sums + g[hr : 2 * hr]
         s = hub_scale[:, :1]
-        a = ((act[...].astype(F32) + sums) * s).astype(BF16)
-        agg[...] = a
+        a = ((act[...].astype(F32) + group_sum(own, got)) * s).astype(BF16)
         y = dot(a, w[...])
-        logits[...] = y
         d = ((y - target[...].astype(F32)) / total).astype(BF16)
-        dz[...] = d
+        agg[...] = a[:hr]
+        logits[...] = y[:hr]
+        dz[...] = d[:hr]
         q[...] = (dot_nt(d, w[...]) * s).astype(BF16)
 
-    h1_z, h1_x, agg1_x, got2 = together(
-        over_z(h1), to_wide(h1, 2), to_wide(agg1_t, 2), [to_hub(x, k) for k, x in enumerate(sends2, 1)]
-    )
+    h1_z, h1_x = together(over_z(h1), to_wide(h1, 2))
+    got2 = [to_hub(part2, k) for k in mates]
+    agg1_z, agg1_x, h1_z_late = together(over_z(agg1_t), to_wide(agg1_t, 2), h1_z[0])
+    h1_on = onward(h1_x, h1_z, h1_z_late)
+    h1_on, adj_t_give, got2 = together(h1_on, adj_t_give, got2)
     hub_logits, agg2_hub, dz2_hub, q_hub = call(
         hub_second,
         "hub_second",
-        [shaped(hr, classes, F32), shaped(hr, units, BF16), shaped(hr, classes, BF16), shaped(hr, units, BF16)],
-        [h1_hub, hub_scale, w_second, hub_target, own2] + got2,
-    )
-    h1_on, agg1_z, q_hub, adj_t_give = together(onward(h1_x, h1_z), over_z(agg1_t), q_hub, adj_t_give)
+        [shaped(hr, classes, F32), shaped(hr, units, BF16), shaped(hr, classes, BF16), shaped(group, units, BF16)],
+        [h1_hub, hub_scale, w_second, hub_target, part2] + got2,
+    )
     adj_t_mate = to_wide(adj_t_give, 1)
     agg1_on = onward(agg1_x, agg1_z)
     h1_mate = [to_wide(join(h1, h1_x, *h1_z, *h1_on), 1)]
-    q_hub_mates = [to_hub(q_hub, k) for k in mates]
     pieces2 = [h1, h1_x] + h1_z + h1_on
     turned = [agg1_t, agg1_x] + agg1_z + agg1_on
     n_own = len(pieces2)
 
-    def low_second(adj, link_t, scale, w, target, act_hub, agg_hub, dz_hub, *refs):
-        pieces, refs = refs[: n_own + 1], refs[n_own + 1 :]
-        got, (logits, grad, q_out) = refs[: n_hub - 1], refs[n_hub - 1 :]
-        around = jnp.concatenate([act_hub[...]] + [g[:hr].astype(BF16) for g in got], axis=0)
-        around = jnp.concatenate([around, around], axis=0)
+    def low_second(adj, link_t, scale, w, target, act_hub, *refs):
+        pieces, (logits, grad, q_out) = refs[: n_own + 1], refs[n_own + 1 :]
+        around = jnp.concatenate([act_hub[...], act_hub[...]], axis=0)
         s = tile_sum(adj, pieces) + pieces[0][...].astype(F32) + dot(link_t[...], around)
         a = (s * scale[:, :1]).astype(BF16)
         y = dot(a, w[...])
         logits[...] = y
         d = ((y - target[...].astype(F32)) / total).astype(BF16)
         q_out[...] = (dot_nt(d, w[...]) * scale[:, :1]).astype(BF16)
-        grad[...] = dot_tn(a, d) + dot_tn(agg_hub[...], dz_hub[...])
+        grad[...] = dot_tn(a, d)
 
     low_logits, grad_second, q_low = call(
         low_second,
         "low_second",
         [shaped(rows, classes, F32), shaped(units, classes, F32), shaped(rows, units, BF16)],
-        [adj, link_t, scale, w_second, low_target, h1_hub, agg2_hub, dz2_hub] + pieces2 + h1_mate + got2,
-    )
-
-    q_low, q_hub_mates = together(q_low, q_hub_mates)
+        [adj, link_t, scale, w_second, low_target, h1_hub] + pieces2 + h1_mate,
+    )
+
     q_mate = to_wide(q_low, 1)
 
-    def back_first(adj_t, adj_t_mate, link, link_t, q, q_mate, grad_second, act_hub, agg_hub, q_hub, *refs):
+    def back_first(
+        adj_t, adj_t_mate, link, link_t, q, q_mate, grad_low, act_hub, agg_hub, q_hub, agg2_hub, dz_hub, *refs
+    ):
         pieces, refs = refs[:n_own], refs[n_own:]
-        turned, refs = refs[:n_own], refs[n_own:]
-        got, refs = refs[: n_hub - 1], refs[n_hub - 1 :]
-        q_mates, (keep, give) = refs[: n_hub - 1], refs[n_hub - 1 :]
+        turned, (keep, give) = refs[:n_own], refs[n_own:]
         q_own = q[...]
-        around = jnp.concatenate([q_hub[...]] + [g[...] for g in q_mates], axis=0)
-        around = jnp.concatenate([around, around], axis=0)
+        around = jnp.concatenate([q_hub[...], q_hub[...]], axis=0)
         grad, at = None, 0
         for piece, agg in zip(pieces, turned):
             for n in range(0, piece.shape[0], rows):
@@ -351,30 +357,30 @@
                 grad = term if grad is None else grad + term
                 at += rows
         sums = dot(link[:, :rows], q_own) + dot(link[:, rows:], q_own)
-        for k in range(n_hub):
-            term = sums[k * hr : (k + 1) * hr]
-            act = act_hub[...].astype(F32) if k == 0 else got[k - 1][:hr]
-            agg = agg_hub[...] if k == 0 else got[k - 1][2 * hr :].astype(BF16)
-            if k == 0:
-                term = term + q_hub[...].astype(F32)
-            grad = grad + dot_tn(agg, jnp.where(act > 0.0, term, 0.0).astype(BF16))
+        mine = lax.broadcasted_iota(jnp.int32, (group, units), 0) < hr
+        sums = sums + jnp.where(mine, q_hub[...].astype(F32), 0.0)
+        sums = jnp.where(act_hub[...].astype(F32) > 0.0, sums, 0.0).astype(BF16)
+        grad = grad + dot_tn(agg_hub[...], sums)
+        grad_second = grad_low[...] + dot_tn(agg2_hub[...], dz_hub[...])
         core = lax.axis_index(WIDE) & 1
 
         @pl.when(core == 0)
         def _():
             keep[...] = grad
-            give[...] = grad_second[...]
+            give[...] = grad_second
 
         @pl.when(core == 1)
         def _():
-            keep[...] = grad_second[...]
+            keep[...] = grad_second
             give[...] = grad
 
     keep, give = call(
         back_first,
         "back_first",
         [shaped(units, classes, F32), shaped(units, classes, F32)],
-        [adj_t, adj_t_mate, link, link_t, q_low, q_mate, grad_second, h1_hub, agg1_hub, q_hub] + pieces2 + turned + got2 + q_hub_mates,
+        [adj_t, adj_t_mate, link, link_t, q_low, q_mate, grad_second, h1_hub, agg1_hub, q_hub, agg2_hub, dz2_hub]
+        + pieces2
+        + turned,
     )
     got = to_wide(give, 1)
 
@@ -392,16 +398,15 @@
             out[...] = keep[at] + got[at]
 
     shares = call(split, "split", [shaped(share, classes, F32) for _ in range(n_share)], [keep, got])
-    shares = [shares[0]] + [to_both(shares[k], *steps[k]) for k in range(1, n_share)]
+    shares = [to_both(shares[k], *steps[k]) for k in range(n_share - 1, 0, -1)] + [shares[0]]
 
     def add_up(*refs):
         refs[-1][...] = pairwise([r[...] for r in refs[:-1]])
 
     (mine,) = call(add_up, "add_xy", [shaped(share, classes, F32)], shares)
-    (mine,) = call(
-        add_up, "add_z", [shaped(share, classes, F32)], [mine] + [to_wide(mine, 4 * k) for k in range(1, nz)]
-    )
-    mine = [mine] + [to_both(mine, *steps[k]) for k in range(1, n_share)]
+    parts = [mine] + [to_wide(mine, 4 * k) for k in range(1, nz)]
+    (mine,) = call(add_up, "add_z", [shaped(share, classes, F32)], parts)
+    mine = [to_both(mine, *steps[k]) for k in range(n_share - 1, 0, -1)] + [mine]
     other = [to_wide(m, 1) for m in mine]
 
     def assemble(*refs):
@@ -411,7 +416,7 @@
 
         def write(mine_out, other_out):
             for k in range(n_share):
-                at = pl.ds(pl.multiple_of((me ^ k) * share, share), share)
+                at = pl.ds(pl.multiple_of((me ^ (n_share - 1 - k)) * share, share), share)
                 mine_out[at] = mine[k][...]
                 other_out[at] = other[k][...]
 

time: 92.7 us -> 87.2 us (0.941)
  starting transfers between devices: 40.6 us -> 36.1 us
    ppermute x31, starting transfers between devices: 28.9 us -> 25.9 us  [to_wide(): lax.ppermute(x, WIDE, [(i, i ^ k) for i in range(lax.axis_size(WIDE))])]
    ppermute x3 -> x2, starting transfers between devices: 4.57 us -> 3.04 us  [to_hub(): return lax.ppermute(x, HUB, [(i, i ^ k) for i in range(n_hub)])]
    ppermute x3 -> x2, waiting for transfers between devices: 2.58 us -> 2.4 us  [to_hub(): return lax.ppermute(x, HUB, [(i, i ^ k) for i in range(n_hub)])]
    pallas_call x17 -> x18, Pallas kernels: 11 us -> 10.9 us  [call(): pl.pallas_call(body, name=name, out_shape=outs, in_specs=[pl.BlockSpec(me...]
  transfers between devices with their start and end apart: 40 -> 39, of which waited for: 22 -> 22; matrix products, arithmetic and copies ran while one was open for 1% -> 1% of each run, Pallas kernels for 8% -> 9%
where the time goes in v4:
time: 87.2 us; the launch traced here: 87 us
  starting transfers between devices  36.1 us (41%)
  waiting for transfers between devices  35.2 us (40%)
  Pallas kernels  10.9 us (12%)
  local copies, waits for them, and re-layouts  3.19 us (4%)
    ppermute x31, waiting for transfers between devices, to_wide(): lax.ppermute(x, WIDE, [(i, i ^ k) for i in range(lax.axis_size(WIDE))])  26.1 us
    ppermute x31, starting transfers between devices, to_wide(): lax.ppermute(x, WIDE, [(i, i ^ k) for i in range(lax.axis_size(WIDE))])  25.9 us
    pallas_call x18, Pallas kernels, call(): pl.pallas_call(body, name=name, out_shape=outs, in_specs=[pl.BlockSpec(me...  10.9 us
    ppermute x6, starting transfers between devices, to_both(): return lax.ppermute(x, (WIDE, HUB), pairs)  7.11 us
    ppermute x6, waiting for transfers between devices, to_both(): return lax.ppermute(x, (WIDE, HUB), pairs)  6.75 us
    unnamed x12, local copies, waits for them, and re-layouts  3.19 us
    ppermute x2, starting transfers between devices, to_hub(): return lax.ppermute(x, HUB, [(i, i ^ k) for i in range(n_hub)])  3.04 us
    ppermute x2, waiting for transfers between devices, to_hub(): return lax.ppermute(x, HUB, [(i, i ^ k) for i in range(n_hub)])  2.4 us
  transfers between devices with their start and end apart: 39, of which 22 were waited for; matrix products, arithmetic and copies ran while one was open for 1% of the time, Pallas kernels for 9%

profile of v4, /device:TPU:0, one launch (start us, length us, event | category | flops | bytes accessed | tf_op | source)
XLA Modules:
  0.0 87.0 jit_solution(9876453160341968385)
XLA Ops:
  0.6 5.1 %collective-permute-start = (bf16[256,256]{1,0:T(8,128)(2,1)}, bf16[256,256]{1,0:T(8,128)(2,1)S(1)}, u32[]{:S(2)}, u32[]{:S(2)}) collective-permute-start(bf16[256,256]{1,0:T(8,128)(2,1)} %feats.1), channel_id=1, source_target_pairs={{0,24},{2,26},{4,28},{6,30},{8,16},{10,18},{12,20},{14,22},{16,8},... | collective-permute-start | bytes 393224 | tf_op jit(solution)/shard_map/ppermute | solution.py:46
  5.8 1.5 %collective-permute-start.2 = (bf16[256,256]{1,0:T(8,128)(2,1)}, bf16[256,256]{1,0:T(8,128)(2,1)S(1)}, u32[]{:S(2)}, u32[]{:S(2)}) collective-permute-start(bf16[256,256]{1,0:T(8,128)(2,1)} %feats.1), channel_id=1, source_target_pairs={{0,4},{2,6},{4,0},{6,2},{8,12},{10,14},{12,8},{14,10},{16,20},{18,... | collective-permute-start | bytes 393224 | tf_op jit(solution)/shard_map/ppermute | solution.py:46
  11.0 1.3 %collective-permute-done.1.refs_1_.refs_3_ = bf16[256,256]{1,0:T(8,128)(2,1)S(1)} collective-permute-done((bf16[256,256]{1,0:T(8,128)(2,1)}, bf16[256,256]{1,0:T(8,128)(2,1)S(1)}, u32[]{:S(2)}, u32[]{:S(2)}) %collective-permute-start.1) | collective-permute-done | bytes 131104 | tf_op jit(solution)/shard_map/ppermute | solution.py:46
  12.5 1.6 %collective-permute-start.5 = (bf16[512,256]{1,0:T(8,128)(2,1)S(1)}, bf16[512,256]{1,0:T(8,128)(2,1)S(1)}, u32[]{:S(2)}, u32[]{:S(2)}) collective-permute-start(bf16[512,256]{1,0:T(8,128)(2,1)S(1)} %join.6), channel_id=1, source_target_pairs={{0,4},{2,6},{4,0},{6,2},{8,12},{10,14},{12,8},{14,10},{16,20},{18,... | collective-permute-start | bytes 786440 | tf_op jit(solution)/shard_map/ppermute | solution.py:46
  14.6 1.8 %collective-permute-start.4 = (bf16[256,256]{1,0:T(8,128)(2,1)S(1)}, bf16[256,256]{1,0:T(8,128)(2,1)S(1)}, u32[]{:S(2)}, u32[]{:S(2)}) collective-permute-start(bf16[256,256]{1,0:T(8,128)(2,1)S(1)} %collective-permute-done.refs_0_.refs_2_), channel_id=1, source_target_pairs={{0,8},{2,10},{4,12},{6,14},{8,0},{10,2},{12,4},{14,6},{16,24},{18,... | collective-permute-start | bytes 393224 | tf_op jit(solution)/shard_map/ppermute | solution.py:46
  16.4 1.5 %collective-permute-start.7 = (f32[48,384]{1,0:T(8,128)S(1)}, f32[48,384]{1,0:T(8,128)S(1)}, u32[]{:S(2)}, u32[]{:S(2)}) collective-permute-start(f32[48,384]{1,0:T(8,128)S(1)} %get-tuple-element.75.own), channel_id=1, source_target_pairs={{0,1},{1,0},{2,3},{3,2},{4,5},{5,4},{6,7},{7,6},{8,9},{9,8},{10,11... | collective-permute-start | bytes 221192 | tf_op jit(solution)/shard_map/ppermute | solution.py:137
  18.6 3.8 %adjacency.1 = (bf16[256,4096]{1,0:T(8,128)(2,1)S(1)}, bf16[2048,256]{1,0:T(8,128)(2,1)S(1)}, bf16[2048,256]{1,0:T(8,128)(2,1)S(1)}, f32[256,128]{1,0:T(8,128)S(1)}) custom-call(bf16[32,128,128]{2,1,0:T(8,128)(2,1)S(1)} %copy-done, s32[2,16]{1,0:T(2,128)S(1)} %copy-done.5, f32[256,128]{1,0:T(8,128)S(1)} %get-tuple-element.67.low_count), custom_call_target="tpu_custom_call" | custom-call | bytes 14680064 | tf_op jit(solution)/shard_map/adjacency/pallas_call | solution.py:22
  24.4 1.1 %collective-permute-done.8.last = bf16[1024,256]{1,0:T(8,128)(2,1)S(1)} collective-permute-done((bf16[1024,256]{1,0:T(8,128)(2,1)S(1)}, bf16[1024,256]{1,0:T(8,128)(2,1)S(1)}, u32[]{:S(2)}, u32[]{:S(2)}) %collective-permute-start.8) | collective-permute-done | bytes 524320 | tf_op jit(solution)/shard_map/ppermute | solution.py:46
  26.1 2.7 %collective-permute-start.9 = (bf16[256,256]{1,0:T(8,128)(2,1)S(1)}, bf16[256,256]{1,0:T(8,128)(2,1)S(1)}, u32[]{:S(2)}, u32[]{:S(2)}) collective-permute-start(bf16[256,256]{1,0:T(8,128)(2,1)S(1)} %get-tuple-element.87.refs_0_), channel_id=1, source_target_pairs={{0,24},{2,26},{4,28},{6,30},{8,16},{10,18},{12,20},{14,22},{16,8},... | collective-permute-start | bytes 393224 | tf_op jit(solution)/shard_map/ppermute | solution.py:46
  29.4 1.1 %collective-permute-start.13 = (bf16[256,256]{1,0:T(8,128)(2,1)S(1)}, bf16[256,256]{1,0:T(8,128)(2,1)S(1)}, u32[]{:S(2)}, u32[]{:S(2)}) collective-permute-start(bf16[256,256]{1,0:T(8,128)(2,1)S(1)} %get-tuple-element.91.refs_7_), channel_id=1, source_target_pairs={{0,24},{2,26},{4,28},{6,30},{8,16},{10,18},{12,20},{14,22},{16,8},... | collective-permute-start | bytes 393224 | tf_op jit(solution)/shard_map/ppermute | solution.py:46
  30.5 1.1 %collective-permute-start.14 = (bf16[256,256]{1,0:T(8,128)(2,1)S(1)}, bf16[256,256]{1,0:T(8,128)(2,1)S(1)}, u32[]{:S(2)}, u32[]{:S(2)}) collective-permute-start(bf16[256,256]{1,0:T(8,128)(2,1)S(1)} %get-tuple-element.91.refs_7_), channel_id=1, source_target_pairs={{0,8},{2,10},{4,12},{6,14},{8,0},{10,2},{12,4},{14,6},{16,24},{18,... | collective-permute-start | bytes 393224 | tf_op jit(solution)/shard_map/ppermute | solution.py:46
  31.6 2.7 %collective-permute-done.9.refs_0_.refs_2_ = bf16[256,256]{1,0:T(8,128)(2,1)S(1)} collective-permute-done((bf16[256,256]{1,0:T(8,128)(2,1)S(1)}, bf16[256,256]{1,0:T(8,128)(2,1)S(1)}, u32[]{:S(2)}, u32[]{:S(2)}) %collective-permute-start.9) | collective-permute-done | bytes 131104 | tf_op jit(solution)/shard_map/ppermute | solution.py:46
  34.9 2.9 %collective-permute-done.10.refs_1_.refs_3_ = bf16[256,256]{1,0:T(8,128)(2,1)S(1)} collective-permute-done((bf16[256,256]{1,0:T(8,128)(2,1)S(1)}, bf16[256,256]{1,0:T(8,128)(2,1)S(1)}, u32[]{:S(2)}, u32[]{:S(2)}) %collective-permute-start.10) | collective-permute-done | bytes 131104 | tf_op jit(solution)/shard_map/ppermute | solution.py:46
  40.0 3.1 %collective-permute-done.14.refs_1_.refs_10_ = bf16[256,256]{1,0:T(8,128)(2,1)S(1)} collective-permute-done((bf16[256,256]{1,0:T(8,128)(2,1)S(1)}, bf16[256,256]{1,0:T(8,128)(2,1)S(1)}, u32[]{:S(2)}, u32[]{:S(2)}) %collective-permute-start.14) | collective-permute-done | bytes 131104 | tf_op jit(solution)/shard_map/ppermute | solution.py:46
  43.7 1.5 %collective-permute-start.18 = (f32[32,256]{1,0:T(8,128)S(1)}, f32[32,256]{1,0:T(8,128)S(1)}, u32[]{:S(2)}, u32[]{:S(2)}) collective-permute-start(f32[32,256]{1,0:T(8,128)S(1)} %get-tuple-element.94.own), channel_id=1, source_target_pairs={{0,1},{1,0},{2,3},{3,2},{4,5},{5,4},{6,7},{7,6},{8,9},{9,8},{10,11... | collective-permute-start | bytes 98312 | tf_op jit(solution)/shard_map/ppermute | solution.py:137
  45.2 2.4 %collective-permute-done.18.refs_0_ = f32[32,256]{1,0:T(8,128)S(1)} collective-permute-done((f32[32,256]{1,0:T(8,128)S(1)}, f32[32,256]{1,0:T(8,128)S(1)}, u32[]{:S(2)}, u32[]{:S(2)}) %collective-permute-start.18) | collective-permute-done | bytes 32800 | tf_op jit(solution)/shard_map/ppermute | solution.py:137
  47.6 1.8 %collective-permute-done.16.refs_5_ = bf16[256,256]{1,0:T(8,128)(2,1)S(1)} collective-permute-done((bf16[256,256]{1,0:T(8,128)(2,1)S(1)}, bf16[256,256]{1,0:T(8,128)(2,1)S(1)}, u32[]{:S(2)}, u32[]{:S(2)}) %collective-permute-start.16) | collective-permute-done | bytes 131104 | tf_op jit(solution)/shard_map/ppermute | solution.py:46
  50.6 1.6 %collective-permute-start.22 = (bf16[256,256]{1,0:T(8,128)(2,1)S(1)}, bf16[256,256]{1,0:T(8,128)(2,1)S(1)}, u32[]{:S(2)}, u32[]{:S(2)}) collective-permute-start(bf16[256,256]{1,0:T(8,128)(2,1)S(1)} %collective-permute-done.15.refs_8_), channel_id=1, source_target_pairs={{0,16},{2,18},{4,20},{6,22},{8,24},{10,26},{12,28},{14,30},{16,0},... | collective-permute-start | bytes 393224 | tf_op jit(solution)/shard_map/ppermute | solution.py:46
  52.2 1.7 %low_second.1 = (f32[256,256]{1,0:T(8,128)}, f32[256,256]{1,0:T(8,128)S(1)}, bf16[256,256]{1,0:T(8,128)(2,1)S(1)}) custom-call(bf16[256,4096]{1,0:T(8,128)(2,1)S(1)} %get-tuple-element.68.adj, bf16[256,64]{1,0:T(8,128)(2,1)S(1)} %get-tuple-element.69.link_t, f32[256,128]{1,0:T(8,128)S(1)} %get-tuple-element.76.scale, bf16[256,256]{1,0:T(8,128)(2,1)S(1)} %copy-done.1, ...), custom_call_target="tpu_custom_call" | custom-call | bytes 1048576 | tf_op jit(solution)/shard_map/low_second/pallas_call | solution.py:22
  54.9 4.7 %collective-permute-done.22.refs_11_ = bf16[256,256]{1,0:T(8,128)(2,1)S(1)} collective-permute-done((bf16[256,256]{1,0:T(8,128)(2,1)S(1)}, bf16[256,256]{1,0:T(8,128)(2,1)S(1)}, u32[]{:S(2)}, u32[]{:S(2)}) %collective-permute-start.22) | collective-permute-done | bytes 131104 | tf_op jit(solution)/shard_map/ppermute | solution.py:46
  59.6 1.6 %back_first.1 = (f32[256,256]{1,0:T(8,128)S(1)}, f32[256,256]{1,0:T(8,128)S(1)}) custom-call(bf16[2048,256]{1,0:T(8,128)(2,1)S(1)} %get-tuple-element.103.adj_t, bf16[2048,256]{1,0:T(8,128)(2,1)S(1)} %collective-permute-done.20.adj_t_mate, bf16[32,512]{1,0:T(8,128)(2,1)S(1)} %get-tuple-element.81.link, bf16[256,64]{1,0:T(8,128)(2,1)S(1)} %get-tuple-element.69.link_t, ...), custom_call_target="tpu_custom_call" | custom-call | bytes 1048576 | tf_op jit(solution)/shard_map/back_first/pallas_call | solution.py:22
  61.3 1.5 %collective-permute-done.25.got = f32[256,256]{1,0:T(8,128)S(1)} collective-permute-done((f32[256,256]{1,0:T(8,128)S(1)}, f32[256,256]{1,0:T(8,128)S(1)}, u32[]{:S(2)}, u32[]{:S(2)}) %collective-permute-start.25) | collective-permute-done | bytes 262176 | tf_op jit(solution)/shard_map/ppermute | solution.py:46
  62.8 2.6 %collective-permute-start.26 = (f32[64,256]{1,0:T(8,128)S(1)}, f32[64,256]{1,0:T(8,128)S(1)}, u32[]{:S(2)}, u32[]{:S(2)}) collective-permute-start(f32[64,256]{1,0:T(8,128)S(1)} %get-tuple-element.116), channel_id=1, source_target_pairs={{0,5},{1,4},{2,7},{3,6},{4,1},{5,0},{6,3},{7,2},{8,13},{9,12},{10,... | collective-permute-start | bytes 196616 | tf_op jit(solution)/shard_map/ppermute | solution.py:52
  66.4 2.0 %collective-permute-done.26.refs_0_ = f32[64,256]{1,0:T(8,128)S(1)} collective-permute-done((f32[64,256]{1,0:T(8,128)S(1)}, f32[64,256]{1,0:T(8,128)S(1)}, u32[]{:S(2)}, u32[]{:S(2)}) %collective-permute-start.26) | collective-permute-done | bytes 65568 | tf_op jit(solution)/shard_map/ppermute | solution.py:52
  68.3 1.3 %collective-permute-done.27.refs_1_ = f32[64,256]{1,0:T(8,128)S(1)} collective-permute-done((f32[64,256]{1,0:T(8,128)S(1)}, f32[64,256]{1,0:T(8,128)S(1)}, u32[]{:S(2)}, u32[]{:S(2)}) %collective-permute-start.27) | collective-permute-done | bytes 65568 | tf_op jit(solution)/shard_map/ppermute | solution.py:52
  70.2 2.0 %collective-permute-start.30 = (f32[64,256]{1,0:T(8,128)S(1)}, f32[64,256]{1,0:T(8,128)S(1)}, u32[]{:S(2)}, u32[]{:S(2)}) collective-permute-start(f32[64,256]{1,0:T(8,128)S(1)} %add_xy.1.refs_0_), channel_id=1, source_target_pairs={{0,16},{2,18},{4,20},{6,22},{8,24},{10,26},{12,28},{14,30},{16,0},... | collective-permute-start | bytes 196616 | tf_op jit(solution)/shard_map/ppermute | solution.py:46
  72.2 2.4 %collective-permute-start.31 = (f32[64,256]{1,0:T(8,128)S(1)}, f32[64,256]{1,0:T(8,128)S(1)}, u32[]{:S(2)}, u32[]{:S(2)}) collective-permute-start(f32[64,256]{1,0:T(8,128)S(1)} %add_xy.1.refs_0_), channel_id=1, source_target_pairs={{0,24},{2,26},{4,28},{6,30},{8,16},{10,18},{12,20},{14,22},{16,8},... | collective-permute-start | bytes 196616 | tf_op jit(solution)/shard_map/ppermute | solution.py:46
  74.6 1.6 %collective-permute-done.30.refs_2_ = f32[64,256]{1,0:T(8,128)S(1)} collective-permute-done((f32[64,256]{1,0:T(8,128)S(1)}, f32[64,256]{1,0:T(8,128)S(1)}, u32[]{:S(2)}, u32[]{:S(2)}) %collective-permute-start.30) | collective-permute-done | bytes 65568 | tf_op jit(solution)/shard_map/ppermute | solution.py:46
  76.2 2.1 %collective-permute-done.31.refs_3_ = f32[64,256]{1,0:T(8,128)S(1)} collective-permute-done((f32[64,256]{1,0:T(8,128)S(1)}, f32[64,256]{1,0:T(8,128)S(1)}, u32[]{:S(2)}, u32[]{:S(2)}) %collective-permute-start.31) | collective-permute-done | bytes 65568 | tf_op jit(solution)/shard_map/ppermute | solution.py:46
  78.3 1.9 %collective-permute-start.32 = (f32[64,256]{1,0:T(8,128)S(1)}, f32[64,256]{1,0:T(8,128)S(1)}, u32[]{:S(2)}, u32[]{:S(2)}) collective-permute-start(f32[64,256]{1,0:T(8,128)S(1)} %add_z.1.refs_3_), channel_id=1, source_target_pairs={{0,5},{1,4},{2,7},{3,6},{4,1},{5,0},{6,3},{7,2},{8,13},{9,12},{10,... | collective-permute-start | bytes 196616 | tf_op jit(solution)/shard_map/ppermute | solution.py:52
  80.6 1.3 %collective-permute-start.34 = (f32[64,256]{1,0:T(8,128)S(1)}, f32[64,256]{1,0:T(8,128)S(1)}, u32[]{:S(2)}, u32[]{:S(2)}) collective-permute-start(f32[64,256]{1,0:T(8,128)S(1)} %add_z.1.refs_3_), channel_id=1, source_target_pairs={{0,1},{1,0},{2,3},{3,2},{4,5},{5,4},{6,7},{7,6},{8,9},{9,8},{10,11... | collective-permute-start | bytes 196616 | tf_op jit(solution)/shard_map/ppermute | solution.py:52
  81.9 1.7 %collective-permute-done.32.refs_0_ = f32[64,256]{1,0:T(8,128)S(1)} collective-permute-done((f32[64,256]{1,0:T(8,128)S(1)}, f32[64,256]{1,0:T(8,128)S(1)}, u32[]{:S(2)}, u32[]{:S(2)}) %collective-permute-start.32) | collective-permute-done | bytes 65568 | tf_op jit(solution)/shard_map/ppermute | solution.py:52
  (78 shorter events, 19.1 us)
Async XLA Ops:
  0.6 10.4 %collective-permute-start = (bf16[256,256]{1,0:T(8,128)(2,1)}, bf16[256,256]{1,0:T(8,128)(2,1)S(1)}, u32[]{:S(2)}, u32[]{:S(2)}) collective-permute-start(bf16[256,256]{1,0:T(8,128)(2,1)} %feats.1), channel_id=1, source_target_pairs={{0,24},{2,26},{4,28},{6,30},{8,16},{10,18},{12,20},{14,22},{16,8},... | collective-permute-start | bytes 393224 | tf_op jit(solution)/shard_map/ppermute | solution.py:46
  5.8 6.6 %collective-permute-start.1 = (bf16[256,256]{1,0:T(8,128)(2,1)}, bf16[256,256]{1,0:T(8,128)(2,1)S(1)}, u32[]{:S(2)}, u32[]{:S(2)}) collective-permute-start(bf16[256,256]{1,0:T(8,128)(2,1)} %feats.1), channel_id=1, source_target_pairs={{0,8},{2,10},{4,12},{6,14},{8,0},{10,2},{12,4},{14,6},{16,24},{18,... | collective-permute-start | bytes 393224 | tf_op jit(solution)/shard_map/ppermute | solution.py:46
  5.8 6.6 %collective-permute-start.2 = (bf16[256,256]{1,0:T(8,128)(2,1)}, bf16[256,256]{1,0:T(8,128)(2,1)S(1)}, u32[]{:S(2)}, u32[]{:S(2)}) collective-permute-start(bf16[256,256]{1,0:T(8,128)(2,1)} %feats.1), channel_id=1, source_target_pairs={{0,4},{2,6},{4,0},{6,2},{8,12},{10,14},{12,8},{14,10},{16,20},{18,... | collective-permute-start | bytes 393224 | tf_op jit(solution)/shard_map/ppermute | solution.py:46
  12.4 11.0 %collective-permute-start.6 = (bf16[1024,256]{1,0:T(8,128)(2,1)S(1)}, bf16[1024,256]{1,0:T(8,128)(2,1)S(1)}, u32[]{:S(2)}, u32[]{:S(2)}) collective-permute-start(bf16[1024,256]{1,0:T(8,128)(2,1)S(1)} %join.7), channel_id=1, source_target_pairs={{0,2},{2,0},{4,6},{6,4},{8,10},{10,8},{12,14},{14,12},{16,18},{18,... | collective-permute-start | bytes 1572872 | tf_op jit(solution)/shard_map/ppermute | solution.py:46
  12.5 10.9 %collective-permute-start.5 = (bf16[512,256]{1,0:T(8,128)(2,1)S(1)}, bf16[512,256]{1,0:T(8,128)(2,1)S(1)}, u32[]{:S(2)}, u32[]{:S(2)}) collective-permute-start(bf16[512,256]{1,0:T(8,128)(2,1)S(1)} %join.6), channel_id=1, source_target_pairs={{0,4},{2,6},{4,0},{6,2},{8,12},{10,14},{12,8},{14,10},{16,20},{18,... | collective-permute-start | bytes 786440 | tf_op jit(solution)/shard_map/ppermute | solution.py:46
  14.1 9.4 %collective-permute-start.3 = (bf16[256,256]{1,0:T(8,128)(2,1)S(1)}, bf16[256,256]{1,0:T(8,128)(2,1)S(1)}, u32[]{:S(2)}, u32[]{:S(2)}) collective-permute-start(bf16[256,256]{1,0:T(8,128)(2,1)S(1)} %collective-permute-done.2.refs_1_), channel_id=1, source_target_pairs={{0,16},{2,18},{4,20},{6,22},{8,24},{10,26},{12,28},{14,30},{16,0},... | collective-permute-start | bytes 393224 | tf_op jit(solution)/shard_map/ppermute | solution.py:46
  14.6 8.9 %collective-permute-start.4 = (bf16[256,256]{1,0:T(8,128)(2,1)S(1)}, bf16[256,256]{1,0:T(8,128)(2,1)S(1)}, u32[]{:S(2)}, u32[]{:S(2)}) collective-permute-start(bf16[256,256]{1,0:T(8,128)(2,1)S(1)} %collective-permute-done.refs_0_.refs_2_), channel_id=1, source_target_pairs={{0,8},{2,10},{4,12},{6,14},{8,0},{10,2},{12,4},{14,6},{16,24},{18,... | collective-permute-start | bytes 393224 | tf_op jit(solution)/shard_map/ppermute | solution.py:46
  16.4 6.0 %collective-permute-start.7 = (f32[48,384]{1,0:T(8,128)S(1)}, f32[48,384]{1,0:T(8,128)S(1)}, u32[]{:S(2)}, u32[]{:S(2)}) collective-permute-start(f32[48,384]{1,0:T(8,128)S(1)} %get-tuple-element.75.own), channel_id=1, source_target_pairs={{0,1},{1,0},{2,3},{3,2},{4,5},{5,4},{6,7},{7,6},{8,9},{9,8},{10,11... | collective-permute-start | bytes 221192 | tf_op jit(solution)/shard_map/ppermute | solution.py:137
  26.1 8.2 %collective-permute-start.9 = (bf16[256,256]{1,0:T(8,128)(2,1)S(1)}, bf16[256,256]{1,0:T(8,128)(2,1)S(1)}, u32[]{:S(2)}, u32[]{:S(2)}) collective-permute-start(bf16[256,256]{1,0:T(8,128)(2,1)S(1)} %get-tuple-element.87.refs_0_), channel_id=1, source_target_pairs={{0,24},{2,26},{4,28},{6,30},{8,16},{10,18},{12,20},{14,22},{16,8},... | collective-permute-start | bytes 393224 | tf_op jit(solution)/shard_map/ppermute | solution.py:46
  28.8 8.9 %collective-permute-start.10 = (bf16[256,256]{1,0:T(8,128)(2,1)S(1)}, bf16[256,256]{1,0:T(8,128)(2,1)S(1)}, u32[]{:S(2)}, u32[]{:S(2)}) collective-permute-start(bf16[256,256]{1,0:T(8,128)(2,1)S(1)} %get-tuple-element.87.refs_0_), channel_id=1, source_target_pairs={{0,8},{2,10},{4,12},{6,14},{8,0},{10,2},{12,4},{14,6},{16,24},{18,... | collective-permute-start | bytes 393224 | tf_op jit(solution)/shard_map/ppermute | solution.py:46
  28.8 8.9 %collective-permute-start.11 = (bf16[256,256]{1,0:T(8,128)(2,1)S(1)}, bf16[256,256]{1,0:T(8,128)(2,1)S(1)}, u32[]{:S(2)}, u32[]{:S(2)}) collective-permute-start(bf16[256,256]{1,0:T(8,128)(2,1)S(1)} %get-tuple-element.87.refs_0_), channel_id=1, source_target_pairs={{0,4},{2,6},{4,0},{6,2},{8,12},{10,14},{12,8},{14,10},{16,20},{18,... | collective-permute-start | bytes 393224 | tf_op jit(solution)/shard_map/ppermute | solution.py:46
  29.4 10.6 %collective-permute-start.13 = (bf16[256,256]{1,0:T(8,128)(2,1)S(1)}, bf16[256,256]{1,0:T(8,128)(2,1)S(1)}, u32[]{:S(2)}, u32[]{:S(2)}) collective-permute-start(bf16[256,256]{1,0:T(8,128)(2,1)S(1)} %get-tuple-element.91.refs_7_), channel_id=1, source_target_pairs={{0,24},{2,26},{4,28},{6,30},{8,16},{10,18},{12,20},{14,22},{16,8},... | collective-permute-start | bytes 393224 | tf_op jit(solution)/shard_map/ppermute | solution.py:46
  30.5 12.6 %collective-permute-start.14 = (bf16[256,256]{1,0:T(8,128)(2,1)S(1)}, bf16[256,256]{1,0:T(8,128)(2,1)S(1)}, u32[]{:S(2)}, u32[]{:S(2)}) collective-permute-start(bf16[256,256]{1,0:T(8,128)(2,1)S(1)} %get-tuple-element.91.refs_7_), channel_id=1, source_target_pairs={{0,8},{2,10},{4,12},{6,14},{8,0},{10,2},{12,4},{14,6},{16,24},{18,... | collective-permute-start | bytes 393224 | tf_op jit(solution)/shard_map/ppermute | solution.py:46
  34.3 8.8 %collective-permute-start.15 = (bf16[256,256]{1,0:T(8,128)(2,1)S(1)}, bf16[256,256]{1,0:T(8,128)(2,1)S(1)}, u32[]{:S(2)}, u32[]{:S(2)}) collective-permute-start(bf16[256,256]{1,0:T(8,128)(2,1)S(1)} %get-tuple-element.91.refs_7_), channel_id=1, source_target_pairs={{0,4},{2,6},{4,0},{6,2},{8,12},{10,14},{12,8},{14,10},{16,20},{18,... | collective-permute-start | bytes 393224 | tf_op jit(solution)/shard_map/ppermute | solution.py:46
  37.8 11.7 %collective-permute-start.17 = (bf16[512,256]{1,0:T(8,128)(2,1)S(1)}, bf16[512,256]{1,0:T(8,128)(2,1)S(1)}, u32[]{:S(2)}, u32[]{:S(2)}) collective-permute-start(bf16[512,256]{1,0:T(8,128)(2,1)S(1)} %join.9), channel_id=1, source_target_pairs={{0,4},{2,6},{4,0},{6,2},{8,12},{10,14},{12,8},{14,10},{16,20},{18,... | collective-permute-start | bytes 786440 | tf_op jit(solution)/shard_map/ppermute | solution.py:46
  38.4 9.3 %collective-permute-start.12 = (bf16[256,256]{1,0:T(8,128)(2,1)S(1)}, bf16[256,256]{1,0:T(8,128)(2,1)S(1)}, u32[]{:S(2)}, u32[]{:S(2)}) collective-permute-start(bf16[256,256]{1,0:T(8,128)(2,1)S(1)} %collective-permute-done.11.refs_1_), channel_id=1, source_target_pairs={{0,16},{2,18},{4,20},{6,22},{8,24},{10,26},{12,28},{14,30},{16,0},... | collective-permute-start | bytes 393224 | tf_op jit(solution)/shard_map/ppermute | solution.py:46
  43.1 6.3 %collective-permute-start.16 = (bf16[256,256]{1,0:T(8,128)(2,1)S(1)}, bf16[256,256]{1,0:T(8,128)(2,1)S(1)}, u32[]{:S(2)}, u32[]{:S(2)}) collective-permute-start(bf16[256,256]{1,0:T(8,128)(2,1)S(1)} %collective-permute-done.9.refs_0_.refs_2_), channel_id=1, source_target_pairs={{0,8},{2,10},{4,12},{6,14},{8,0},{10,2},{12,4},{14,6},{16,24},{18,... | collective-permute-start | bytes 393224 | tf_op jit(solution)/shard_map/ppermute | solution.py:46
  43.7 3.9 %collective-permute-start.18 = (f32[32,256]{1,0:T(8,128)S(1)}, f32[32,256]{1,0:T(8,128)S(1)}, u32[]{:S(2)}, u32[]{:S(2)}) collective-permute-start(f32[32,256]{1,0:T(8,128)S(1)} %get-tuple-element.94.own), channel_id=1, source_target_pairs={{0,1},{1,0},{2,3},{3,2},{4,5},{5,4},{6,7},{7,6},{8,9},{9,8},{10,11... | collective-permute-start | bytes 98312 | tf_op jit(solution)/shard_map/ppermute | solution.py:137
  49.6 10.0 %collective-permute-start.20 = (bf16[2048,256]{1,0:T(8,128)(2,1)S(1)}, bf16[2048,256]{1,0:T(8,128)(2,1)S(1)}, u32[]{:S(2)}, u32[]{:S(2)}) collective-permute-start(bf16[2048,256]{1,0:T(8,128)(2,1)S(1)} %get-tuple-element.104), channel_id=1, source_target_pairs={{0,2},{2,0},{4,6},{6,4},{8,10},{10,8},{12,14},{14,12},{16,18},{18,... | collective-permute-start | bytes 3145736 | tf_op jit(solution)/shard_map/ppermute | solution.py:46
  50.1 9.5 %collective-permute-start.24 = (bf16[512,256]{1,0:T(8,128)(2,1)S(1)}, bf16[512,256]{1,0:T(8,128)(2,1)S(1)}, u32[]{:S(2)}, u32[]{:S(2)}) collective-permute-start(bf16[512,256]{1,0:T(8,128)(2,1)S(1)} %join.11), channel_id=1, source_target_pairs={{0,4},{2,6},{4,0},{6,2},{8,12},{10,14},{12,8},{14,10},{16,20},{18,... | collective-permute-start | bytes 786440 | tf_op jit(solution)/shard_map/ppermute | solution.py:46
  50.6 9.0 %collective-permute-start.23 = (bf16[256,256]{1,0:T(8,128)(2,1)S(1)}, bf16[256,256]{1,0:T(8,128)(2,1)S(1)}, u32[]{:S(2)}, u32[]{:S(2)}) collective-permute-start(bf16[256,256]{1,0:T(8,128)(2,1)S(1)} %collective-permute-done.13.refs_0_.refs_9_), channel_id=1, source_target_pairs={{0,8},{2,10},{4,12},{6,14},{8,0},{10,2},{12,4},{14,6},{16,24},{18,... | collective-permute-start | bytes 393224 | tf_op jit(solution)/shard_map/ppermute | solution.py:46
  50.6 9.0 %collective-permute-start.22 = (bf16[256,256]{1,0:T(8,128)(2,1)S(1)}, bf16[256,256]{1,0:T(8,128)(2,1)S(1)}, u32[]{:S(2)}, u32[]{:S(2)}) collective-permute-start(bf16[256,256]{1,0:T(8,128)(2,1)S(1)} %collective-permute-done.15.refs_8_), channel_id=1, source_target_pairs={{0,16},{2,18},{4,20},{6,22},{8,24},{10,26},{12,28},{14,30},{16,0},... | collective-permute-start | bytes 393224 | tf_op jit(solution)/shard_map/ppermute | solution.py:46
  53.9 5.7 %collective-permute-start.21 = (bf16[256,256]{1,0:T(8,128)(2,1)S(1)}, bf16[256,256]{1,0:T(8,128)(2,1)S(1)}, u32[]{:S(2)}, u32[]{:S(2)}) collective-permute-start(bf16[256,256]{1,0:T(8,128)(2,1)S(1)} %get-tuple-element.105.q), channel_id=1, source_target_pairs={{0,2},{2,0},{4,6},{6,4},{8,10},{10,8},{12,14},{14,12},{16,18},{18,... | collective-permute-start | bytes 393224 | tf_op jit(solution)/shard_map/ppermute | solution.py:46
  62.8 5.5 %collective-permute-start.26 = (f32[64,256]{1,0:T(8,128)S(1)}, f32[64,256]{1,0:T(8,128)S(1)}, u32[]{:S(2)}, u32[]{:S(2)}) collective-permute-start(f32[64,256]{1,0:T(8,128)S(1)} %get-tuple-element.116), channel_id=1, source_target_pairs={{0,5},{1,4},{2,7},{3,6},{4,1},{5,0},{6,3},{7,2},{8,13},{9,12},{10,... | collective-permute-start | bytes 196616 | tf_op jit(solution)/shard_map/ppermute | solution.py:52
  65.4 4.3 %collective-permute-start.27 = (f32[64,256]{1,0:T(8,128)S(1)}, f32[64,256]{1,0:T(8,128)S(1)}, u32[]{:S(2)}, u32[]{:S(2)}) collective-permute-start(f32[64,256]{1,0:T(8,128)S(1)} %get-tuple-element.117), channel_id=1, source_target_pairs={{0,4},{1,5},{2,6},{3,7},{4,0},{5,1},{6,2},{7,3},{8,12},{9,13},{10,... | collective-permute-start | bytes 196616 | tf_op jit(solution)/shard_map/ppermute | solution.py:52
  65.9 4.3 %collective-permute-start.28 = (f32[64,256]{1,0:T(8,128)S(1)}, f32[64,256]{1,0:T(8,128)S(1)}, u32[]{:S(2)}, u32[]{:S(2)}) collective-permute-start(f32[64,256]{1,0:T(8,128)S(1)} %get-tuple-element.118), channel_id=1, source_target_pairs={{0,1},{1,0},{2,3},{3,2},{4,5},{5,4},{6,7},{7,6},{8,9},{9,8},{10,11... | collective-permute-start | bytes 196616 | tf_op jit(solution)/shard_map/ppermute | solution.py:52
  70.1 4.5 %collective-permute-start.29 = (f32[64,256]{1,0:T(8,128)S(1)}, f32[64,256]{1,0:T(8,128)S(1)}, u32[]{:S(2)}, u32[]{:S(2)}) collective-permute-start(f32[64,256]{1,0:T(8,128)S(1)} %add_xy.1.refs_0_), channel_id=1, source_target_pairs={{0,8},{2,10},{4,12},{6,14},{8,0},{10,2},{12,4},{14,6},{16,24},{18,... | collective-permute-start | bytes 196616 | tf_op jit(solution)/shard_map/ppermute | solution.py:46
  70.2 6.0 %collective-permute-start.30 = (f32[64,256]{1,0:T(8,128)S(1)}, f32[64,256]{1,0:T(8,128)S(1)}, u32[]{:S(2)}, u32[]{:S(2)}) collective-permute-start(f32[64,256]{1,0:T(8,128)S(1)} %add_xy.1.refs_0_), channel_id=1, source_target_pairs={{0,16},{2,18},{4,20},{6,22},{8,24},{10,26},{12,28},{14,30},{16,0},... | collective-permute-start | bytes 196616 | tf_op jit(solution)/shard_map/ppermute | solution.py:46
  72.2 6.1 %collective-permute-start.31 = (f32[64,256]{1,0:T(8,128)S(1)}, f32[64,256]{1,0:T(8,128)S(1)}, u32[]{:S(2)}, u32[]{:S(2)}) collective-permute-start(f32[64,256]{1,0:T(8,128)S(1)} %add_xy.1.refs_0_), channel_id=1, source_target_pairs={{0,24},{2,26},{4,28},{6,30},{8,16},{10,18},{12,20},{14,22},{16,8},... | collective-permute-start | bytes 196616 | tf_op jit(solution)/shard_map/ppermute | solution.py:46
  78.3 5.2 %collective-permute-start.32 = (f32[64,256]{1,0:T(8,128)S(1)}, f32[64,256]{1,0:T(8,128)S(1)}, u32[]{:S(2)}, u32[]{:S(2)}) collective-permute-start(f32[64,256]{1,0:T(8,128)S(1)} %add_z.1.refs_3_), channel_id=1, source_target_pairs={{0,5},{1,4},{2,7},{3,6},{4,1},{5,0},{6,3},{7,2},{8,13},{9,12},{10,... | collective-permute-start | bytes 196616 | tf_op jit(solution)/shard_map/ppermute | solution.py:52
  80.2 4.3 %collective-permute-start.33 = (f32[64,256]{1,0:T(8,128)S(1)}, f32[64,256]{1,0:T(8,128)S(1)}, u32[]{:S(2)}, u32[]{:S(2)}) collective-permute-start(f32[64,256]{1,0:T(8,128)S(1)} %add_z.1.refs_3_), channel_id=1, source_target_pairs={{0,4},{1,5},{2,6},{3,7},{4,0},{5,1},{6,2},{7,3},{8,12},{9,13},{10,... | collective-permute-start | bytes 196616 | tf_op jit(solution)/shard_map/ppermute | solution.py:52
  80.6 4.3 %collective-permute-start.34 = (f32[64,256]{1,0:T(8,128)S(1)}, f32[64,256]{1,0:T(8,128)S(1)}, u32[]{:S(2)}, u32[]{:S(2)}) collective-permute-start(f32[64,256]{1,0:T(8,128)S(1)} %add_z.1.refs_3_), channel_id=1, source_target_pairs={{0,1},{1,0},{2,3},{3,2},{4,5},{5,4},{6,7},{7,6},{8,9},{9,8},{10,11... | collective-permute-start | bytes 196616 | tf_op jit(solution)/shard_map/ppermute | solution.py:52
  (13 other events, 60.0 us)

commit v5 on v4

--- a/solution.py
+++ b/solution.py
@@ -248,8 +248,8 @@
         labels = rest[:, feat : feat + 1].astype(jnp.int32)
         target[...] = (lax.broadcasted_iota(jnp.int32, (group, classes), 1) == labels).astype(BF16)
 
-    feats_on, feats_mate, scale, got1 = together(
-        feats_on, feats_mate, scale, [to_hub(part1, k) for k in mates]
+    feats_on, scale, got1 = together(
+        feats_on, scale, [to_hub(part1, k) for k in mates]
     )
     feats_mate.append(to_wide(join(*feats_on), 1))
     pieces1 = [near_feats, feats_x] + feats_z + feats_on + feats_mate
@@ -302,8 +302,9 @@
         q[...] = (dot_nt(d, w[...]) * s).astype(BF16)
 
     h1_z, h1_x = together(over_z(h1), to_wide(h1, 2))
-    got2 = [to_hub(part2, k) for k in mates]
     agg1_z, agg1_x, h1_z_late = together(over_z(agg1_t), to_wide(agg1_t, 2), h1_z[0])
+    part2_late, _ = together(part2, agg1_x)
+    got2 = [to_hub(part2_late, k) for k in mates]
     h1_on = onward(h1_x, h1_z, h1_z_late)
     h1_on, adj_t_give, got2 = together(h1_on, adj_t_give, got2)
     hub_logits, agg2_hub, dz2_hub, q_hub = call(
@@ -404,7 +405,7 @@
         refs[-1][...] = pairwise([r[...] for r in refs[:-1]])
 
     (mine,) = call(add_up, "add_xy", [shaped(share, classes, F32)], shares)
-    parts = [mine] + [to_wide(mine, 4 * k) for k in range(1, nz)]
+    parts = [to_wide(mine, 4 * k) for k in range(2, nz)] + [mine, to_wide(mine, 4)]
     (mine,) = call(add_up, "add_z", [shaped(share, classes, F32)], parts)
     mine = [to_both(mine, *steps[k]) for k in range(n_share - 1, 0, -1)] + [mine]
     other = [to_wide(m, 1) for m in mine]

time: 87.2 us -> 85.4 us (0.979)
  waiting for transfers between devices: 35.2 us -> 32.4 us
  starting transfers between devices: 36.1 us -> 37 us
    ppermute x31, waiting for transfers between devices: 26.1 us -> 22.9 us  [to_wide(): lax.ppermute(x, WIDE, [(i, i ^ k) for i in range(lax.axis_size(WIDE))])]
    ppermute x31, starting transfers between devices: 25.9 us -> 27.4 us  [to_wide(): lax.ppermute(x, WIDE, [(i, i ^ k) for i in range(lax.axis_size(WIDE))])]
  transfers between devices with their start and end apart: 39 -> 39, of which waited for: 22 -> 19; matrix products, arithmetic and copies ran while one was open for 1% -> 1% of each run, Pallas kernels for 9% -> 9%
where the time goes in v5:
time: 85.4 us; the launch traced here: 85.1 us
  starting transfers between devices  37 us (43%)
  waiting for transfers between devices  32.4 us (38%)
  Pallas kernels  10.9 us (13%)
  local copies, waits for them, and re-layouts  3.19 us (4%)
    ppermute x31, starting transfers between devices, to_wide(): lax.ppermute(x, WIDE, [(i, i ^ k) for i in range(lax.axis_size(WIDE))])  27.4 us
    ppermute x31, waiting for transfers between devices, to_wide(): lax.ppermute(x, WIDE, [(i, i ^ k) for i in range(lax.axis_size(WIDE))])  22.9 us
    pallas_call x18, Pallas kernels, call(): pl.pallas_call(body, name=name, out_shape=outs, in_specs=[pl.BlockSpec(me...  10.9 us
    ppermute x6, starting transfers between devices, to_both(): return lax.ppermute(x, (WIDE, HUB), pairs)  7.11 us
    ppermute x6, waiting for transfers between devices, to_both(): return lax.ppermute(x, (WIDE, HUB), pairs)  6.67 us
    unnamed x12, local copies, waits for them, and re-layouts  3.18 us
    ppermute x2, waiting for transfers between devices, to_hub(): return lax.ppermute(x, HUB, [(i, i ^ k) for i in range(n_hub)])  2.89 us
    ppermute x2, starting transfers between devices, to_hub(): return lax.ppermute(x, HUB, [(i, i ^ k) for i in range(n_hub)])  2.55 us
  transfers between devices with their start and end apart: 39, of which 19 were waited for; matrix products, arithmetic and copies ran while one was open for 1% of the time, Pallas kernels for 9%

profile of v5, /device:TPU:0, one launch (start us, length us, event | category | flops | bytes accessed | tf_op | source)
XLA Modules:
  0.0 85.1 jit_solution(6780570338237026753)
XLA Ops:
  0.6 5.1 %collective-permute-start = (bf16[256,256]{1,0:T(8,128)(2,1)}, bf16[256,256]{1,0:T(8,128)(2,1)S(1)}, u32[]{:S(2)}, u32[]{:S(2)}) collective-permute-start(bf16[256,256]{1,0:T(8,128)(2,1)} %feats.1), channel_id=1, source_target_pairs={{0,24},{2,26},{4,28},{6,30},{8,16},{10,18},{12,20},{14,22},{16,8},... | collective-permute-start | bytes 393224 | tf_op jit(solution)/shard_map/ppermute | solution.py:46
  5.8 1.5 %collective-permute-start.2 = (bf16[256,256]{1,0:T(8,128)(2,1)}, bf16[256,256]{1,0:T(8,128)(2,1)S(1)}, u32[]{:S(2)}, u32[]{:S(2)}) collective-permute-start(bf16[256,256]{1,0:T(8,128)(2,1)} %feats.1), channel_id=1, source_target_pairs={{0,4},{2,6},{4,0},{6,2},{8,12},{10,14},{12,8},{14,10},{16,20},{18,... | collective-permute-start | bytes 393224 | tf_op jit(solution)/shard_map/ppermute | solution.py:46
  11.0 1.3 %collective-permute-done.1.refs_1_.refs_3_ = bf16[256,256]{1,0:T(8,128)(2,1)S(1)} collective-permute-done((bf16[256,256]{1,0:T(8,128)(2,1)}, bf16[256,256]{1,0:T(8,128)(2,1)S(1)}, u32[]{:S(2)}, u32[]{:S(2)}) %collective-permute-start.1) | collective-permute-done | bytes 131104 | tf_op jit(solution)/shard_map/ppermute | solution.py:46
  12.4 1.6 %collective-permute-start.5 = (bf16[512,256]{1,0:T(8,128)(2,1)S(1)}, bf16[512,256]{1,0:T(8,128)(2,1)S(1)}, u32[]{:S(2)}, u32[]{:S(2)}) collective-permute-start(bf16[512,256]{1,0:T(8,128)(2,1)S(1)} %join.6), channel_id=1, source_target_pairs={{0,4},{2,6},{4,0},{6,2},{8,12},{10,14},{12,8},{14,10},{16,20},{18,... | collective-permute-start | bytes 786440 | tf_op jit(solution)/shard_map/ppermute | solution.py:46
  14.5 1.8 %collective-permute-start.4 = (bf16[256,256]{1,0:T(8,128)(2,1)S(1)}, bf16[256,256]{1,0:T(8,128)(2,1)S(1)}, u32[]{:S(2)}, u32[]{:S(2)}) collective-permute-start(bf16[256,256]{1,0:T(8,128)(2,1)S(1)} %collective-permute-done.refs_0_.refs_2_), channel_id=1, source_target_pairs={{0,8},{2,10},{4,12},{6,14},{8,0},{10,2},{12,4},{14,6},{16,24},{18,... | collective-permute-start | bytes 393224 | tf_op jit(solution)/shard_map/ppermute | solution.py:46
  16.3 1.5 %collective-permute-start.6 = (f32[48,384]{1,0:T(8,128)S(1)}, f32[48,384]{1,0:T(8,128)S(1)}, u32[]{:S(2)}, u32[]{:S(2)}) collective-permute-start(f32[48,384]{1,0:T(8,128)S(1)} %get-tuple-element.74.own), channel_id=1, source_target_pairs={{0,1},{1,0},{2,3},{3,2},{4,5},{5,4},{6,7},{7,6},{8,9},{9,8},{10,11... | collective-permute-start | bytes 221192 | tf_op jit(solution)/shard_map/ppermute | solution.py:137
  18.6 3.8 %adjacency.1 = (bf16[256,4096]{1,0:T(8,128)(2,1)S(1)}, bf16[2048,256]{1,0:T(8,128)(2,1)S(1)}, bf16[2048,256]{1,0:T(8,128)(2,1)S(1)}, f32[256,128]{1,0:T(8,128)S(1)}) custom-call(bf16[32,128,128]{2,1,0:T(8,128)(2,1)S(1)} %copy-done, s32[2,16]{1,0:T(2,128)S(1)} %copy-done.5, f32[256,128]{1,0:T(8,128)S(1)} %get-tuple-element.67.low_count), custom_call_target="tpu_custom_call" | custom-call | bytes 14680064 | tf_op jit(solution)/shard_map/adjacency/pallas_call | solution.py:22
  25.2 2.1 %collective-permute-start.9 = (bf16[256,256]{1,0:T(8,128)(2,1)S(1)}, bf16[256,256]{1,0:T(8,128)(2,1)S(1)}, u32[]{:S(2)}, u32[]{:S(2)}) collective-permute-start(bf16[256,256]{1,0:T(8,128)(2,1)S(1)} %get-tuple-element.86.refs_0_), channel_id=1, source_target_pairs={{0,24},{2,26},{4,28},{6,30},{8,16},{10,18},{12,20},{14,22},{16,8},... | collective-permute-start | bytes 393224 | tf_op jit(solution)/shard_map/ppermute | solution.py:46
  28.6 1.0 %collective-permute-start.13 = (bf16[256,256]{1,0:T(8,128)(2,1)S(1)}, bf16[256,256]{1,0:T(8,128)(2,1)S(1)}, u32[]{:S(2)}, u32[]{:S(2)}) collective-permute-start(bf16[256,256]{1,0:T(8,128)(2,1)S(1)} %get-tuple-element.90.refs_7_), channel_id=1, source_target_pairs={{0,24},{2,26},{4,28},{6,30},{8,16},{10,18},{12,20},{14,22},{16,8},... | collective-permute-start | bytes 393224 | tf_op jit(solution)/shard_map/ppermute | solution.py:46
  29.6 1.1 %collective-permute-start.14 = (bf16[256,256]{1,0:T(8,128)(2,1)S(1)}, bf16[256,256]{1,0:T(8,128)(2,1)S(1)}, u32[]{:S(2)}, u32[]{:S(2)}) collective-permute-start(bf16[256,256]{1,0:T(8,128)(2,1)S(1)} %get-tuple-element.90.refs_7_), channel_id=1, source_target_pairs={{0,8},{2,10},{4,12},{6,14},{8,0},{10,2},{12,4},{14,6},{16,24},{18,... | collective-permute-start | bytes 393224 | tf_op jit(solution)/shard_map/ppermute | solution.py:46
  30.8 2.7 %collective-permute-done.9.refs_0_.refs_2_ = bf16[256,256]{1,0:T(8,128)(2,1)S(1)} collective-permute-done((bf16[256,256]{1,0:T(8,128)(2,1)S(1)}, bf16[256,256]{1,0:T(8,128)(2,1)S(1)}, u32[]{:S(2)}, u32[]{:S(2)}) %collective-permute-start.9) | collective-permute-done | bytes 131104 | tf_op jit(solution)/shard_map/ppermute | solution.py:46
  34.0 2.4 %collective-permute-done.10.refs_1_.refs_3_ = bf16[256,256]{1,0:T(8,128)(2,1)S(1)} collective-permute-done((bf16[256,256]{1,0:T(8,128)(2,1)S(1)}, bf16[256,256]{1,0:T(8,128)(2,1)S(1)}, u32[]{:S(2)}, u32[]{:S(2)}) %collective-permute-start.10) | collective-permute-done | bytes 131104 | tf_op jit(solution)/shard_map/ppermute | solution.py:46
  37.0 2.1 %collective-permute-start.12 = (bf16[256,256]{1,0:T(8,128)(2,1)S(1)}, bf16[256,256]{1,0:T(8,128)(2,1)S(1)}, u32[]{:S(2)}, u32[]{:S(2)}) collective-permute-start(bf16[256,256]{1,0:T(8,128)(2,1)S(1)} %collective-permute-done.11.refs_1_), channel_id=1, source_target_pairs={{0,16},{2,18},{4,20},{6,22},{8,24},{10,26},{12,28},{14,30},{16,0},... | collective-permute-start | bytes 393224 | tf_op jit(solution)/shard_map/ppermute | solution.py:46
  39.1 3.6 %collective-permute-done.14.refs_1_.refs_10_ = bf16[256,256]{1,0:T(8,128)(2,1)S(1)} collective-permute-done((bf16[256,256]{1,0:T(8,128)(2,1)S(1)}, bf16[256,256]{1,0:T(8,128)(2,1)S(1)}, u32[]{:S(2)}, u32[]{:S(2)}) %collective-permute-start.14) | collective-permute-done | bytes 131104 | tf_op jit(solution)/shard_map/ppermute | solution.py:46
  42.7 1.0 %collective-permute-start.18 = (f32[32,256]{1,0:T(8,128)S(1)}, f32[32,256]{1,0:T(8,128)S(1)}, u32[]{:S(2)}, u32[]{:S(2)}) collective-permute-start(f32[32,256]{1,0:T(8,128)S(1)} %get-tuple-element.95.own), channel_id=1, source_target_pairs={{0,1},{1,0},{2,3},{3,2},{4,5},{5,4},{6,7},{7,6},{8,9},{9,8},{10,11... | collective-permute-start | bytes 98312 | tf_op jit(solution)/shard_map/ppermute | solution.py:137
  43.8 2.9 %collective-permute-done.18.refs_0_ = f32[32,256]{1,0:T(8,128)S(1)} collective-permute-done((f32[32,256]{1,0:T(8,128)S(1)}, f32[32,256]{1,0:T(8,128)S(1)}, u32[]{:S(2)}, u32[]{:S(2)}) %collective-permute-start.18) | collective-permute-done | bytes 32800 | tf_op jit(solution)/shard_map/ppermute | solution.py:137
  46.7 1.8 %collective-permute-done.16.refs_5_ = bf16[256,256]{1,0:T(8,128)(2,1)S(1)} collective-permute-done((bf16[256,256]{1,0:T(8,128)(2,1)S(1)}, bf16[256,256]{1,0:T(8,128)(2,1)S(1)}, u32[]{:S(2)}, u32[]{:S(2)}) %collective-permute-start.16) | collective-permute-done | bytes 131104 | tf_op jit(solution)/shard_map/ppermute | solution.py:46
  49.1 1.2 %collective-permute-start.24 = (bf16[512,256]{1,0:T(8,128)(2,1)S(1)}, bf16[512,256]{1,0:T(8,128)(2,1)S(1)}, u32[]{:S(2)}, u32[]{:S(2)}) collective-permute-start(bf16[512,256]{1,0:T(8,128)(2,1)S(1)} %join.11), channel_id=1, source_target_pairs={{0,4},{2,6},{4,0},{6,2},{8,12},{10,14},{12,8},{14,10},{16,20},{18,... | collective-permute-start | bytes 786440 | tf_op jit(solution)/shard_map/ppermute | solution.py:46
  50.3 2.0 %collective-permute-start.23 = (bf16[256,256]{1,0:T(8,128)(2,1)S(1)}, bf16[256,256]{1,0:T(8,128)(2,1)S(1)}, u32[]{:S(2)}, u32[]{:S(2)}) collective-permute-start(bf16[256,256]{1,0:T(8,128)(2,1)S(1)} %collective-permute-done.13.refs_0_.refs_9_), channel_id=1, source_target_pairs={{0,8},{2,10},{4,12},{6,14},{8,0},{10,2},{12,4},{14,6},{16,24},{18,... | collective-permute-start | bytes 393224 | tf_op jit(solution)/shard_map/ppermute | solution.py:46
  52.3 1.7 %low_second.1 = (f32[256,256]{1,0:T(8,128)}, f32[256,256]{1,0:T(8,128)S(1)}, bf16[256,256]{1,0:T(8,128)(2,1)S(1)}) custom-call(bf16[256,4096]{1,0:T(8,128)(2,1)S(1)} %get-tuple-element.68.adj, bf16[256,64]{1,0:T(8,128)(2,1)S(1)} %get-tuple-element.69.link_t, f32[256,128]{1,0:T(8,128)S(1)} %get-tuple-element.75.scale, bf16[256,256]{1,0:T(8,128)(2,1)S(1)} %copy-done.1, ...), custom_call_target="tpu_custom_call" | custom-call | bytes 1048576 | tf_op jit(solution)/shard_map/low_second/pallas_call | solution.py:22
  54.8 3.5 %collective-permute-done.22.refs_11_ = bf16[256,256]{1,0:T(8,128)(2,1)S(1)} collective-permute-done((bf16[256,256]{1,0:T(8,128)(2,1)S(1)}, bf16[256,256]{1,0:T(8,128)(2,1)S(1)}, u32[]{:S(2)}, u32[]{:S(2)}) %collective-permute-start.22) | collective-permute-done | bytes 131104 | tf_op jit(solution)/shard_map/ppermute | solution.py:46
  58.3 1.6 %back_first.1 = (f32[256,256]{1,0:T(8,128)S(1)}, f32[256,256]{1,0:T(8,128)S(1)}) custom-call(bf16[2048,256]{1,0:T(8,128)(2,1)S(1)} %get-tuple-element.104.adj_t, bf16[2048,256]{1,0:T(8,128)(2,1)S(1)} %collective-permute-done.20.adj_t_mate, bf16[32,512]{1,0:T(8,128)(2,1)S(1)} %get-tuple-element.80.link, bf16[256,64]{1,0:T(8,128)(2,1)S(1)} %get-tuple-element.69.link_t, ...), custom_call_target="tpu_custom_call" | custom-call | bytes 1048576 | tf_op jit(solution)/shard_map/back_first/pallas_call | solution.py:22
  60.0 1.5 %collective-permute-done.25.got = f32[256,256]{1,0:T(8,128)S(1)} collective-permute-done((f32[256,256]{1,0:T(8,128)S(1)}, f32[256,256]{1,0:T(8,128)S(1)}, u32[]{:S(2)}, u32[]{:S(2)}) %collective-permute-start.25) | collective-permute-done | bytes 262176 | tf_op jit(solution)/shard_map/ppermute | solution.py:46
  61.6 2.1 %collective-permute-start.26 = (f32[64,256]{1,0:T(8,128)S(1)}, f32[64,256]{1,0:T(8,128)S(1)}, u32[]{:S(2)}, u32[]{:S(2)}) collective-permute-start(f32[64,256]{1,0:T(8,128)S(1)} %get-tuple-element.116), channel_id=1, source_target_pairs={{0,5},{1,4},{2,7},{3,6},{4,1},{5,0},{6,3},{7,2},{8,13},{9,12},{10,... | collective-permute-start | bytes 196616 | tf_op jit(solution)/shard_map/ppermute | solution.py:52
  64.2 0.9 %collective-permute-start.28 = (f32[64,256]{1,0:T(8,128)S(1)}, f32[64,256]{1,0:T(8,128)S(1)}, u32[]{:S(2)}, u32[]{:S(2)}) collective-permute-start(f32[64,256]{1,0:T(8,128)S(1)} %get-tuple-element.118), channel_id=1, source_target_pairs={{0,1},{1,0},{2,3},{3,2},{4,5},{5,4},{6,7},{7,6},{8,9},{9,8},{10,11... | collective-permute-start | bytes 196616 | tf_op jit(solution)/shard_map/ppermute | solution.py:52
  65.1 2.1 %collective-permute-done.26.refs_0_ = f32[64,256]{1,0:T(8,128)S(1)} collective-permute-done((f32[64,256]{1,0:T(8,128)S(1)}, f32[64,256]{1,0:T(8,128)S(1)}, u32[]{:S(2)}, u32[]{:S(2)}) %collective-permute-start.26) | collective-permute-done | bytes 65568 | tf_op jit(solution)/shard_map/ppermute | solution.py:52
  68.9 2.0 %collective-permute-start.30 = (f32[64,256]{1,0:T(8,128)S(1)}, f32[64,256]{1,0:T(8,128)S(1)}, u32[]{:S(2)}, u32[]{:S(2)}) collective-permute-start(f32[64,256]{1,0:T(8,128)S(1)} %add_xy.1.refs_2_), channel_id=1, source_target_pairs={{0,24},{2,26},{4,28},{6,30},{8,16},{10,18},{12,20},{14,22},{16,8},... | collective-permute-start | bytes 196616 | tf_op jit(solution)/shard_map/ppermute | solution.py:46
  70.8 1.2 %collective-permute-start.31 = (f32[64,256]{1,0:T(8,128)S(1)}, f32[64,256]{1,0:T(8,128)S(1)}, u32[]{:S(2)}, u32[]{:S(2)}) collective-permute-start(f32[64,256]{1,0:T(8,128)S(1)} %add_xy.1.refs_2_), channel_id=1, source_target_pairs={{0,8},{2,10},{4,12},{6,14},{8,0},{10,2},{12,4},{14,6},{16,24},{18,... | collective-permute-start | bytes 196616 | tf_op jit(solution)/shard_map/ppermute | solution.py:46
  72.1 3.7 %collective-permute-done.29.refs_0_ = f32[64,256]{1,0:T(8,128)S(1)} collective-permute-done((f32[64,256]{1,0:T(8,128)S(1)}, f32[64,256]{1,0:T(8,128)S(1)}, u32[]{:S(2)}, u32[]{:S(2)}) %collective-permute-start.29) | collective-permute-done | bytes 65568 | tf_op jit(solution)/shard_map/ppermute | solution.py:46
  76.2 1.8 %collective-permute-start.32 = (f32[64,256]{1,0:T(8,128)S(1)}, f32[64,256]{1,0:T(8,128)S(1)}, u32[]{:S(2)}, u32[]{:S(2)}) collective-permute-start(f32[64,256]{1,0:T(8,128)S(1)} %add_z.1.refs_3_), channel_id=1, source_target_pairs={{0,5},{1,4},{2,7},{3,6},{4,1},{5,0},{6,3},{7,2},{8,13},{9,12},{10,... | collective-permute-start | bytes 196616 | tf_op jit(solution)/shard_map/ppermute | solution.py:52
  78.8 0.9 %collective-permute-start.34 = (f32[64,256]{1,0:T(8,128)S(1)}, f32[64,256]{1,0:T(8,128)S(1)}, u32[]{:S(2)}, u32[]{:S(2)}) collective-permute-start(f32[64,256]{1,0:T(8,128)S(1)} %add_z.1.refs_3_), channel_id=1, source_target_pairs={{0,1},{1,0},{2,3},{3,2},{4,5},{5,4},{6,7},{7,6},{8,9},{9,8},{10,11... | collective-permute-start | bytes 196616 | tf_op jit(solution)/shard_map/ppermute | solution.py:52
  79.7 1.7 %collective-permute-done.32.refs_0_ = f32[64,256]{1,0:T(8,128)S(1)} collective-permute-done((f32[64,256]{1,0:T(8,128)S(1)}, f32[64,256]{1,0:T(8,128)S(1)}, u32[]{:S(2)}, u32[]{:S(2)}) %collective-permute-start.32) | collective-permute-done | bytes 65568 | tf_op jit(solution)/shard_map/ppermute | solution.py:52
  (78 shorter events, 19.0 us)
Async XLA Ops:
  0.6 10.4 %collective-permute-start = (bf16[256,256]{1,0:T(8,128)(2,1)}, bf16[256,256]{1,0:T(8,128)(2,1)S(1)}, u32[]{:S(2)}, u32[]{:S(2)}) collective-permute-start(bf16[256,256]{1,0:T(8,128)(2,1)} %feats.1), channel_id=1, source_target_pairs={{0,24},{2,26},{4,28},{6,30},{8,16},{10,18},{12,20},{14,22},{16,8},... | collective-permute-start | bytes 393224 | tf_op jit(solution)/shard_map/ppermute | solution.py:46
  5.8 6.6 %collective-permute-start.1 = (bf16[256,256]{1,0:T(8,128)(2,1)}, bf16[256,256]{1,0:T(8,128)(2,1)S(1)}, u32[]{:S(2)}, u32[]{:S(2)}) collective-permute-start(bf16[256,256]{1,0:T(8,128)(2,1)} %feats.1), channel_id=1, source_target_pairs={{0,8},{2,10},{4,12},{6,14},{8,0},{10,2},{12,4},{14,6},{16,24},{18,... | collective-permute-start | bytes 393224 | tf_op jit(solution)/shard_map/ppermute | solution.py:46
  5.8 6.6 %collective-permute-start.2 = (bf16[256,256]{1,0:T(8,128)(2,1)}, bf16[256,256]{1,0:T(8,128)(2,1)S(1)}, u32[]{:S(2)}, u32[]{:S(2)}) collective-permute-start(bf16[256,256]{1,0:T(8,128)(2,1)} %feats.1), channel_id=1, source_target_pairs={{0,4},{2,6},{4,0},{6,2},{8,12},{10,14},{12,8},{14,10},{16,20},{18,... | collective-permute-start | bytes 393224 | tf_op jit(solution)/shard_map/ppermute | solution.py:46
  12.4 10.1 %collective-permute-start.5 = (bf16[512,256]{1,0:T(8,128)(2,1)S(1)}, bf16[512,256]{1,0:T(8,128)(2,1)S(1)}, u32[]{:S(2)}, u32[]{:S(2)}) collective-permute-start(bf16[512,256]{1,0:T(8,128)(2,1)S(1)} %join.6), channel_id=1, source_target_pairs={{0,4},{2,6},{4,0},{6,2},{8,12},{10,14},{12,8},{14,10},{16,20},{18,... | collective-permute-start | bytes 786440 | tf_op jit(solution)/shard_map/ppermute | solution.py:46
  14.0 8.5 %collective-permute-start.3 = (bf16[256,256]{1,0:T(8,128)(2,1)S(1)}, bf16[256,256]{1,0:T(8,128)(2,1)S(1)}, u32[]{:S(2)}, u32[]{:S(2)}) collective-permute-start(bf16[256,256]{1,0:T(8,128)(2,1)S(1)} %collective-permute-done.2.refs_1_), channel_id=1, source_target_pairs={{0,16},{2,18},{4,20},{6,22},{8,24},{10,26},{12,28},{14,30},{16,0},... | collective-permute-start | bytes 393224 | tf_op jit(solution)/shard_map/ppermute | solution.py:46
  14.5 8.0 %collective-permute-start.4 = (bf16[256,256]{1,0:T(8,128)(2,1)S(1)}, bf16[256,256]{1,0:T(8,128)(2,1)S(1)}, u32[]{:S(2)}, u32[]{:S(2)}) collective-permute-start(bf16[256,256]{1,0:T(8,128)(2,1)S(1)} %collective-permute-done.refs_0_.refs_2_), channel_id=1, source_target_pairs={{0,8},{2,10},{4,12},{6,14},{8,0},{10,2},{12,4},{14,6},{16,24},{18,... | collective-permute-start | bytes 393224 | tf_op jit(solution)/shard_map/ppermute | solution.py:46
  16.3 6.1 %collective-permute-start.6 = (f32[48,384]{1,0:T(8,128)S(1)}, f32[48,384]{1,0:T(8,128)S(1)}, u32[]{:S(2)}, u32[]{:S(2)}) collective-permute-start(f32[48,384]{1,0:T(8,128)S(1)} %get-tuple-element.74.own), channel_id=1, source_target_pairs={{0,1},{1,0},{2,3},{3,2},{4,5},{5,4},{6,7},{7,6},{8,9},{9,8},{10,11... | collective-permute-start | bytes 221192 | tf_op jit(solution)/shard_map/ppermute | solution.py:137
  17.9 5.4 %collective-permute-start.7 = (bf16[1024,256]{1,0:T(8,128)(2,1)S(1)}, bf16[1024,256]{1,0:T(8,128)(2,1)S(1)}, u32[]{:S(2)}, u32[]{:S(2)}) collective-permute-start(bf16[1024,256]{1,0:T(8,128)(2,1)S(1)} %join.7), channel_id=1, source_target_pairs={{0,2},{2,0},{4,6},{6,4},{8,10},{10,8},{12,14},{14,12},{16,18},{18,... | collective-permute-start | bytes 1572872 | tf_op jit(solution)/shard_map/ppermute | solution.py:46
  25.2 8.2 %collective-permute-start.9 = (bf16[256,256]{1,0:T(8,128)(2,1)S(1)}, bf16[256,256]{1,0:T(8,128)(2,1)S(1)}, u32[]{:S(2)}, u32[]{:S(2)}) collective-permute-start(bf16[256,256]{1,0:T(8,128)(2,1)S(1)} %get-tuple-element.86.refs_0_), channel_id=1, source_target_pairs={{0,24},{2,26},{4,28},{6,30},{8,16},{10,18},{12,20},{14,22},{16,8},... | collective-permute-start | bytes 393224 | tf_op jit(solution)/shard_map/ppermute | solution.py:46
  27.3 9.0 %collective-permute-start.10 = (bf16[256,256]{1,0:T(8,128)(2,1)S(1)}, bf16[256,256]{1,0:T(8,128)(2,1)S(1)}, u32[]{:S(2)}, u32[]{:S(2)}) collective-permute-start(bf16[256,256]{1,0:T(8,128)(2,1)S(1)} %get-tuple-element.86.refs_0_), channel_id=1, source_target_pairs={{0,8},{2,10},{4,12},{6,14},{8,0},{10,2},{12,4},{14,6},{16,24},{18,... | collective-permute-start | bytes 393224 | tf_op jit(solution)/shard_map/ppermute | solution.py:46
  28.1 8.3 %collective-permute-start.11 = (bf16[256,256]{1,0:T(8,128)(2,1)S(1)}, bf16[256,256]{1,0:T(8,128)(2,1)S(1)}, u32[]{:S(2)}, u32[]{:S(2)}) collective-permute-start(bf16[256,256]{1,0:T(8,128)(2,1)S(1)} %get-tuple-element.86.refs_0_), channel_id=1, source_target_pairs={{0,4},{2,6},{4,0},{6,2},{8,12},{10,14},{12,8},{14,10},{16,20},{18,... | collective-permute-start | bytes 393224 | tf_op jit(solution)/shard_map/ppermute | solution.py:46
  28.6 10.5 %collective-permute-start.13 = (bf16[256,256]{1,0:T(8,128)(2,1)S(1)}, bf16[256,256]{1,0:T(8,128)(2,1)S(1)}, u32[]{:S(2)}, u32[]{:S(2)}) collective-permute-start(bf16[256,256]{1,0:T(8,128)(2,1)S(1)} %get-tuple-element.90.refs_7_), channel_id=1, source_target_pairs={{0,24},{2,26},{4,28},{6,30},{8,16},{10,18},{12,20},{14,22},{16,8},... | collective-permute-start | bytes 393224 | tf_op jit(solution)/shard_map/ppermute | solution.py:46
  29.6 13.1 %collective-permute-start.14 = (bf16[256,256]{1,0:T(8,128)(2,1)S(1)}, bf16[256,256]{1,0:T(8,128)(2,1)S(1)}, u32[]{:S(2)}, u32[]{:S(2)}) collective-permute-start(bf16[256,256]{1,0:T(8,128)(2,1)S(1)} %get-tuple-element.90.refs_7_), channel_id=1, source_target_pairs={{0,8},{2,10},{4,12},{6,14},{8,0},{10,2},{12,4},{14,6},{16,24},{18,... | collective-permute-start | bytes 393224 | tf_op jit(solution)/shard_map/ppermute | solution.py:46
  33.4 9.3 %collective-permute-start.15 = (bf16[256,256]{1,0:T(8,128)(2,1)S(1)}, bf16[256,256]{1,0:T(8,128)(2,1)S(1)}, u32[]{:S(2)}, u32[]{:S(2)}) collective-permute-start(bf16[256,256]{1,0:T(8,128)(2,1)S(1)} %get-tuple-element.90.refs_7_), channel_id=1, source_target_pairs={{0,4},{2,6},{4,0},{6,2},{8,12},{10,14},{12,8},{14,10},{16,20},{18,... | collective-permute-start | bytes 393224 | tf_op jit(solution)/shard_map/ppermute | solution.py:46
  36.4 12.0 %collective-permute-start.17 = (bf16[512,256]{1,0:T(8,128)(2,1)S(1)}, bf16[512,256]{1,0:T(8,128)(2,1)S(1)}, u32[]{:S(2)}, u32[]{:S(2)}) collective-permute-start(bf16[512,256]{1,0:T(8,128)(2,1)S(1)} %join.9), channel_id=1, source_target_pairs={{0,4},{2,6},{4,0},{6,2},{8,12},{10,14},{12,8},{14,10},{16,20},{18,... | collective-permute-start | bytes 786440 | tf_op jit(solution)/shard_map/ppermute | solution.py:46
  37.0 9.7 %collective-permute-start.12 = (bf16[256,256]{1,0:T(8,128)(2,1)S(1)}, bf16[256,256]{1,0:T(8,128)(2,1)S(1)}, u32[]{:S(2)}, u32[]{:S(2)}) collective-permute-start(bf16[256,256]{1,0:T(8,128)(2,1)S(1)} %collective-permute-done.11.refs_1_), channel_id=1, source_target_pairs={{0,16},{2,18},{4,20},{6,22},{8,24},{10,26},{12,28},{14,30},{16,0},... | collective-permute-start | bytes 393224 | tf_op jit(solution)/shard_map/ppermute | solution.py:46
  42.7 5.7 %collective-permute-start.16 = (bf16[256,256]{1,0:T(8,128)(2,1)S(1)}, bf16[256,256]{1,0:T(8,128)(2,1)S(1)}, u32[]{:S(2)}, u32[]{:S(2)}) collective-permute-start(bf16[256,256]{1,0:T(8,128)(2,1)S(1)} %collective-permute-done.9.refs_0_.refs_2_), channel_id=1, source_target_pairs={{0,8},{2,10},{4,12},{6,14},{8,0},{10,2},{12,4},{14,6},{16,24},{18,... | collective-permute-start | bytes 393224 | tf_op jit(solution)/shard_map/ppermute | solution.py:46
  42.7 3.9 %collective-permute-start.18 = (f32[32,256]{1,0:T(8,128)S(1)}, f32[32,256]{1,0:T(8,128)S(1)}, u32[]{:S(2)}, u32[]{:S(2)}) collective-permute-start(f32[32,256]{1,0:T(8,128)S(1)} %get-tuple-element.95.own), channel_id=1, source_target_pairs={{0,1},{1,0},{2,3},{3,2},{4,5},{5,4},{6,7},{7,6},{8,9},{9,8},{10,11... | collective-permute-start | bytes 98312 | tf_op jit(solution)/shard_map/ppermute | solution.py:137
  48.6 9.8 %collective-permute-start.20 = (bf16[2048,256]{1,0:T(8,128)(2,1)S(1)}, bf16[2048,256]{1,0:T(8,128)(2,1)S(1)}, u32[]{:S(2)}, u32[]{:S(2)}) collective-permute-start(bf16[2048,256]{1,0:T(8,128)(2,1)S(1)} %get-tuple-element.105), channel_id=1, source_target_pairs={{0,2},{2,0},{4,6},{6,4},{8,10},{10,8},{12,14},{14,12},{16,18},{18,... | collective-permute-start | bytes 3145736 | tf_op jit(solution)/shard_map/ppermute | solution.py:46
  49.1 9.3 %collective-permute-start.24 = (bf16[512,256]{1,0:T(8,128)(2,1)S(1)}, bf16[512,256]{1,0:T(8,128)(2,1)S(1)}, u32[]{:S(2)}, u32[]{:S(2)}) collective-permute-start(bf16[512,256]{1,0:T(8,128)(2,1)S(1)} %join.11), channel_id=1, source_target_pairs={{0,4},{2,6},{4,0},{6,2},{8,12},{10,14},{12,8},{14,10},{16,20},{18,... | collective-permute-start | bytes 786440 | tf_op jit(solution)/shard_map/ppermute | solution.py:46
  50.3 8.0 %collective-permute-start.22 = (bf16[256,256]{1,0:T(8,128)(2,1)S(1)}, bf16[256,256]{1,0:T(8,128)(2,1)S(1)}, u32[]{:S(2)}, u32[]{:S(2)}) collective-permute-start(bf16[256,256]{1,0:T(8,128)(2,1)S(1)} %collective-permute-done.15.refs_8_), channel_id=1, source_target_pairs={{0,16},{2,18},{4,20},{6,22},{8,24},{10,26},{12,28},{14,30},{16,0},... | collective-permute-start | bytes 393224 | tf_op jit(solution)/shard_map/ppermute | solution.py:46
  50.3 8.0 %collective-permute-start.23 = (bf16[256,256]{1,0:T(8,128)(2,1)S(1)}, bf16[256,256]{1,0:T(8,128)(2,1)S(1)}, u32[]{:S(2)}, u32[]{:S(2)}) collective-permute-start(bf16[256,256]{1,0:T(8,128)(2,1)S(1)} %collective-permute-done.13.refs_0_.refs_9_), channel_id=1, source_target_pairs={{0,8},{2,10},{4,12},{6,14},{8,0},{10,2},{12,4},{14,6},{16,24},{18,... | collective-permute-start | bytes 393224 | tf_op jit(solution)/shard_map/ppermute | solution.py:46
  54.0 4.3 %collective-permute-start.21 = (bf16[256,256]{1,0:T(8,128)(2,1)S(1)}, bf16[256,256]{1,0:T(8,128)(2,1)S(1)}, u32[]{:S(2)}, u32[]{:S(2)}) collective-permute-start(bf16[256,256]{1,0:T(8,128)(2,1)S(1)} %get-tuple-element.106.q), channel_id=1, source_target_pairs={{0,2},{2,0},{4,6},{6,4},{8,10},{10,8},{12,14},{14,12},{16,18},{18,... | collective-permute-start | bytes 393224 | tf_op jit(solution)/shard_map/ppermute | solution.py:46
  61.6 5.7 %collective-permute-start.26 = (f32[64,256]{1,0:T(8,128)S(1)}, f32[64,256]{1,0:T(8,128)S(1)}, u32[]{:S(2)}, u32[]{:S(2)}) collective-permute-start(f32[64,256]{1,0:T(8,128)S(1)} %get-tuple-element.116), channel_id=1, source_target_pairs={{0,5},{1,4},{2,7},{3,6},{4,1},{5,0},{6,3},{7,2},{8,13},{9,12},{10,... | collective-permute-start | bytes 196616 | tf_op jit(solution)/shard_map/ppermute | solution.py:52
  63.6 4.3 %collective-permute-start.27 = (f32[64,256]{1,0:T(8,128)S(1)}, f32[64,256]{1,0:T(8,128)S(1)}, u32[]{:S(2)}, u32[]{:S(2)}) collective-permute-start(f32[64,256]{1,0:T(8,128)S(1)} %get-tuple-element.117), channel_id=1, source_target_pairs={{0,4},{1,5},{2,6},{3,7},{4,0},{5,1},{6,2},{7,3},{8,12},{9,13},{10,... | collective-permute-start | bytes 196616 | tf_op jit(solution)/shard_map/ppermute | solution.py:52
  64.2 4.3 %collective-permute-start.28 = (f32[64,256]{1,0:T(8,128)S(1)}, f32[64,256]{1,0:T(8,128)S(1)}, u32[]{:S(2)}, u32[]{:S(2)}) collective-permute-start(f32[64,256]{1,0:T(8,128)S(1)} %get-tuple-element.118), channel_id=1, source_target_pairs={{0,1},{1,0},{2,3},{3,2},{4,5},{5,4},{6,7},{7,6},{8,9},{9,8},{10,11... | collective-permute-start | bytes 196616 | tf_op jit(solution)/shard_map/ppermute | solution.py:52
  68.5 7.3 %collective-permute-start.29 = (f32[64,256]{1,0:T(8,128)S(1)}, f32[64,256]{1,0:T(8,128)S(1)}, u32[]{:S(2)}, u32[]{:S(2)}) collective-permute-start(f32[64,256]{1,0:T(8,128)S(1)} %add_xy.1.refs_2_), channel_id=1, source_target_pairs={{0,16},{2,18},{4,20},{6,22},{8,24},{10,26},{12,28},{14,30},{16,0},... | collective-permute-start | bytes 196616 | tf_op jit(solution)/shard_map/ppermute | solution.py:46
  68.9 6.9 %collective-permute-start.30 = (f32[64,256]{1,0:T(8,128)S(1)}, f32[64,256]{1,0:T(8,128)S(1)}, u32[]{:S(2)}, u32[]{:S(2)}) collective-permute-start(f32[64,256]{1,0:T(8,128)S(1)} %add_xy.1.refs_2_), channel_id=1, source_target_pairs={{0,24},{2,26},{4,28},{6,30},{8,16},{10,18},{12,20},{14,22},{16,8},... | collective-permute-start | bytes 196616 | tf_op jit(solution)/shard_map/ppermute | solution.py:46
  70.8 5.3 %collective-permute-start.31 = (f32[64,256]{1,0:T(8,128)S(1)}, f32[64,256]{1,0:T(8,128)S(1)}, u32[]{:S(2)}, u32[]{:S(2)}) collective-permute-start(f32[64,256]{1,0:T(8,128)S(1)} %add_xy.1.refs_2_), channel_id=1, source_target_pairs={{0,8},{2,10},{4,12},{6,14},{8,0},{10,2},{12,4},{14,6},{16,24},{18,... | collective-permute-start | bytes 196616 | tf_op jit(solution)/shard_map/ppermute | solution.py:46
  76.2 5.2 %collective-permute-start.32 = (f32[64,256]{1,0:T(8,128)S(1)}, f32[64,256]{1,0:T(8,128)S(1)}, u32[]{:S(2)}, u32[]{:S(2)}) collective-permute-start(f32[64,256]{1,0:T(8,128)S(1)} %add_z.1.refs_3_), channel_id=1, source_target_pairs={{0,5},{1,4},{2,7},{3,6},{4,1},{5,0},{6,3},{7,2},{8,13},{9,12},{10,... | collective-permute-start | bytes 196616 | tf_op jit(solution)/shard_map/ppermute | solution.py:52
  77.9 4.3 %collective-permute-start.33 = (f32[64,256]{1,0:T(8,128)S(1)}, f32[64,256]{1,0:T(8,128)S(1)}, u32[]{:S(2)}, u32[]{:S(2)}) collective-permute-start(f32[64,256]{1,0:T(8,128)S(1)} %add_z.1.refs_3_), channel_id=1, source_target_pairs={{0,4},{1,5},{2,6},{3,7},{4,0},{5,1},{6,2},{7,3},{8,12},{9,13},{10,... | collective-permute-start | bytes 196616 | tf_op jit(solution)/shard_map/ppermute | solution.py:52
  78.8 4.3 %collective-permute-start.34 = (f32[64,256]{1,0:T(8,128)S(1)}, f32[64,256]{1,0:T(8,128)S(1)}, u32[]{:S(2)}, u32[]{:S(2)}) collective-permute-start(f32[64,256]{1,0:T(8,128)S(1)} %add_z.1.refs_3_), channel_id=1, source_target_pairs={{0,1},{1,0},{2,3},{3,2},{4,5},{5,4},{6,7},{7,6},{8,9},{9,8},{10,11... | collective-permute-start | bytes 196616 | tf_op jit(solution)/shard_map/ppermute | solution.py:52
  (13 other events, 62.6 us)

commit v6 on v5

--- a/solution.py
+++ b/solution.py
@@ -202,24 +202,25 @@
                 start = pl.multiple_of((place * blocks + b % blocks) * tile, tile)
                 value = tiles[r * per_block + k]
                 turned = value.T
-                at = pl.ds(pl.multiple_of((rel & 1) * half + start, tile), tile)
+                side = rel & 1
+                at = pl.ds(pl.multiple_of(side * half + start, tile), tile)
                 adj[r * tile : (r + 1) * tile, at] = value
-
-                @pl.when(rel & 1 == 0)
-                def _():
-                    adj_t[pl.ds(start, tile), r * tile : (r + 1) * tile] = turned
-
-                @pl.when(rel & 1 == 1)
-                def _():
-                    adj_t_give[pl.ds(start, tile), r * tile : (r + 1) * tile] = turned
-
+                own = pl.multiple_of(jnp.where(side == 0, start, half), tile)
+                give = pl.multiple_of(jnp.where(side == 1, start, half), tile)
+                adj_t[pl.ds(own, tile), r * tile : (r + 1) * tile] = turned
+                adj_t_give[pl.ds(give, tile), r * tile : (r + 1) * tile] = turned
         deg = dot(adj[...], jnp.ones((2 * half, LANES), BF16))
         scale[...] = lax.rsqrt(1.0 + deg + low_count[...])
 
     adj, adj_t, adj_t_give, scale = call(
         adjacency,
         "adjacency",
-        [shaped(rows, 2 * half, BF16), shaped(half, rows, BF16), shaped(half, rows, BF16), shaped(rows, LANES, F32)],
+        [
+            shaped(rows, 2 * half, BF16),
+            shaped(half + tile, rows, BF16),
+            shaped(half + tile, rows, BF16),
+            shaped(rows, LANES, F32),
+        ],
         [low_tiles, tile_cols, low_count],
         smem=(1,),
         traffic=14 << 20,

time: 85.4 us -> 85.1 us (level)
  waiting for transfers between devices: 32.4 us -> 35.4 us
  Pallas kernels: 10.9 us -> 9.13 us
    ppermute x31, waiting for transfers between devices: 22.9 us -> 25.8 us  [to_wide(): lax.ppermute(x, WIDE, [(i, i ^ k) for i in range(lax.axis_size(WIDE))])]
    pallas_call x18, Pallas kernels: 10.9 us -> 9.13 us  [call(): pl.pallas_call(body, name=name, out_shape=outs, in_specs=[pl.BlockSpec(me...]
    ppermute x31, starting transfers between devices: 27.4 us -> 26.1 us  [to_wide(): lax.ppermute(x, WIDE, [(i, i ^ k) for i in range(lax.axis_size(WIDE))])]
  transfers between devices with their start and end apart: 39 -> 39, of which waited for: 19 -> 23; matrix products, arithmetic and copies ran while one was open for 1% -> 1% of each run, Pallas kernels for 9% -> 7%
where the time goes in v6:
time: 85.1 us; the launch traced here: 84.9 us
  starting transfers between devices  36.3 us (43%)
  waiting for transfers between devices  35.4 us (42%)
  Pallas kernels  9.13 us (11%)
  local copies, waits for them, and re-layouts  2.52 us (3%)
    ppermute x31, starting transfers between devices, to_wide(): lax.ppermute(x, WIDE, [(i, i ^ k) for i in range(lax.axis_size(WIDE))])  26.1 us
    ppermute x31, waiting for transfers between devices, to_wide(): lax.ppermute(x, WIDE, [(i, i ^ k) for i in range(lax.axis_size(WIDE))])  25.8 us
    pallas_call x18, Pallas kernels, call(): pl.pallas_call(body, name=name, out_shape=outs, in_specs=[pl.BlockSpec(me...  9.13 us
    ppermute x6, starting transfers between devices, to_both(): return lax.ppermute(x, (WIDE, HUB), pairs)  7.11 us
    ppermute x6, waiting for transfers between devices, to_both(): return lax.ppermute(x, (WIDE, HUB), pairs)  6.49 us
    ppermute x2, starting transfers between devices, to_hub(): return lax.ppermute(x, HUB, [(i, i ^ k) for i in range(n_hub)])  3.09 us
    ppermute x2, waiting for transfers between devices, to_hub(): return lax.ppermute(x, HUB, [(i, i ^ k) for i in range(n_hub)])  3.04 us
    unnamed x12, local copies, waits for them, and re-layouts  2.51 us
  transfers between devices with their start and end apart: 39, of which 23 were waited for; matrix products, arithmetic and copies ran while one was open for 1% of the time, Pallas kernels for 7%

profile of v6, /device:TPU:0, one launch (start us, length us, event | category | flops | bytes accessed | tf_op | source)
XLA Modules:
  0.0 84.9 jit_solution(7809726009955502576)
XLA Ops:
  0.6 5.1 %collective-permute-start = (bf16[256,256]{1,0:T(8,128)(2,1)}, bf16[256,256]{1,0:T(8,128)(2,1)S(1)}, u32[]{:S(2)}, u32[]{:S(2)}) collective-permute-start(bf16[256,256]{1,0:T(8,128)(2,1)} %feats.1), channel_id=1, source_target_pairs={{0,24},{2,26},{4,28},{6,30},{8,16},{10,18},{12,20},{14,22},{16,8},... | collective-permute-start | bytes 393224 | tf_op jit(solution)/shard_map/ppermute | solution.py:46
  5.8 1.5 %collective-permute-start.2 = (bf16[256,256]{1,0:T(8,128)(2,1)}, bf16[256,256]{1,0:T(8,128)(2,1)S(1)}, u32[]{:S(2)}, u32[]{:S(2)}) collective-permute-start(bf16[256,256]{1,0:T(8,128)(2,1)} %feats.1), channel_id=1, source_target_pairs={{0,4},{2,6},{4,0},{6,2},{8,12},{10,14},{12,8},{14,10},{16,20},{18,... | collective-permute-start | bytes 393224 | tf_op jit(solution)/shard_map/ppermute | solution.py:46
  11.0 1.3 %collective-permute-done.1.refs_1_.refs_3_ = bf16[256,256]{1,0:T(8,128)(2,1)S(1)} collective-permute-done((bf16[256,256]{1,0:T(8,128)(2,1)}, bf16[256,256]{1,0:T(8,128)(2,1)S(1)}, u32[]{:S(2)}, u32[]{:S(2)}) %collective-permute-start.1) | collective-permute-done | bytes 131104 | tf_op jit(solution)/shard_map/ppermute | solution.py:46
  12.4 1.6 %collective-permute-start.5 = (bf16[512,256]{1,0:T(8,128)(2,1)S(1)}, bf16[512,256]{1,0:T(8,128)(2,1)S(1)}, u32[]{:S(2)}, u32[]{:S(2)}) collective-permute-start(bf16[512,256]{1,0:T(8,128)(2,1)S(1)} %join.6), channel_id=1, source_target_pairs={{0,4},{2,6},{4,0},{6,2},{8,12},{10,14},{12,8},{14,10},{16,20},{18,... | collective-permute-start | bytes 786440 | tf_op jit(solution)/shard_map/ppermute | solution.py:46
  14.5 1.8 %collective-permute-start.4 = (bf16[256,256]{1,0:T(8,128)(2,1)S(1)}, bf16[256,256]{1,0:T(8,128)(2,1)S(1)}, u32[]{:S(2)}, u32[]{:S(2)}) collective-permute-start(bf16[256,256]{1,0:T(8,128)(2,1)S(1)} %collective-permute-done.refs_0_.refs_2_), channel_id=1, source_target_pairs={{0,8},{2,10},{4,12},{6,14},{8,0},{10,2},{12,4},{14,6},{16,24},{18,... | collective-permute-start | bytes 393224 | tf_op jit(solution)/shard_map/ppermute | solution.py:46
  16.3 1.5 %collective-permute-start.6 = (f32[48,384]{1,0:T(8,128)S(1)}, f32[48,384]{1,0:T(8,128)S(1)}, u32[]{:S(2)}, u32[]{:S(2)}) collective-permute-start(f32[48,384]{1,0:T(8,128)S(1)} %get-tuple-element.74.own), channel_id=1, source_target_pairs={{0,1},{1,0},{2,3},{3,2},{4,5},{5,4},{6,7},{7,6},{8,9},{9,8},{10,11... | collective-permute-start | bytes 221192 | tf_op jit(solution)/shard_map/ppermute | solution.py:137
  18.0 2.0 %adjacency.1 = (bf16[256,4096]{1,0:T(8,128)(2,1)S(1)}, bf16[2176,256]{1,0:T(8,128)(2,1)S(1)}, bf16[2176,256]{1,0:T(8,128)(2,1)S(1)}, f32[256,128]{1,0:T(8,128)S(1)}) custom-call(bf16[32,128,128]{2,1,0:T(8,128)(2,1)S(1)} %copy-done, s32[2,16]{1,0:T(2,128)S(1)} %copy-done.5, f32[256,128]{1,0:T(8,128)S(1)} %get-tuple-element.67.low_count), custom_call_target="tpu_custom_call" | custom-call | bytes 14680064 | tf_op jit(solution)/shard_map/adjacency/pallas_call | solution.py:22
  20.7 1.7 %collective-permute-done.3.refs_4_.refs_0_ = bf16[256,256]{1,0:T(8,128)(2,1)S(1)} collective-permute-done((bf16[256,256]{1,0:T(8,128)(2,1)S(1)}, bf16[256,256]{1,0:T(8,128)(2,1)S(1)}, u32[]{:S(2)}, u32[]{:S(2)}) %collective-permute-start.3) | collective-permute-done | bytes 131104 | tf_op jit(solution)/shard_map/ppermute | solution.py:46
  23.4 1.1 %collective-permute-done.8.last = bf16[1024,256]{1,0:T(8,128)(2,1)S(1)} collective-permute-done((bf16[1024,256]{1,0:T(8,128)(2,1)S(1)}, bf16[1024,256]{1,0:T(8,128)(2,1)S(1)}, u32[]{:S(2)}, u32[]{:S(2)}) %collective-permute-start.8) | collective-permute-done | bytes 524320 | tf_op jit(solution)/shard_map/ppermute | solution.py:46
  25.0 1.8 %collective-permute-start.9 = (bf16[256,256]{1,0:T(8,128)(2,1)S(1)}, bf16[256,256]{1,0:T(8,128)(2,1)S(1)}, u32[]{:S(2)}, u32[]{:S(2)}) collective-permute-start(bf16[256,256]{1,0:T(8,128)(2,1)S(1)} %get-tuple-element.86.refs_0_), channel_id=1, source_target_pairs={{0,24},{2,26},{4,28},{6,30},{8,16},{10,18},{12,20},{14,22},{16,8},... | collective-permute-start | bytes 393224 | tf_op jit(solution)/shard_map/ppermute | solution.py:46
  27.3 2.2 %collective-permute-start.13 = (bf16[256,256]{1,0:T(8,128)(2,1)S(1)}, bf16[256,256]{1,0:T(8,128)(2,1)S(1)}, u32[]{:S(2)}, u32[]{:S(2)}) collective-permute-start(bf16[256,256]{1,0:T(8,128)(2,1)S(1)} %get-tuple-element.90.refs_7_), channel_id=1, source_target_pairs={{0,24},{2,26},{4,28},{6,30},{8,16},{10,18},{12,20},{14,22},{16,8},... | collective-permute-start | bytes 393224 | tf_op jit(solution)/shard_map/ppermute | solution.py:46
  29.5 1.1 %collective-permute-start.14 = (bf16[256,256]{1,0:T(8,128)(2,1)S(1)}, bf16[256,256]{1,0:T(8,128)(2,1)S(1)}, u32[]{:S(2)}, u32[]{:S(2)}) collective-permute-start(bf16[256,256]{1,0:T(8,128)(2,1)S(1)} %get-tuple-element.90.refs_7_), channel_id=1, source_target_pairs={{0,8},{2,10},{4,12},{6,14},{8,0},{10,2},{12,4},{14,6},{16,24},{18,... | collective-permute-start | bytes 393224 | tf_op jit(solution)/shard_map/ppermute | solution.py:46
  30.6 2.6 %collective-permute-done.9.refs_0_.refs_2_ = bf16[256,256]{1,0:T(8,128)(2,1)S(1)} collective-permute-done((bf16[256,256]{1,0:T(8,128)(2,1)S(1)}, bf16[256,256]{1,0:T(8,128)(2,1)S(1)}, u32[]{:S(2)}, u32[]{:S(2)}) %collective-permute-start.9) | collective-permute-done | bytes 131104 | tf_op jit(solution)/shard_map/ppermute | solution.py:46
  33.9 2.4 %collective-permute-done.10.refs_1_.refs_3_ = bf16[256,256]{1,0:T(8,128)(2,1)S(1)} collective-permute-done((bf16[256,256]{1,0:T(8,128)(2,1)S(1)}, bf16[256,256]{1,0:T(8,128)(2,1)S(1)}, u32[]{:S(2)}, u32[]{:S(2)}) %collective-permute-start.10) | collective-permute-done | bytes 131104 | tf_op jit(solution)/shard_map/ppermute | solution.py:46
  37.5 1.5 %collective-permute-done.13.refs_0_.refs_9_ = bf16[256,256]{1,0:T(8,128)(2,1)S(1)} collective-permute-done((bf16[256,256]{1,0:T(8,128)(2,1)S(1)}, bf16[256,256]{1,0:T(8,128)(2,1)S(1)}, u32[]{:S(2)}, u32[]{:S(2)}) %collective-permute-start.13) | collective-permute-done | bytes 131104 | tf_op jit(solution)/shard_map/ppermute | solution.py:46
  39.0 3.2 %collective-permute-done.14.refs_1_.refs_10_ = bf16[256,256]{1,0:T(8,128)(2,1)S(1)} collective-permute-done((bf16[256,256]{1,0:T(8,128)(2,1)S(1)}, bf16[256,256]{1,0:T(8,128)(2,1)S(1)}, u32[]{:S(2)}, u32[]{:S(2)}) %collective-permute-start.14) | collective-permute-done | bytes 131104 | tf_op jit(solution)/shard_map/ppermute | solution.py:46
  42.2 1.6 %collective-permute-start.18 = (f32[32,256]{1,0:T(8,128)S(1)}, f32[32,256]{1,0:T(8,128)S(1)}, u32[]{:S(2)}, u32[]{:S(2)}) collective-permute-start(f32[32,256]{1,0:T(8,128)S(1)} %get-tuple-element.95.own), channel_id=1, source_target_pairs={{0,1},{1,0},{2,3},{3,2},{4,5},{5,4},{6,7},{7,6},{8,9},{9,8},{10,11... | collective-permute-start | bytes 98312 | tf_op jit(solution)/shard_map/ppermute | solution.py:137
  43.8 2.3 %collective-permute-done.18.refs_0_ = f32[32,256]{1,0:T(8,128)S(1)} collective-permute-done((f32[32,256]{1,0:T(8,128)S(1)}, f32[32,256]{1,0:T(8,128)S(1)}, u32[]{:S(2)}, u32[]{:S(2)}) %collective-permute-start.18) | collective-permute-done | bytes 32800 | tf_op jit(solution)/shard_map/ppermute | solution.py:137
  46.1 1.7 %collective-permute-done.16.refs_5_ = bf16[256,256]{1,0:T(8,128)(2,1)S(1)} collective-permute-done((bf16[256,256]{1,0:T(8,128)(2,1)S(1)}, bf16[256,256]{1,0:T(8,128)(2,1)S(1)}, u32[]{:S(2)}, u32[]{:S(2)}) %collective-permute-start.16) | collective-permute-done | bytes 131104 | tf_op jit(solution)/shard_map/ppermute | solution.py:46
  49.8 2.5 %collective-permute-start.23 = (bf16[256,256]{1,0:T(8,128)(2,1)S(1)}, bf16[256,256]{1,0:T(8,128)(2,1)S(1)}, u32[]{:S(2)}, u32[]{:S(2)}) collective-permute-start(bf16[256,256]{1,0:T(8,128)(2,1)S(1)} %collective-permute-done.13.refs_0_.refs_9_), channel_id=1, source_target_pairs={{0,8},{2,10},{4,12},{6,14},{8,0},{10,2},{12,4},{14,6},{16,24},{18,... | collective-permute-start | bytes 393224 | tf_op jit(solution)/shard_map/ppermute | solution.py:46
  52.3 1.7 %low_second.1 = (f32[256,256]{1,0:T(8,128)}, f32[256,256]{1,0:T(8,128)S(1)}, bf16[256,256]{1,0:T(8,128)(2,1)S(1)}) custom-call(bf16[256,4096]{1,0:T(8,128)(2,1)S(1)} %get-tuple-element.68.adj, bf16[256,64]{1,0:T(8,128)(2,1)S(1)} %get-tuple-element.69.link_t, f32[256,128]{1,0:T(8,128)S(1)} %get-tuple-element.75.scale, bf16[256,256]{1,0:T(8,128)(2,1)S(1)} %copy-done.1, ...), custom_call_target="tpu_custom_call" | custom-call | bytes 1048576 | tf_op jit(solution)/shard_map/low_second/pallas_call | solution.py:22
  54.7 3.3 %collective-permute-done.22.refs_11_ = bf16[256,256]{1,0:T(8,128)(2,1)S(1)} collective-permute-done((bf16[256,256]{1,0:T(8,128)(2,1)S(1)}, bf16[256,256]{1,0:T(8,128)(2,1)S(1)}, u32[]{:S(2)}, u32[]{:S(2)}) %collective-permute-start.22) | collective-permute-done | bytes 131104 | tf_op jit(solution)/shard_map/ppermute | solution.py:46
  58.2 1.6 %back_first.1 = (f32[256,256]{1,0:T(8,128)S(1)}, f32[256,256]{1,0:T(8,128)S(1)}) custom-call(bf16[2176,256]{1,0:T(8,128)(2,1)S(1)} %get-tuple-element.104.adj_t, bf16[2176,256]{1,0:T(8,128)(2,1)S(1)} %collective-permute-done.20.adj_t_mate, bf16[32,512]{1,0:T(8,128)(2,1)S(1)} %get-tuple-element.80.link, bf16[256,64]{1,0:T(8,128)(2,1)S(1)} %get-tuple-element.69.link_t, ...), custom_call_target="tpu_custom_call" | custom-call | bytes 1048576 | tf_op jit(solution)/shard_map/back_first/pallas_call | solution.py:22
  59.9 1.5 %collective-permute-done.25.got = f32[256,256]{1,0:T(8,128)S(1)} collective-permute-done((f32[256,256]{1,0:T(8,128)S(1)}, f32[256,256]{1,0:T(8,128)S(1)}, u32[]{:S(2)}, u32[]{:S(2)}) %collective-permute-start.25) | collective-permute-done | bytes 262176 | tf_op jit(solution)/shard_map/ppermute | solution.py:46
  61.5 2.1 %collective-permute-start.26 = (f32[64,256]{1,0:T(8,128)S(1)}, f32[64,256]{1,0:T(8,128)S(1)}, u32[]{:S(2)}, u32[]{:S(2)}) collective-permute-start(f32[64,256]{1,0:T(8,128)S(1)} %get-tuple-element.116), channel_id=1, source_target_pairs={{0,5},{1,4},{2,7},{3,6},{4,1},{5,0},{6,3},{7,2},{8,13},{9,12},{10,... | collective-permute-start | bytes 196616 | tf_op jit(solution)/shard_map/ppermute | solution.py:52
  65.0 2.3 %collective-permute-done.26.refs_0_ = f32[64,256]{1,0:T(8,128)S(1)} collective-permute-done((f32[64,256]{1,0:T(8,128)S(1)}, f32[64,256]{1,0:T(8,128)S(1)}, u32[]{:S(2)}, u32[]{:S(2)}) %collective-permute-start.26) | collective-permute-done | bytes 65568 | tf_op jit(solution)/shard_map/ppermute | solution.py:52
  68.9 2.0 %collective-permute-start.30 = (f32[64,256]{1,0:T(8,128)S(1)}, f32[64,256]{1,0:T(8,128)S(1)}, u32[]{:S(2)}, u32[]{:S(2)}) collective-permute-start(f32[64,256]{1,0:T(8,128)S(1)} %add_xy.1.refs_2_), channel_id=1, source_target_pairs={{0,24},{2,26},{4,28},{6,30},{8,16},{10,18},{12,20},{14,22},{16,8},... | collective-permute-start | bytes 196616 | tf_op jit(solution)/shard_map/ppermute | solution.py:46
  70.8 1.3 %collective-permute-start.31 = (f32[64,256]{1,0:T(8,128)S(1)}, f32[64,256]{1,0:T(8,128)S(1)}, u32[]{:S(2)}, u32[]{:S(2)}) collective-permute-start(f32[64,256]{1,0:T(8,128)S(1)} %add_xy.1.refs_2_), channel_id=1, source_target_pairs={{0,8},{2,10},{4,12},{6,14},{8,0},{10,2},{12,4},{14,6},{16,24},{18,... | collective-permute-start | bytes 196616 | tf_op jit(solution)/shard_map/ppermute | solution.py:46
  72.1 3.5 %collective-permute-done.29.refs_0_ = f32[64,256]{1,0:T(8,128)S(1)} collective-permute-done((f32[64,256]{1,0:T(8,128)S(1)}, f32[64,256]{1,0:T(8,128)S(1)}, u32[]{:S(2)}, u32[]{:S(2)}) %collective-permute-start.29) | collective-permute-done | bytes 65568 | tf_op jit(solution)/shard_map/ppermute | solution.py:46
  76.2 1.9 %collective-permute-start.32 = (f32[64,256]{1,0:T(8,128)S(1)}, f32[64,256]{1,0:T(8,128)S(1)}, u32[]{:S(2)}, u32[]{:S(2)}) collective-permute-start(f32[64,256]{1,0:T(8,128)S(1)} %add_z.1.refs_3_), channel_id=1, source_target_pairs={{0,5},{1,4},{2,7},{3,6},{4,1},{5,0},{6,3},{7,2},{8,13},{9,12},{10,... | collective-permute-start | bytes 196616 | tf_op jit(solution)/shard_map/ppermute | solution.py:52
  78.5 1.2 %collective-permute-start.34 = (f32[64,256]{1,0:T(8,128)S(1)}, f32[64,256]{1,0:T(8,128)S(1)}, u32[]{:S(2)}, u32[]{:S(2)}) collective-permute-start(f32[64,256]{1,0:T(8,128)S(1)} %add_z.1.refs_3_), channel_id=1, source_target_pairs={{0,1},{1,0},{2,3},{3,2},{4,5},{5,4},{6,7},{7,6},{8,9},{9,8},{10,11... | collective-permute-start | bytes 196616 | tf_op jit(solution)/shard_map/ppermute | solution.py:52
  79.8 1.7 %collective-permute-done.32.refs_0_ = f32[64,256]{1,0:T(8,128)S(1)} collective-permute-done((f32[64,256]{1,0:T(8,128)S(1)}, f32[64,256]{1,0:T(8,128)S(1)}, u32[]{:S(2)}, u32[]{:S(2)}) %collective-permute-start.32) | collective-permute-done | bytes 65568 | tf_op jit(solution)/shard_map/ppermute | solution.py:52
  (78 shorter events, 19.3 us)
Async XLA Ops:
  0.6 10.4 %collective-permute-start = (bf16[256,256]{1,0:T(8,128)(2,1)}, bf16[256,256]{1,0:T(8,128)(2,1)S(1)}, u32[]{:S(2)}, u32[]{:S(2)}) collective-permute-start(bf16[256,256]{1,0:T(8,128)(2,1)} %feats.1), channel_id=1, source_target_pairs={{0,24},{2,26},{4,28},{6,30},{8,16},{10,18},{12,20},{14,22},{16,8},... | collective-permute-start | bytes 393224 | tf_op jit(solution)/shard_map/ppermute | solution.py:46
  5.8 6.6 %collective-permute-start.1 = (bf16[256,256]{1,0:T(8,128)(2,1)}, bf16[256,256]{1,0:T(8,128)(2,1)S(1)}, u32[]{:S(2)}, u32[]{:S(2)}) collective-permute-start(bf16[256,256]{1,0:T(8,128)(2,1)} %feats.1), channel_id=1, source_target_pairs={{0,8},{2,10},{4,12},{6,14},{8,0},{10,2},{12,4},{14,6},{16,24},{18,... | collective-permute-start | bytes 393224 | tf_op jit(solution)/shard_map/ppermute | solution.py:46
  5.8 6.6 %collective-permute-start.2 = (bf16[256,256]{1,0:T(8,128)(2,1)}, bf16[256,256]{1,0:T(8,128)(2,1)S(1)}, u32[]{:S(2)}, u32[]{:S(2)}) collective-permute-start(bf16[256,256]{1,0:T(8,128)(2,1)} %feats.1), channel_id=1, source_target_pairs={{0,4},{2,6},{4,0},{6,2},{8,12},{10,14},{12,8},{14,10},{16,20},{18,... | collective-permute-start | bytes 393224 | tf_op jit(solution)/shard_map/ppermute | solution.py:46
  12.4 10.0 %collective-permute-start.5 = (bf16[512,256]{1,0:T(8,128)(2,1)S(1)}, bf16[512,256]{1,0:T(8,128)(2,1)S(1)}, u32[]{:S(2)}, u32[]{:S(2)}) collective-permute-start(bf16[512,256]{1,0:T(8,128)(2,1)S(1)} %join.6), channel_id=1, source_target_pairs={{0,4},{2,6},{4,0},{6,2},{8,12},{10,14},{12,8},{14,10},{16,20},{18,... | collective-permute-start | bytes 786440 | tf_op jit(solution)/shard_map/ppermute | solution.py:46
  14.0 8.4 %collective-permute-start.3 = (bf16[256,256]{1,0:T(8,128)(2,1)S(1)}, bf16[256,256]{1,0:T(8,128)(2,1)S(1)}, u32[]{:S(2)}, u32[]{:S(2)}) collective-permute-start(bf16[256,256]{1,0:T(8,128)(2,1)S(1)} %collective-permute-done.2.refs_1_), channel_id=1, source_target_pairs={{0,16},{2,18},{4,20},{6,22},{8,24},{10,26},{12,28},{14,30},{16,0},... | collective-permute-start | bytes 393224 | tf_op jit(solution)/shard_map/ppermute | solution.py:46
  14.5 7.9 %collective-permute-start.4 = (bf16[256,256]{1,0:T(8,128)(2,1)S(1)}, bf16[256,256]{1,0:T(8,128)(2,1)S(1)}, u32[]{:S(2)}, u32[]{:S(2)}) collective-permute-start(bf16[256,256]{1,0:T(8,128)(2,1)S(1)} %collective-permute-done.refs_0_.refs_2_), channel_id=1, source_target_pairs={{0,8},{2,10},{4,12},{6,14},{8,0},{10,2},{12,4},{14,6},{16,24},{18,... | collective-permute-start | bytes 393224 | tf_op jit(solution)/shard_map/ppermute | solution.py:46
  16.3 4.4 %collective-permute-start.6 = (f32[48,384]{1,0:T(8,128)S(1)}, f32[48,384]{1,0:T(8,128)S(1)}, u32[]{:S(2)}, u32[]{:S(2)}) collective-permute-start(f32[48,384]{1,0:T(8,128)S(1)} %get-tuple-element.74.own), channel_id=1, source_target_pairs={{0,1},{1,0},{2,3},{3,2},{4,5},{5,4},{6,7},{7,6},{8,9},{9,8},{10,11... | collective-permute-start | bytes 221192 | tf_op jit(solution)/shard_map/ppermute | solution.py:137
  17.9 4.9 %collective-permute-start.7 = (bf16[1024,256]{1,0:T(8,128)(2,1)S(1)}, bf16[1024,256]{1,0:T(8,128)(2,1)S(1)}, u32[]{:S(2)}, u32[]{:S(2)}) collective-permute-start(bf16[1024,256]{1,0:T(8,128)(2,1)S(1)} %join.7), channel_id=1, source_target_pairs={{0,2},{2,0},{4,6},{6,4},{8,10},{10,8},{12,14},{14,12},{16,18},{18,... | collective-permute-start | bytes 1572872 | tf_op jit(solution)/shard_map/ppermute | solution.py:46
  25.0 8.2 %collective-permute-start.9 = (bf16[256,256]{1,0:T(8,128)(2,1)S(1)}, bf16[256,256]{1,0:T(8,128)(2,1)S(1)}, u32[]{:S(2)}, u32[]{:S(2)}) collective-permute-start(bf16[256,256]{1,0:T(8,128)(2,1)S(1)} %get-tuple-element.86.refs_0_), channel_id=1, source_target_pairs={{0,24},{2,26},{4,28},{6,30},{8,16},{10,18},{12,20},{14,22},{16,8},... | collective-permute-start | bytes 393224 | tf_op jit(solution)/shard_map/ppermute | solution.py:46
  26.9 9.5 %collective-permute-start.10 = (bf16[256,256]{1,0:T(8,128)(2,1)S(1)}, bf16[256,256]{1,0:T(8,128)(2,1)S(1)}, u32[]{:S(2)}, u32[]{:S(2)}) collective-permute-start(bf16[256,256]{1,0:T(8,128)(2,1)S(1)} %get-tuple-element.86.refs_0_), channel_id=1, source_target_pairs={{0,8},{2,10},{4,12},{6,14},{8,0},{10,2},{12,4},{14,6},{16,24},{18,... | collective-permute-start | bytes 393224 | tf_op jit(solution)/shard_map/ppermute | solution.py:46
  26.9 9.5 %collective-permute-start.11 = (bf16[256,256]{1,0:T(8,128)(2,1)S(1)}, bf16[256,256]{1,0:T(8,128)(2,1)S(1)}, u32[]{:S(2)}, u32[]{:S(2)}) collective-permute-start(bf16[256,256]{1,0:T(8,128)(2,1)S(1)} %get-tuple-element.86.refs_0_), channel_id=1, source_target_pairs={{0,4},{2,6},{4,0},{6,2},{8,12},{10,14},{12,8},{14,10},{16,20},{18,... | collective-permute-start | bytes 393224 | tf_op jit(solution)/shard_map/ppermute | solution.py:46
  27.3 11.7 %collective-permute-start.13 = (bf16[256,256]{1,0:T(8,128)(2,1)S(1)}, bf16[256,256]{1,0:T(8,128)(2,1)S(1)}, u32[]{:S(2)}, u32[]{:S(2)}) collective-permute-start(bf16[256,256]{1,0:T(8,128)(2,1)S(1)} %get-tuple-element.90.refs_7_), channel_id=1, source_target_pairs={{0,24},{2,26},{4,28},{6,30},{8,16},{10,18},{12,20},{14,22},{16,8},... | collective-permute-start | bytes 393224 | tf_op jit(solution)/shard_map/ppermute | solution.py:46
  29.5 12.7 %collective-permute-start.14 = (bf16[256,256]{1,0:T(8,128)(2,1)S(1)}, bf16[256,256]{1,0:T(8,128)(2,1)S(1)}, u32[]{:S(2)}, u32[]{:S(2)}) collective-permute-start(bf16[256,256]{1,0:T(8,128)(2,1)S(1)} %get-tuple-element.90.refs_7_), channel_id=1, source_target_pairs={{0,8},{2,10},{4,12},{6,14},{8,0},{10,2},{12,4},{14,6},{16,24},{18,... | collective-permute-start | bytes 393224 | tf_op jit(solution)/shard_map/ppermute | solution.py:46
  33.2 8.9 %collective-permute-start.15 = (bf16[256,256]{1,0:T(8,128)(2,1)S(1)}, bf16[256,256]{1,0:T(8,128)(2,1)S(1)}, u32[]{:S(2)}, u32[]{:S(2)}) collective-permute-start(bf16[256,256]{1,0:T(8,128)(2,1)S(1)} %get-tuple-element.90.refs_7_), channel_id=1, source_target_pairs={{0,4},{2,6},{4,0},{6,2},{8,12},{10,14},{12,8},{14,10},{16,20},{18,... | collective-permute-start | bytes 393224 | tf_op jit(solution)/shard_map/ppermute | solution.py:46
  36.4 11.5 %collective-permute-start.17 = (bf16[512,256]{1,0:T(8,128)(2,1)S(1)}, bf16[512,256]{1,0:T(8,128)(2,1)S(1)}, u32[]{:S(2)}, u32[]{:S(2)}) collective-permute-start(bf16[512,256]{1,0:T(8,128)(2,1)S(1)} %join.9), channel_id=1, source_target_pairs={{0,4},{2,6},{4,0},{6,2},{8,12},{10,14},{12,8},{14,10},{16,20},{18,... | collective-permute-start | bytes 786440 | tf_op jit(solution)/shard_map/ppermute | solution.py:46
  37.0 9.1 %collective-permute-start.12 = (bf16[256,256]{1,0:T(8,128)(2,1)S(1)}, bf16[256,256]{1,0:T(8,128)(2,1)S(1)}, u32[]{:S(2)}, u32[]{:S(2)}) collective-permute-start(bf16[256,256]{1,0:T(8,128)(2,1)S(1)} %collective-permute-done.11.refs_1_), channel_id=1, source_target_pairs={{0,16},{2,18},{4,20},{6,22},{8,24},{10,26},{12,28},{14,30},{16,0},... | collective-permute-start | bytes 393224 | tf_op jit(solution)/shard_map/ppermute | solution.py:46
  42.2 5.6 %collective-permute-start.16 = (bf16[256,256]{1,0:T(8,128)(2,1)S(1)}, bf16[256,256]{1,0:T(8,128)(2,1)S(1)}, u32[]{:S(2)}, u32[]{:S(2)}) collective-permute-start(bf16[256,256]{1,0:T(8,128)(2,1)S(1)} %collective-permute-done.9.refs_0_.refs_2_), channel_id=1, source_target_pairs={{0,8},{2,10},{4,12},{6,14},{8,0},{10,2},{12,4},{14,6},{16,24},{18,... | collective-permute-start | bytes 393224 | tf_op jit(solution)/shard_map/ppermute | solution.py:46
  47.9 4.4 %collective-permute-start.19 = (bf16[2048,256]{1,0:T(8,128)(2,1)S(1)}, bf16[2048,256]{1,0:T(8,128)(2,1)S(1)}, u32[]{:S(2)}, u32[]{:S(2)}) collective-permute-start(bf16[2048,256]{1,0:T(8,128)(2,1)S(1)} %join.10), channel_id=1, source_target_pairs={{0,2},{2,0},{4,6},{6,4},{8,10},{10,8},{12,14},{14,12},{16,18},{18,... | collective-permute-start | bytes 3145736 | tf_op jit(solution)/shard_map/ppermute | solution.py:46
  48.0 10.3 %collective-permute-start.20 = (bf16[2176,256]{1,0:T(8,128)(2,1)S(1)}, bf16[2176,256]{1,0:T(8,128)(2,1)S(1)}, u32[]{:S(2)}, u32[]{:S(2)}) collective-permute-start(bf16[2176,256]{1,0:T(8,128)(2,1)S(1)} %get-tuple-element.105), channel_id=1, source_target_pairs={{0,2},{2,0},{4,6},{6,4},{8,10},{10,8},{12,14},{14,12},{16,18},{18,... | collective-permute-start | bytes 3342344 | tf_op jit(solution)/shard_map/ppermute | solution.py:46
  48.5 9.7 %collective-permute-start.24 = (bf16[512,256]{1,0:T(8,128)(2,1)S(1)}, bf16[512,256]{1,0:T(8,128)(2,1)S(1)}, u32[]{:S(2)}, u32[]{:S(2)}) collective-permute-start(bf16[512,256]{1,0:T(8,128)(2,1)S(1)} %join.11), channel_id=1, source_target_pairs={{0,4},{2,6},{4,0},{6,2},{8,12},{10,14},{12,8},{14,10},{16,20},{18,... | collective-permute-start | bytes 786440 | tf_op jit(solution)/shard_map/ppermute | solution.py:46
  49.1 9.0 %collective-permute-start.22 = (bf16[256,256]{1,0:T(8,128)(2,1)S(1)}, bf16[256,256]{1,0:T(8,128)(2,1)S(1)}, u32[]{:S(2)}, u32[]{:S(2)}) collective-permute-start(bf16[256,256]{1,0:T(8,128)(2,1)S(1)} %collective-permute-done.15.refs_8_), channel_id=1, source_target_pairs={{0,16},{2,18},{4,20},{6,22},{8,24},{10,26},{12,28},{14,30},{16,0},... | collective-permute-start | bytes 393224 | tf_op jit(solution)/shard_map/ppermute | solution.py:46
  49.8 8.4 %collective-permute-start.23 = (bf16[256,256]{1,0:T(8,128)(2,1)S(1)}, bf16[256,256]{1,0:T(8,128)(2,1)S(1)}, u32[]{:S(2)}, u32[]{:S(2)}) collective-permute-start(bf16[256,256]{1,0:T(8,128)(2,1)S(1)} %collective-permute-done.13.refs_0_.refs_9_), channel_id=1, source_target_pairs={{0,8},{2,10},{4,12},{6,14},{8,0},{10,2},{12,4},{14,6},{16,24},{18,... | collective-permute-start | bytes 393224 | tf_op jit(solution)/shard_map/ppermute | solution.py:46
  54.0 4.3 %collective-permute-start.21 = (bf16[256,256]{1,0:T(8,128)(2,1)S(1)}, bf16[256,256]{1,0:T(8,128)(2,1)S(1)}, u32[]{:S(2)}, u32[]{:S(2)}) collective-permute-start(bf16[256,256]{1,0:T(8,128)(2,1)S(1)} %get-tuple-element.106.q), channel_id=1, source_target_pairs={{0,2},{2,0},{4,6},{6,4},{8,10},{10,8},{12,14},{14,12},{16,18},{18,... | collective-permute-start | bytes 393224 | tf_op jit(solution)/shard_map/ppermute | solution.py:46
  61.5 5.9 %collective-permute-start.26 = (f32[64,256]{1,0:T(8,128)S(1)}, f32[64,256]{1,0:T(8,128)S(1)}, u32[]{:S(2)}, u32[]{:S(2)}) collective-permute-start(f32[64,256]{1,0:T(8,128)S(1)} %get-tuple-element.116), channel_id=1, source_target_pairs={{0,5},{1,4},{2,7},{3,6},{4,1},{5,0},{6,3},{7,2},{8,13},{9,12},{10,... | collective-permute-start | bytes 196616 | tf_op jit(solution)/shard_map/ppermute | solution.py:52
  63.6 4.3 %collective-permute-start.27 = (f32[64,256]{1,0:T(8,128)S(1)}, f32[64,256]{1,0:T(8,128)S(1)}, u32[]{:S(2)}, u32[]{:S(2)}) collective-permute-start(f32[64,256]{1,0:T(8,128)S(1)} %get-tuple-element.117), channel_id=1, source_target_pairs={{0,4},{1,5},{2,6},{3,7},{4,0},{5,1},{6,2},{7,3},{8,12},{9,13},{10,... | collective-permute-start | bytes 196616 | tf_op jit(solution)/shard_map/ppermute | solution.py:52
  64.2 4.3 %collective-permute-start.28 = (f32[64,256]{1,0:T(8,128)S(1)}, f32[64,256]{1,0:T(8,128)S(1)}, u32[]{:S(2)}, u32[]{:S(2)}) collective-permute-start(f32[64,256]{1,0:T(8,128)S(1)} %get-tuple-element.118), channel_id=1, source_target_pairs={{0,1},{1,0},{2,3},{3,2},{4,5},{5,4},{6,7},{7,6},{8,9},{9,8},{10,11... | collective-permute-start | bytes 196616 | tf_op jit(solution)/shard_map/ppermute | solution.py:52
  68.5 7.0 %collective-permute-start.29 = (f32[64,256]{1,0:T(8,128)S(1)}, f32[64,256]{1,0:T(8,128)S(1)}, u32[]{:S(2)}, u32[]{:S(2)}) collective-permute-start(f32[64,256]{1,0:T(8,128)S(1)} %add_xy.1.refs_2_), channel_id=1, source_target_pairs={{0,16},{2,18},{4,20},{6,22},{8,24},{10,26},{12,28},{14,30},{16,0},... | collective-permute-start | bytes 196616 | tf_op jit(solution)/shard_map/ppermute | solution.py:46
  68.9 6.7 %collective-permute-start.30 = (f32[64,256]{1,0:T(8,128)S(1)}, f32[64,256]{1,0:T(8,128)S(1)}, u32[]{:S(2)}, u32[]{:S(2)}) collective-permute-start(f32[64,256]{1,0:T(8,128)S(1)} %add_xy.1.refs_2_), channel_id=1, source_target_pairs={{0,24},{2,26},{4,28},{6,30},{8,16},{10,18},{12,20},{14,22},{16,8},... | collective-permute-start | bytes 196616 | tf_op jit(solution)/shard_map/ppermute | solution.py:46
  70.8 5.4 %collective-permute-start.31 = (f32[64,256]{1,0:T(8,128)S(1)}, f32[64,256]{1,0:T(8,128)S(1)}, u32[]{:S(2)}, u32[]{:S(2)}) collective-permute-start(f32[64,256]{1,0:T(8,128)S(1)} %add_xy.1.refs_2_), channel_id=1, source_target_pairs={{0,8},{2,10},{4,12},{6,14},{8,0},{10,2},{12,4},{14,6},{16,24},{18,... | collective-permute-start | bytes 196616 | tf_op jit(solution)/shard_map/ppermute | solution.py:46
  76.2 5.2 %collective-permute-start.32 = (f32[64,256]{1,0:T(8,128)S(1)}, f32[64,256]{1,0:T(8,128)S(1)}, u32[]{:S(2)}, u32[]{:S(2)}) collective-permute-start(f32[64,256]{1,0:T(8,128)S(1)} %add_z.1.refs_3_), channel_id=1, source_target_pairs={{0,5},{1,4},{2,7},{3,6},{4,1},{5,0},{6,3},{7,2},{8,13},{9,12},{10,... | collective-permute-start | bytes 196616 | tf_op jit(solution)/shard_map/ppermute | solution.py:52
  78.1 4.3 %collective-permute-start.33 = (f32[64,256]{1,0:T(8,128)S(1)}, f32[64,256]{1,0:T(8,128)S(1)}, u32[]{:S(2)}, u32[]{:S(2)}) collective-permute-start(f32[64,256]{1,0:T(8,128)S(1)} %add_z.1.refs_3_), channel_id=1, source_target_pairs={{0,4},{1,5},{2,6},{3,7},{4,0},{5,1},{6,2},{7,3},{8,12},{9,13},{10,... | collective-permute-start | bytes 196616 | tf_op jit(solution)/shard_map/ppermute | solution.py:52
  78.5 4.3 %collective-permute-start.34 = (f32[64,256]{1,0:T(8,128)S(1)}, f32[64,256]{1,0:T(8,128)S(1)}, u32[]{:S(2)}, u32[]{:S(2)}) collective-permute-start(f32[64,256]{1,0:T(8,128)S(1)} %add_z.1.refs_3_), channel_id=1, source_target_pairs={{0,1},{1,0},{2,3},{3,2},{4,5},{5,4},{6,7},{7,6},{8,9},{9,8},{10,11... | collective-permute-start | bytes 196616 | tf_op jit(solution)/shard_map/ppermute | solution.py:52
  (13 other events, 46.4 us)

commit v7 on v6

--- a/solution.py
+++ b/solution.py
@@ -400,7 +400,8 @@
             out[...] = keep[at] + got[at]
 
     shares = call(split, "split", [shaped(share, classes, F32) for _ in range(n_share)], [keep, got])
-    shares = [to_both(shares[k], *steps[k]) for k in range(n_share - 1, 0, -1)] + [shares[0]]
+    turn = [n_share - 1] + list(range(1, n_share - 1))
+    shares = [to_both(shares[k], *steps[k]) for k in turn] + [shares[0]]
 
     def add_up(*refs):
         refs[-1][...] = pairwise([r[...] for r in refs[:-1]])

time: 85.1 us -> 85.8 us (level)
  transfers between devices with their start and end apart: 39 -> 39, of which waited for: 23 -> 22; matrix products, arithmetic and copies ran while one was open for 1% -> 1% of each run, Pallas kernels for 7% -> 7%
where the time goes in v7:
time: 85.8 us; the launch traced here: 85.6 us
  starting transfers between devices  36.2 us (42%)
  waiting for transfers between devices  36.2 us (42%)
  Pallas kernels  9.13 us (11%)
  local copies, waits for them, and re-layouts  2.52 us (3%)
    ppermute x31, starting transfers between devices, to_wide(): lax.ppermute(x, WIDE, [(i, i ^ k) for i in range(lax.axis_size(WIDE))])  26 us
    ppermute x31, waiting for transfers between devices, to_wide(): lax.ppermute(x, WIDE, [(i, i ^ k) for i in range(lax.axis_size(WIDE))])  25.8 us
    pallas_call x18, Pallas kernels, call(): pl.pallas_call(body, name=name, out_shape=outs, in_specs=[pl.BlockSpec(me...  9.13 us
    ppermute x6, waiting for transfers between devices, to_both(): return lax.ppermute(x, (WIDE, HUB), pairs)  7.32 us
    ppermute x6, starting transfers between devices, to_both(): return lax.ppermute(x, (WIDE, HUB), pairs)  7.11 us
    ppermute x2, starting transfers between devices, to_hub(): return lax.ppermute(x, HUB, [(i, i ^ k) for i in range(n_hub)])  3.09 us
    ppermute x2, waiting for transfers between devices, to_hub(): return lax.ppermute(x, HUB, [(i, i ^ k) for i in range(n_hub)])  3.04 us
    unnamed x12, local copies, waits for them, and re-layouts  2.51 us
  transfers between devices with their start and end apart: 39, of which 22 were waited for; matrix products, arithmetic and copies ran while one was open for 1% of the time, Pallas kernels for 7%

profile of v7, /device:TPU:0, one launch (start us, length us, event | category | flops | bytes accessed | tf_op | source)
XLA Modules:
  0.0 85.6 jit_solution(17830857259932974134)
XLA Ops:
  0.6 5.1 %collective-permute-start = (bf16[256,256]{1,0:T(8,128)(2,1)}, bf16[256,256]{1,0:T(8,128)(2,1)S(1)}, u32[]{:S(2)}, u32[]{:S(2)}) collective-permute-start(bf16[256,256]{1,0:T(8,128)(2,1)} %feats.1), channel_id=1, source_target_pairs={{0,24},{2,26},{4,28},{6,30},{8,16},{10,18},{12,20},{14,22},{16,8},... | collective-permute-start | bytes 393224 | tf_op jit(solution)/shard_map/ppermute | solution.py:46
  5.8 1.5 %collective-permute-start.2 = (bf16[256,256]{1,0:T(8,128)(2,1)}, bf16[256,256]{1,0:T(8,128)(2,1)S(1)}, u32[]{:S(2)}, u32[]{:S(2)}) collective-permute-start(bf16[256,256]{1,0:T(8,128)(2,1)} %feats.1), channel_id=1, source_target_pairs={{0,4},{2,6},{4,0},{6,2},{8,12},{10,14},{12,8},{14,10},{16,20},{18,... | collective-permute-start | bytes 393224 | tf_op jit(solution)/shard_map/ppermute | solution.py:46
  11.0 1.3 %collective-permute-done.1.refs_1_.refs_3_ = bf16[256,256]{1,0:T(8,128)(2,1)S(1)} collective-permute-done((bf16[256,256]{1,0:T(8,128)(2,1)}, bf16[256,256]{1,0:T(8,128)(2,1)S(1)}, u32[]{:S(2)}, u32[]{:S(2)}) %collective-permute-start.1) | collective-permute-done | bytes 131104 | tf_op jit(solution)/shard_map/ppermute | solution.py:46
  12.4 1.6 %collective-permute-start.5 = (bf16[512,256]{1,0:T(8,128)(2,1)S(1)}, bf16[512,256]{1,0:T(8,128)(2,1)S(1)}, u32[]{:S(2)}, u32[]{:S(2)}) collective-permute-start(bf16[512,256]{1,0:T(8,128)(2,1)S(1)} %join.6), channel_id=1, source_target_pairs={{0,4},{2,6},{4,0},{6,2},{8,12},{10,14},{12,8},{14,10},{16,20},{18,... | collective-permute-start | bytes 786440 | tf_op jit(solution)/shard_map/ppermute | solution.py:46
  14.5 1.8 %collective-permute-start.4 = (bf16[256,256]{1,0:T(8,128)(2,1)S(1)}, bf16[256,256]{1,0:T(8,128)(2,1)S(1)}, u32[]{:S(2)}, u32[]{:S(2)}) collective-permute-start(bf16[256,256]{1,0:T(8,128)(2,1)S(1)} %collective-permute-done.refs_0_.refs_2_), channel_id=1, source_target_pairs={{0,8},{2,10},{4,12},{6,14},{8,0},{10,2},{12,4},{14,6},{16,24},{18,... | collective-permute-start | bytes 393224 | tf_op jit(solution)/shard_map/ppermute | solution.py:46
  16.3 1.5 %collective-permute-start.6 = (f32[48,384]{1,0:T(8,128)S(1)}, f32[48,384]{1,0:T(8,128)S(1)}, u32[]{:S(2)}, u32[]{:S(2)}) collective-permute-start(f32[48,384]{1,0:T(8,128)S(1)} %get-tuple-element.74.own), channel_id=1, source_target_pairs={{0,1},{1,0},{2,3},{3,2},{4,5},{5,4},{6,7},{7,6},{8,9},{9,8},{10,11... | collective-permute-start | bytes 221192 | tf_op jit(solution)/shard_map/ppermute | solution.py:137
  18.0 2.0 %adjacency.1 = (bf16[256,4096]{1,0:T(8,128)(2,1)S(1)}, bf16[2176,256]{1,0:T(8,128)(2,1)S(1)}, bf16[2176,256]{1,0:T(8,128)(2,1)S(1)}, f32[256,128]{1,0:T(8,128)S(1)}) custom-call(bf16[32,128,128]{2,1,0:T(8,128)(2,1)S(1)} %copy-done, s32[2,16]{1,0:T(2,128)S(1)} %copy-done.5, f32[256,128]{1,0:T(8,128)S(1)} %get-tuple-element.67.low_count), custom_call_target="tpu_custom_call" | custom-call | bytes 14680064 | tf_op jit(solution)/shard_map/adjacency/pallas_call | solution.py:22
  20.7 1.7 %collective-permute-done.3.refs_4_.refs_0_ = bf16[256,256]{1,0:T(8,128)(2,1)S(1)} collective-permute-done((bf16[256,256]{1,0:T(8,128)(2,1)S(1)}, bf16[256,256]{1,0:T(8,128)(2,1)S(1)}, u32[]{:S(2)}, u32[]{:S(2)}) %collective-permute-start.3) | collective-permute-done | bytes 131104 | tf_op jit(solution)/shard_map/ppermute | solution.py:46
  25.0 1.8 %collective-permute-start.9 = (bf16[256,256]{1,0:T(8,128)(2,1)S(1)}, bf16[256,256]{1,0:T(8,128)(2,1)S(1)}, u32[]{:S(2)}, u32[]{:S(2)}) collective-permute-start(bf16[256,256]{1,0:T(8,128)(2,1)S(1)} %get-tuple-element.86.refs_0_), channel_id=1, source_target_pairs={{0,24},{2,26},{4,28},{6,30},{8,16},{10,18},{12,20},{14,22},{16,8},... | collective-permute-start | bytes 393224 | tf_op jit(solution)/shard_map/ppermute | solution.py:46
  27.3 2.2 %collective-permute-start.13 = (bf16[256,256]{1,0:T(8,128)(2,1)S(1)}, bf16[256,256]{1,0:T(8,128)(2,1)S(1)}, u32[]{:S(2)}, u32[]{:S(2)}) collective-permute-start(bf16[256,256]{1,0:T(8,128)(2,1)S(1)} %get-tuple-element.90.refs_7_), channel_id=1, source_target_pairs={{0,24},{2,26},{4,28},{6,30},{8,16},{10,18},{12,20},{14,22},{16,8},... | collective-permute-start | bytes 393224 | tf_op jit(solution)/shard_map/ppermute | solution.py:46
  30.6 2.6 %collective-permute-done.9.refs_0_.refs_2_ = bf16[256,256]{1,0:T(8,128)(2,1)S(1)} collective-permute-done((bf16[256,256]{1,0:T(8,128)(2,1)S(1)}, bf16[256,256]{1,0:T(8,128)(2,1)S(1)}, u32[]{:S(2)}, u32[]{:S(2)}) %collective-permute-start.9) | collective-permute-done | bytes 131104 | tf_op jit(solution)/shard_map/ppermute | solution.py:46
  33.9 2.4 %collective-permute-done.10.refs_1_.refs_3_ = bf16[256,256]{1,0:T(8,128)(2,1)S(1)} collective-permute-done((bf16[256,256]{1,0:T(8,128)(2,1)S(1)}, bf16[256,256]{1,0:T(8,128)(2,1)S(1)}, u32[]{:S(2)}, u32[]{:S(2)}) %collective-permute-start.10) | collective-permute-done | bytes 131104 | tf_op jit(solution)/shard_map/ppermute | solution.py:46
  37.5 1.5 %collective-permute-done.13.refs_0_.refs_9_ = bf16[256,256]{1,0:T(8,128)(2,1)S(1)} collective-permute-done((bf16[256,256]{1,0:T(8,128)(2,1)S(1)}, bf16[256,256]{1,0:T(8,128)(2,1)S(1)}, u32[]{:S(2)}, u32[]{:S(2)}) %collective-permute-start.13) | collective-permute-done | bytes 131104 | tf_op jit(solution)/shard_map/ppermute | solution.py:46
  39.0 3.2 %collective-permute-done.14.refs_1_.refs_10_ = bf16[256,256]{1,0:T(8,128)(2,1)S(1)} collective-permute-done((bf16[256,256]{1,0:T(8,128)(2,1)S(1)}, bf16[256,256]{1,0:T(8,128)(2,1)S(1)}, u32[]{:S(2)}, u32[]{:S(2)}) %collective-permute-start.14) | collective-permute-done | bytes 131104 | tf_op jit(solution)/shard_map/ppermute | solution.py:46
  42.2 1.6 %collective-permute-start.18 = (f32[32,256]{1,0:T(8,128)S(1)}, f32[32,256]{1,0:T(8,128)S(1)}, u32[]{:S(2)}, u32[]{:S(2)}) collective-permute-start(f32[32,256]{1,0:T(8,128)S(1)} %get-tuple-element.95.own), channel_id=1, source_target_pairs={{0,1},{1,0},{2,3},{3,2},{4,5},{5,4},{6,7},{7,6},{8,9},{9,8},{10,11... | collective-permute-start | bytes 98312 | tf_op jit(solution)/shard_map/ppermute | solution.py:137
  43.8 2.3 %collective-permute-done.18.refs_0_ = f32[32,256]{1,0:T(8,128)S(1)} collective-permute-done((f32[32,256]{1,0:T(8,128)S(1)}, f32[32,256]{1,0:T(8,128)S(1)}, u32[]{:S(2)}, u32[]{:S(2)}) %collective-permute-start.18) | collective-permute-done | bytes 32800 | tf_op jit(solution)/shard_map/ppermute | solution.py:137
  46.1 1.7 %collective-permute-done.16.refs_5_ = bf16[256,256]{1,0:T(8,128)(2,1)S(1)} collective-permute-done((bf16[256,256]{1,0:T(8,128)(2,1)S(1)}, bf16[256,256]{1,0:T(8,128)(2,1)S(1)}, u32[]{:S(2)}, u32[]{:S(2)}) %collective-permute-start.16) | collective-permute-done | bytes 131104 | tf_op jit(solution)/shard_map/ppermute | solution.py:46
  49.8 2.5 %collective-permute-start.23 = (bf16[256,256]{1,0:T(8,128)(2,1)S(1)}, bf16[256,256]{1,0:T(8,128)(2,1)S(1)}, u32[]{:S(2)}, u32[]{:S(2)}) collective-permute-start(bf16[256,256]{1,0:T(8,128)(2,1)S(1)} %collective-permute-done.13.refs_0_.refs_9_), channel_id=1, source_target_pairs={{0,8},{2,10},{4,12},{6,14},{8,0},{10,2},{12,4},{14,6},{16,24},{18,... | collective-permute-start | bytes 393224 | tf_op jit(solution)/shard_map/ppermute | solution.py:46
  52.3 1.7 %low_second.1 = (f32[256,256]{1,0:T(8,128)}, f32[256,256]{1,0:T(8,128)S(1)}, bf16[256,256]{1,0:T(8,128)(2,1)S(1)}) custom-call(bf16[256,4096]{1,0:T(8,128)(2,1)S(1)} %get-tuple-element.68.adj, bf16[256,64]{1,0:T(8,128)(2,1)S(1)} %get-tuple-element.69.link_t, f32[256,128]{1,0:T(8,128)S(1)} %get-tuple-element.75.scale, bf16[256,256]{1,0:T(8,128)(2,1)S(1)} %copy-done.1, ...), custom_call_target="tpu_custom_call" | custom-call | bytes 1048576 | tf_op jit(solution)/shard_map/low_second/pallas_call | solution.py:22
  54.7 3.3 %collective-permute-done.22.refs_11_ = bf16[256,256]{1,0:T(8,128)(2,1)S(1)} collective-permute-done((bf16[256,256]{1,0:T(8,128)(2,1)S(1)}, bf16[256,256]{1,0:T(8,128)(2,1)S(1)}, u32[]{:S(2)}, u32[]{:S(2)}) %collective-permute-start.22) | collective-permute-done | bytes 131104 | tf_op jit(solution)/shard_map/ppermute | solution.py:46
  58.2 1.6 %back_first.1 = (f32[256,256]{1,0:T(8,128)S(1)}, f32[256,256]{1,0:T(8,128)S(1)}) custom-call(bf16[2176,256]{1,0:T(8,128)(2,1)S(1)} %get-tuple-element.104.adj_t, bf16[2176,256]{1,0:T(8,128)(2,1)S(1)} %collective-permute-done.20.adj_t_mate, bf16[32,512]{1,0:T(8,128)(2,1)S(1)} %get-tuple-element.80.link, bf16[256,64]{1,0:T(8,128)(2,1)S(1)} %get-tuple-element.69.link_t, ...), custom_call_target="tpu_custom_call" | custom-call | bytes 1048576 | tf_op jit(solution)/shard_map/back_first/pallas_call | solution.py:22
  59.9 1.5 %collective-permute-done.25.got = f32[256,256]{1,0:T(8,128)S(1)} collective-permute-done((f32[256,256]{1,0:T(8,128)S(1)}, f32[256,256]{1,0:T(8,128)S(1)}, u32[]{:S(2)}, u32[]{:S(2)}) %collective-permute-start.25) | collective-permute-done | bytes 262176 | tf_op jit(solution)/shard_map/ppermute | solution.py:46
  61.5 2.1 %collective-permute-start.26 = (f32[64,256]{1,0:T(8,128)S(1)}, f32[64,256]{1,0:T(8,128)S(1)}, u32[]{:S(2)}, u32[]{:S(2)}) collective-permute-start(f32[64,256]{1,0:T(8,128)S(1)} %get-tuple-element.116), channel_id=1, source_target_pairs={{0,5},{1,4},{2,7},{3,6},{4,1},{5,0},{6,3},{7,2},{8,13},{9,12},{10,... | collective-permute-start | bytes 196616 | tf_op jit(solution)/shard_map/ppermute | solution.py:52
  65.0 1.7 %collective-permute-done.26.refs_0_ = f32[64,256]{1,0:T(8,128)S(1)} collective-permute-done((f32[64,256]{1,0:T(8,128)S(1)}, f32[64,256]{1,0:T(8,128)S(1)}, u32[]{:S(2)}, u32[]{:S(2)}) %collective-permute-start.26) | collective-permute-done | bytes 65568 | tf_op jit(solution)/shard_map/ppermute | solution.py:52
  66.8 1.3 %collective-permute-done.27.refs_1_ = f32[64,256]{1,0:T(8,128)S(1)} collective-permute-done((f32[64,256]{1,0:T(8,128)S(1)}, f32[64,256]{1,0:T(8,128)S(1)}, u32[]{:S(2)}, u32[]{:S(2)}) %collective-permute-start.27) | collective-permute-done | bytes 65568 | tf_op jit(solution)/shard_map/ppermute | solution.py:52
  68.9 1.6 %collective-permute-start.30 = (f32[64,256]{1,0:T(8,128)S(1)}, f32[64,256]{1,0:T(8,128)S(1)}, u32[]{:S(2)}, u32[]{:S(2)}) collective-permute-start(f32[64,256]{1,0:T(8,128)S(1)} %add_xy.1.refs_2_), channel_id=1, source_target_pairs={{0,24},{2,26},{4,28},{6,30},{8,16},{10,18},{12,20},{14,22},{16,8},... | collective-permute-start | bytes 196616 | tf_op jit(solution)/shard_map/ppermute | solution.py:46
  70.5 1.5 %collective-permute-start.31 = (f32[64,256]{1,0:T(8,128)S(1)}, f32[64,256]{1,0:T(8,128)S(1)}, u32[]{:S(2)}, u32[]{:S(2)}) collective-permute-start(f32[64,256]{1,0:T(8,128)S(1)} %add_xy.1.refs_2_), channel_id=1, source_target_pairs={{0,8},{2,10},{4,12},{6,14},{8,0},{10,2},{12,4},{14,6},{16,24},{18,... | collective-permute-start | bytes 196616 | tf_op jit(solution)/shard_map/ppermute | solution.py:46
  72.0 3.6 %collective-permute-done.29.refs_0_ = f32[64,256]{1,0:T(8,128)S(1)} collective-permute-done((f32[64,256]{1,0:T(8,128)S(1)}, f32[64,256]{1,0:T(8,128)S(1)}, u32[]{:S(2)}, u32[]{:S(2)}) %collective-permute-start.29) | collective-permute-done | bytes 65568 | tf_op jit(solution)/shard_map/ppermute | solution.py:46
  76.0 1.8 %collective-permute-start.32 = (f32[64,256]{1,0:T(8,128)S(1)}, f32[64,256]{1,0:T(8,128)S(1)}, u32[]{:S(2)}, u32[]{:S(2)}) collective-permute-start(f32[64,256]{1,0:T(8,128)S(1)} %add_z.1.refs_3_), channel_id=1, source_target_pairs={{0,5},{1,4},{2,7},{3,6},{4,1},{5,0},{6,3},{7,2},{8,13},{9,12},{10,... | collective-permute-start | bytes 196616 | tf_op jit(solution)/shard_map/ppermute | solution.py:52
  77.8 1.4 %collective-permute-start.33 = (f32[64,256]{1,0:T(8,128)S(1)}, f32[64,256]{1,0:T(8,128)S(1)}, u32[]{:S(2)}, u32[]{:S(2)}) collective-permute-start(f32[64,256]{1,0:T(8,128)S(1)} %add_z.1.refs_3_), channel_id=1, source_target_pairs={{0,4},{1,5},{2,6},{3,7},{4,0},{5,1},{6,2},{7,3},{8,12},{9,13},{10,... | collective-permute-start | bytes 196616 | tf_op jit(solution)/shard_map/ppermute | solution.py:52
  79.5 1.7 %collective-permute-done.32.refs_0_ = f32[64,256]{1,0:T(8,128)S(1)} collective-permute-done((f32[64,256]{1,0:T(8,128)S(1)}, f32[64,256]{1,0:T(8,128)S(1)}, u32[]{:S(2)}, u32[]{:S(2)}) %collective-permute-start.32) | collective-permute-done | bytes 65568 | tf_op jit(solution)/shard_map/ppermute | solution.py:52
  82.2 1.3 %collective-permute-done.34.refs_2_ = f32[64,256]{1,0:T(8,128)S(1)} collective-permute-done((f32[64,256]{1,0:T(8,128)S(1)}, f32[64,256]{1,0:T(8,128)S(1)}, u32[]{:S(2)}, u32[]{:S(2)}) %collective-permute-start.34) | collective-permute-done | bytes 65568 | tf_op jit(solution)/shard_map/ppermute | solution.py:52
  (78 shorter events, 20.1 us)
Async XLA Ops:
  0.6 10.4 %collective-permute-start = (bf16[256,256]{1,0:T(8,128)(2,1)}, bf16[256,256]{1,0:T(8,128)(2,1)S(1)}, u32[]{:S(2)}, u32[]{:S(2)}) collective-permute-start(bf16[256,256]{1,0:T(8,128)(2,1)} %feats.1), channel_id=1, source_target_pairs={{0,24},{2,26},{4,28},{6,30},{8,16},{10,18},{12,20},{14,22},{16,8},... | collective-permute-start | bytes 393224 | tf_op jit(solution)/shard_map/ppermute | solution.py:46
  5.8 6.6 %collective-permute-start.1 = (bf16[256,256]{1,0:T(8,128)(2,1)}, bf16[256,256]{1,0:T(8,128)(2,1)S(1)}, u32[]{:S(2)}, u32[]{:S(2)}) collective-permute-start(bf16[256,256]{1,0:T(8,128)(2,1)} %feats.1), channel_id=1, source_target_pairs={{0,8},{2,10},{4,12},{6,14},{8,0},{10,2},{12,4},{14,6},{16,24},{18,... | collective-permute-start | bytes 393224 | tf_op jit(solution)/shard_map/ppermute | solution.py:46
  5.8 6.6 %collective-permute-start.2 = (bf16[256,256]{1,0:T(8,128)(2,1)}, bf16[256,256]{1,0:T(8,128)(2,1)S(1)}, u32[]{:S(2)}, u32[]{:S(2)}) collective-permute-start(bf16[256,256]{1,0:T(8,128)(2,1)} %feats.1), channel_id=1, source_target_pairs={{0,4},{2,6},{4,0},{6,2},{8,12},{10,14},{12,8},{14,10},{16,20},{18,... | collective-permute-start | bytes 393224 | tf_op jit(solution)/shard_map/ppermute | solution.py:46
  12.4 10.0 %collective-permute-start.5 = (bf16[512,256]{1,0:T(8,128)(2,1)S(1)}, bf16[512,256]{1,0:T(8,128)(2,1)S(1)}, u32[]{:S(2)}, u32[]{:S(2)}) collective-permute-start(bf16[512,256]{1,0:T(8,128)(2,1)S(1)} %join.6), channel_id=1, source_target_pairs={{0,4},{2,6},{4,0},{6,2},{8,12},{10,14},{12,8},{14,10},{16,20},{18,... | collective-permute-start | bytes 786440 | tf_op jit(solution)/shard_map/ppermute | solution.py:46
  14.0 8.4 %collective-permute-start.3 = (bf16[256,256]{1,0:T(8,128)(2,1)S(1)}, bf16[256,256]{1,0:T(8,128)(2,1)S(1)}, u32[]{:S(2)}, u32[]{:S(2)}) collective-permute-start(bf16[256,256]{1,0:T(8,128)(2,1)S(1)} %collective-permute-done.2.refs_1_), channel_id=1, source_target_pairs={{0,16},{2,18},{4,20},{6,22},{8,24},{10,26},{12,28},{14,30},{16,0},... | collective-permute-start | bytes 393224 | tf_op jit(solution)/shard_map/ppermute | solution.py:46
  14.5 7.9 %collective-permute-start.4 = (bf16[256,256]{1,0:T(8,128)(2,1)S(1)}, bf16[256,256]{1,0:T(8,128)(2,1)S(1)}, u32[]{:S(2)}, u32[]{:S(2)}) collective-permute-start(bf16[256,256]{1,0:T(8,128)(2,1)S(1)} %collective-permute-done.refs_0_.refs_2_), channel_id=1, source_target_pairs={{0,8},{2,10},{4,12},{6,14},{8,0},{10,2},{12,4},{14,6},{16,24},{18,... | collective-permute-start | bytes 393224 | tf_op jit(solution)/shard_map/ppermute | solution.py:46
  16.3 4.4 %collective-permute-start.6 = (f32[48,384]{1,0:T(8,128)S(1)}, f32[48,384]{1,0:T(8,128)S(1)}, u32[]{:S(2)}, u32[]{:S(2)}) collective-permute-start(f32[48,384]{1,0:T(8,128)S(1)} %get-tuple-element.74.own), channel_id=1, source_target_pairs={{0,1},{1,0},{2,3},{3,2},{4,5},{5,4},{6,7},{7,6},{8,9},{9,8},{10,11... | collective-permute-start | bytes 221192 | tf_op jit(solution)/shard_map/ppermute | solution.py:137
  17.9 4.9 %collective-permute-start.7 = (bf16[1024,256]{1,0:T(8,128)(2,1)S(1)}, bf16[1024,256]{1,0:T(8,128)(2,1)S(1)}, u32[]{:S(2)}, u32[]{:S(2)}) collective-permute-start(bf16[1024,256]{1,0:T(8,128)(2,1)S(1)} %join.7), channel_id=1, source_target_pairs={{0,2},{2,0},{4,6},{6,4},{8,10},{10,8},{12,14},{14,12},{16,18},{18,... | collective-permute-start | bytes 1572872 | tf_op jit(solution)/shard_map/ppermute | solution.py:46
  25.0 8.2 %collective-permute-start.9 = (bf16[256,256]{1,0:T(8,128)(2,1)S(1)}, bf16[256,256]{1,0:T(8,128)(2,1)S(1)}, u32[]{:S(2)}, u32[]{:S(2)}) collective-permute-start(bf16[256,256]{1,0:T(8,128)(2,1)S(1)} %get-tuple-element.86.refs_0_), channel_id=1, source_target_pairs={{0,24},{2,26},{4,28},{6,30},{8,16},{10,18},{12,20},{14,22},{16,8},... | collective-permute-start | bytes 393224 | tf_op jit(solution)/shard_map/ppermute | solution.py:46
  26.9 9.5 %collective-permute-start.10 = (bf16[256,256]{1,0:T(8,128)(2,1)S(1)}, bf16[256,256]{1,0:T(8,128)(2,1)S(1)}, u32[]{:S(2)}, u32[]{:S(2)}) collective-permute-start(bf16[256,256]{1,0:T(8,128)(2,1)S(1)} %get-tuple-element.86.refs_0_), channel_id=1, source_target_pairs={{0,8},{2,10},{4,12},{6,14},{8,0},{10,2},{12,4},{14,6},{16,24},{18,... | collective-permute-start | bytes 393224 | tf_op jit(solution)/shard_map/ppermute | solution.py:46
  26.9 9.5 %collective-permute-start.11 = (bf16[256,256]{1,0:T(8,128)(2,1)S(1)}, bf16[256,256]{1,0:T(8,128)(2,1)S(1)}, u32[]{:S(2)}, u32[]{:S(2)}) collective-permute-start(bf16[256,256]{1,0:T(8,128)(2,1)S(1)} %get-tuple-element.86.refs_0_), channel_id=1, source_target_pairs={{0,4},{2,6},{4,0},{6,2},{8,12},{10,14},{12,8},{14,10},{16,20},{18,... | collective-permute-start | bytes 393224 | tf_op jit(solution)/shard_map/ppermute | solution.py:46
  27.3 11.7 %collective-permute-start.13 = (bf16[256,256]{1,0:T(8,128)(2,1)S(1)}, bf16[256,256]{1,0:T(8,128)(2,1)S(1)}, u32[]{:S(2)}, u32[]{:S(2)}) collective-permute-start(bf16[256,256]{1,0:T(8,128)(2,1)S(1)} %get-tuple-element.90.refs_7_), channel_id=1, source_target_pairs={{0,24},{2,26},{4,28},{6,30},{8,16},{10,18},{12,20},{14,22},{16,8},... | collective-permute-start | bytes 393224 | tf_op jit(solution)/shard_map/ppermute | solution.py:46
  29.5 12.7 %collective-permute-start.14 = (bf16[256,256]{1,0:T(8,128)(2,1)S(1)}, bf16[256,256]{1,0:T(8,128)(2,1)S(1)}, u32[]{:S(2)}, u32[]{:S(2)}) collective-permute-start(bf16[256,256]{1,0:T(8,128)(2,1)S(1)} %get-tuple-element.90.refs_7_), channel_id=1, source_target_pairs={{0,8},{2,10},{4,12},{6,14},{8,0},{10,2},{12,4},{14,6},{16,24},{18,... | collective-permute-start | bytes 393224 | tf_op jit(solution)/shard_map/ppermute | solution.py:46
  33.2 8.9 %collective-permute-start.15 = (bf16[256,256]{1,0:T(8,128)(2,1)S(1)}, bf16[256,256]{1,0:T(8,128)(2,1)S(1)}, u32[]{:S(2)}, u32[]{:S(2)}) collective-permute-start(bf16[256,256]{1,0:T(8,128)(2,1)S(1)} %get-tuple-element.90.refs_7_), channel_id=1, source_target_pairs={{0,4},{2,6},{4,0},{6,2},{8,12},{10,14},{12,8},{14,10},{16,20},{18,... | collective-permute-start | bytes 393224 | tf_op jit(solution)/shard_map/ppermute | solution.py:46
  36.4 11.5 %collective-permute-start.17 = (bf16[512,256]{1,0:T(8,128)(2,1)S(1)}, bf16[512,256]{1,0:T(8,128)(2,1)S(1)}, u32[]{:S(2)}, u32[]{:S(2)}) collective-permute-start(bf16[512,256]{1,0:T(8,128)(2,1)S(1)} %join.9), channel_id=1, source_target_pairs={{0,4},{2,6},{4,0},{6,2},{8,12},{10,14},{12,8},{14,10},{16,20},{18,... | collective-permute-start | bytes 786440 | tf_op jit(solution)/shard_map/ppermute | solution.py:46
  37.0 9.1 %collective-permute-start.12 = (bf16[256,256]{1,0:T(8,128)(2,1)S(1)}, bf16[256,256]{1,0:T(8,128)(2,1)S(1)}, u32[]{:S(2)}, u32[]{:S(2)}) collective-permute-start(bf16[256,256]{1,0:T(8,128)(2,1)S(1)} %collective-permute-done.11.refs_1_), channel_id=1, source_target_pairs={{0,16},{2,18},{4,20},{6,22},{8,24},{10,26},{12,28},{14,30},{16,0},... | collective-permute-start | bytes 393224 | tf_op jit(solution)/shard_map/ppermute | solution.py:46
  42.2 5.6 %collective-permute-start.16 = (bf16[256,256]{1,0:T(8,128)(2,1)S(1)}, bf16[256,256]{1,0:T(8,128)(2,1)S(1)}, u32[]{:S(2)}, u32[]{:S(2)}) collective-permute-start(bf16[256,256]{1,0:T(8,128)(2,1)S(1)} %collective-permute-done.9.refs_0_.refs_2_), channel_id=1, source_target_pairs={{0,8},{2,10},{4,12},{6,14},{8,0},{10,2},{12,4},{14,6},{16,24},{18,... | collective-permute-start | bytes 393224 | tf_op jit(solution)/shard_map/ppermute | solution.py:46
  47.9 4.4 %collective-permute-start.19 = (bf16[2048,256]{1,0:T(8,128)(2,1)S(1)}, bf16[2048,256]{1,0:T(8,128)(2,1)S(1)}, u32[]{:S(2)}, u32[]{:S(2)}) collective-permute-start(bf16[2048,256]{1,0:T(8,128)(2,1)S(1)} %join.10), channel_id=1, source_target_pairs={{0,2},{2,0},{4,6},{6,4},{8,10},{10,8},{12,14},{14,12},{16,18},{18,... | collective-permute-start | bytes 3145736 | tf_op jit(solution)/shard_map/ppermute | solution.py:46
  48.0 10.3 %collective-permute-start.20 = (bf16[2176,256]{1,0:T(8,128)(2,1)S(1)}, bf16[2176,256]{1,0:T(8,128)(2,1)S(1)}, u32[]{:S(2)}, u32[]{:S(2)}) collective-permute-start(bf16[2176,256]{1,0:T(8,128)(2,1)S(1)} %get-tuple-element.105), channel_id=1, source_target_pairs={{0,2},{2,0},{4,6},{6,4},{8,10},{10,8},{12,14},{14,12},{16,18},{18,... | collective-permute-start | bytes 3342344 | tf_op jit(solution)/shard_map/ppermute | solution.py:46
  48.5 9.7 %collective-permute-start.24 = (bf16[512,256]{1,0:T(8,128)(2,1)S(1)}, bf16[512,256]{1,0:T(8,128)(2,1)S(1)}, u32[]{:S(2)}, u32[]{:S(2)}) collective-permute-start(bf16[512,256]{1,0:T(8,128)(2,1)S(1)} %join.11), channel_id=1, source_target_pairs={{0,4},{2,6},{4,0},{6,2},{8,12},{10,14},{12,8},{14,10},{16,20},{18,... | collective-permute-start | bytes 786440 | tf_op jit(solution)/shard_map/ppermute | solution.py:46
  49.1 9.0 %collective-permute-start.22 = (bf16[256,256]{1,0:T(8,128)(2,1)S(1)}, bf16[256,256]{1,0:T(8,128)(2,1)S(1)}, u32[]{:S(2)}, u32[]{:S(2)}) collective-permute-start(bf16[256,256]{1,0:T(8,128)(2,1)S(1)} %collective-permute-done.15.refs_8_), channel_id=1, source_target_pairs={{0,16},{2,18},{4,20},{6,22},{8,24},{10,26},{12,28},{14,30},{16,0},... | collective-permute-start | bytes 393224 | tf_op jit(solution)/shard_map/ppermute | solution.py:46
  49.8 8.4 %collective-permute-start.23 = (bf16[256,256]{1,0:T(8,128)(2,1)S(1)}, bf16[256,256]{1,0:T(8,128)(2,1)S(1)}, u32[]{:S(2)}, u32[]{:S(2)}) collective-permute-start(bf16[256,256]{1,0:T(8,128)(2,1)S(1)} %collective-permute-done.13.refs_0_.refs_9_), channel_id=1, source_target_pairs={{0,8},{2,10},{4,12},{6,14},{8,0},{10,2},{12,4},{14,6},{16,24},{18,... | collective-permute-start | bytes 393224 | tf_op jit(solution)/shard_map/ppermute | solution.py:46
  54.0 4.3 %collective-permute-start.21 = (bf16[256,256]{1,0:T(8,128)(2,1)S(1)}, bf16[256,256]{1,0:T(8,128)(2,1)S(1)}, u32[]{:S(2)}, u32[]{:S(2)}) collective-permute-start(bf16[256,256]{1,0:T(8,128)(2,1)S(1)} %get-tuple-element.106.q), channel_id=1, source_target_pairs={{0,2},{2,0},{4,6},{6,4},{8,10},{10,8},{12,14},{14,12},{16,18},{18,... | collective-permute-start | bytes 393224 | tf_op jit(solution)/shard_map/ppermute | solution.py:46
  61.5 5.3 %collective-permute-start.26 = (f32[64,256]{1,0:T(8,128)S(1)}, f32[64,256]{1,0:T(8,128)S(1)}, u32[]{:S(2)}, u32[]{:S(2)}) collective-permute-start(f32[64,256]{1,0:T(8,128)S(1)} %get-tuple-element.116), channel_id=1, source_target_pairs={{0,5},{1,4},{2,7},{3,6},{4,1},{5,0},{6,3},{7,2},{8,13},{9,12},{10,... | collective-permute-start | bytes 196616 | tf_op jit(solution)/shard_map/ppermute | solution.py:52
  63.6 4.5 %collective-permute-start.27 = (f32[64,256]{1,0:T(8,128)S(1)}, f32[64,256]{1,0:T(8,128)S(1)}, u32[]{:S(2)}, u32[]{:S(2)}) collective-permute-start(f32[64,256]{1,0:T(8,128)S(1)} %get-tuple-element.117), channel_id=1, source_target_pairs={{0,1},{1,0},{2,3},{3,2},{4,5},{5,4},{6,7},{7,6},{8,9},{9,8},{10,11... | collective-permute-start | bytes 196616 | tf_op jit(solution)/shard_map/ppermute | solution.py:52
  64.1 4.3 %collective-permute-start.28 = (f32[64,256]{1,0:T(8,128)S(1)}, f32[64,256]{1,0:T(8,128)S(1)}, u32[]{:S(2)}, u32[]{:S(2)}) collective-permute-start(f32[64,256]{1,0:T(8,128)S(1)} %get-tuple-element.118), channel_id=1, source_target_pairs={{0,4},{1,5},{2,6},{3,7},{4,0},{5,1},{6,2},{7,3},{8,12},{9,13},{10,... | collective-permute-start | bytes 196616 | tf_op jit(solution)/shard_map/ppermute | solution.py:52
  68.4 7.1 %collective-permute-start.29 = (f32[64,256]{1,0:T(8,128)S(1)}, f32[64,256]{1,0:T(8,128)S(1)}, u32[]{:S(2)}, u32[]{:S(2)}) collective-permute-start(f32[64,256]{1,0:T(8,128)S(1)} %add_xy.1.refs_2_), channel_id=1, source_target_pairs={{0,16},{2,18},{4,20},{6,22},{8,24},{10,26},{12,28},{14,30},{16,0},... | collective-permute-start | bytes 196616 | tf_op jit(solution)/shard_map/ppermute | solution.py:46
  68.9 6.6 %collective-permute-start.30 = (f32[64,256]{1,0:T(8,128)S(1)}, f32[64,256]{1,0:T(8,128)S(1)}, u32[]{:S(2)}, u32[]{:S(2)}) collective-permute-start(f32[64,256]{1,0:T(8,128)S(1)} %add_xy.1.refs_2_), channel_id=1, source_target_pairs={{0,24},{2,26},{4,28},{6,30},{8,16},{10,18},{12,20},{14,22},{16,8},... | collective-permute-start | bytes 196616 | tf_op jit(solution)/shard_map/ppermute | solution.py:46
  70.5 5.4 %collective-permute-start.31 = (f32[64,256]{1,0:T(8,128)S(1)}, f32[64,256]{1,0:T(8,128)S(1)}, u32[]{:S(2)}, u32[]{:S(2)}) collective-permute-start(f32[64,256]{1,0:T(8,128)S(1)} %add_xy.1.refs_2_), channel_id=1, source_target_pairs={{0,8},{2,10},{4,12},{6,14},{8,0},{10,2},{12,4},{14,6},{16,24},{18,... | collective-permute-start | bytes 196616 | tf_op jit(solution)/shard_map/ppermute | solution.py:46
  76.0 5.2 %collective-permute-start.32 = (f32[64,256]{1,0:T(8,128)S(1)}, f32[64,256]{1,0:T(8,128)S(1)}, u32[]{:S(2)}, u32[]{:S(2)}) collective-permute-start(f32[64,256]{1,0:T(8,128)S(1)} %add_z.1.refs_3_), channel_id=1, source_target_pairs={{0,5},{1,4},{2,7},{3,6},{4,1},{5,0},{6,3},{7,2},{8,13},{9,12},{10,... | collective-permute-start | bytes 196616 | tf_op jit(solution)/shard_map/ppermute | solution.py:52
  77.8 4.4 %collective-permute-start.33 = (f32[64,256]{1,0:T(8,128)S(1)}, f32[64,256]{1,0:T(8,128)S(1)}, u32[]{:S(2)}, u32[]{:S(2)}) collective-permute-start(f32[64,256]{1,0:T(8,128)S(1)} %add_z.1.refs_3_), channel_id=1, source_target_pairs={{0,4},{1,5},{2,6},{3,7},{4,0},{5,1},{6,2},{7,3},{8,12},{9,13},{10,... | collective-permute-start | bytes 196616 | tf_op jit(solution)/shard_map/ppermute | solution.py:52
  79.2 4.3 %collective-permute-start.34 = (f32[64,256]{1,0:T(8,128)S(1)}, f32[64,256]{1,0:T(8,128)S(1)}, u32[]{:S(2)}, u32[]{:S(2)}) collective-permute-start(f32[64,256]{1,0:T(8,128)S(1)} %add_z.1.refs_3_), channel_id=1, source_target_pairs={{0,1},{1,0},{2,3},{3,2},{4,5},{5,4},{6,7},{7,6},{8,9},{9,8},{10,11... | collective-permute-start | bytes 196616 | tf_op jit(solution)/shard_map/ppermute | solution.py:52
  (13 other events, 48.0 us)
